TPU v7x, 128 devices: a whole 4x4x4 slice. The times are simulated.
128 devices in a mesh: tok: 8 (over x_hi, z), feat: 16 (over y, x_lo, core).
Axes of the slice: x: 4 (x_hi: 2, x_lo: 2; x = x_hi * 2 + x_lo), y: 4, z: 4, core: 2. Of those that a mesh axis runs over, the one named last changes fastest.
Arguments:
- activations: bfloat16 [32768, 28672], P('tok', 'feat'), may hold values from -6 to 6
- out_grads: bfloat16 [32768, 8192], P('tok', 'feat'), may hold values from -6 to 6
- query_in: bfloat16 [16, 32, 28672], P('tok', None, 'feat'), may hold values from -0.03125 to 0.03125
- query_out: bfloat16 [16, 32, 8192], P('tok', None, 'feat'), may hold values from -0.0625 to 0.0625
Outputs:
- influence: float32 [16, 32768], P(None, ('tok', 'feat'))
All inputs are finite; a program needn't handle non-finite values.
Results may differ from a plain program's by a relative error of at most 0.0003.
Values may be sent and summed in bfloat16 or wider, within the bound.
No kernel may reach another device: no remote copies, remote signals or barrier semaphores. Data moves between devices by JAX's collectives and lax.ppermute only.
A program may use at most 128 MiB of HBM per device.

v0:
```python
import jax
import jax.numpy as jnp
from jax import lax
from jax.sharding import PartitionSpec as P


def passed_along(value, axis, steps):
    count = lax.axis_size(axis)
    pairs = [(source, (source + steps) % count) for source in range(count)]
    return lax.ppermute(value, axis, pairs)


def local(activations, out_grads, query_in, query_out):
    tok_count = lax.axis_size("tok")
    feat_count = lax.axis_size("feat")
    tok_index = lax.axis_index("tok")
    per_device, rank_size, in_local = query_in.shape
    row_count = activations.shape[0]
    row_share = row_count // feat_count
    query_total = per_device * tok_count
    factors = jnp.concatenate([query_in, query_out], axis=2)
    influence = jnp.zeros((query_total, row_share), jnp.float32)
    current = factors
    for step_index in range(tok_count):
        pair_count = current.shape[0] * rank_size
        in_side = current[:, :, :in_local].reshape(pair_count, in_local)
        out_side = current[:, :, in_local:].reshape(pair_count, -1)
        in_terms = lax.dot_general(
            activations, in_side, (((1,), (1,)), ((), ())), preferred_element_type=jnp.float32
        )
        out_terms = lax.dot_general(
            out_grads, out_side, (((1,), (1,)), ((), ())), preferred_element_type=jnp.float32
        )
        stacked = jnp.stack(
            [
                in_terms.reshape(row_count, -1, rank_size),
                out_terms.reshape(row_count, -1, rank_size),
            ],
            axis=2,
        )
        terms = stacked.reshape(row_count, -1)
        if step_index + 1 < tok_count:
            current = passed_along(current, "tok", 1)
        summed = lax.psum_scatter(terms, "feat", scatter_dimension=0, tiled=True)
        owner = (tok_index - step_index) % tok_count
        grouped = summed.reshape(summed.shape[0], -1, 2, rank_size)
        influence = lax.dynamic_update_slice(
            influence,
            jnp.sum(grouped[:, :, 0, :] * grouped[:, :, 1, :], axis=2).T,
            (owner * per_device, jnp.int32(0)),
        )
    return influence


def solution(mesh):
    in_specs = (P("tok", "feat"), P("tok", "feat"), P("tok", None, "feat"), P("tok", None, "feat"))
    out_specs = P(None, ("tok", "feat"))
    return jax.shard_map(local, mesh=mesh, in_specs=in_specs, out_specs=out_specs, check_vma=False)
```

profile of v0, /device:TPU:1, one launch (start us, length us, event | category | flops | bytes accessed | tf_op | source)
XLA Modules:
  0.0 557.1 jit_solution(17157089560473201064)
XLA Ops:
  6.5 3.6 convolution_bitcast_fusion
  10.1 9.7 %fusion.2 = f32[4096,2,1,32]{0,3,1,2:T(8,128)S(1)} fusion(bf16[2,32,1792]{2,1,0:T(8,128)(2,1)S(1)} %copy-done.1, bf16[4096,1792]{1,0:T(8,128)(2,1)} %param.4), kind=kOutput, calls=%fused_computation.3 | convolution fusion | flops 939524096 | bytes 15958016 | tf_op jit(solution)/shard_map/dot_general | solution.py:28
  20.0 1.5 copy.5
  21.6 2.5 collective-permute-start
  24.2 11.3 %collective-permute-done = bf16[2,32,2304]{2,1,0:T(8,128)(2,1)S(1)} collective-permute-done((bf16[2,32,2304]{2,1,0:T(8,128)(2,1)S(1)}, bf16[2,32,2304]{2,1,0:T(8,128)(2,1)S(1)}, u32[]{:S(2)}, u32[]{:S(2)}) %collective-permute-start) | collective-permute-done | bytes 294944 | tf_op jit(solution)/shard_map/ppermute | solution.py:10
  35.5 3.6 fusion.15
  39.1 9.8 %fusion.14 = f32[64,4096]{1,0:T(8,128)S(1)} fusion(bf16[64,1792]{1,0:T(8,128)(2,1)S(1)} %bitcast.181, bf16[4096,1792]{1,0:T(8,128)(2,1)} %param.4), kind=kOutput, calls=%fused_computation.38 | convolution fusion | flops 939524096 | bytes 15958016 | tf_op jit(solution)/shard_map/dot_general | solution.py:28
  48.9 1.4 pad_maximum_fusion.1
  50.5 13.5 %collective-permute-done.1 = bf16[2,32,2304]{2,1,0:T(8,128)(2,1)S(1)} collective-permute-done((bf16[2,32,2304]{2,1,0:T(8,128)(2,1)S(1)}, bf16[2,32,2304]{2,1,0:T(8,128)(2,1)S(1)}, u32[]{:S(2)}, u32[]{:S(2)}) %collective-permute-start.1) | collective-permute-done | bytes 294944 | tf_op jit(solution)/shard_map/ppermute | solution.py:10
  64.0 3.6 fusion.17
  67.6 9.8 %fusion.16 = f32[64,4096]{1,0:T(8,128)S(1)} fusion(bf16[64,1792]{1,0:T(8,128)(2,1)S(1)} %bitcast.182, bf16[4096,1792]{1,0:T(8,128)(2,1)} %param.4), kind=kOutput, calls=%fused_computation.40 | convolution fusion | flops 939524096 | bytes 15958016 | tf_op jit(solution)/shard_map/dot_general | solution.py:28
  77.4 1.5 pad_maximum_fusion.2
  79.2 12.7 %collective-permute-done.2 = bf16[2,32,2304]{2,1,0:T(8,128)(2,1)S(1)} collective-permute-done((bf16[2,32,2304]{2,1,0:T(8,128)(2,1)S(1)}, bf16[2,32,2304]{2,1,0:T(8,128)(2,1)S(1)}, u32[]{:S(2)}, u32[]{:S(2)}) %collective-permute-start.2) | collective-permute-done | bytes 294944 | tf_op jit(solution)/shard_map/ppermute | solution.py:10
  91.9 3.6 fusion.19
  95.5 9.7 %fusion.18 = f32[64,4096]{1,0:T(8,128)S(1)} fusion(bf16[64,1792]{1,0:T(8,128)(2,1)S(1)} %bitcast.183, bf16[4096,1792]{1,0:T(8,128)(2,1)} %param.4), kind=kOutput, calls=%fused_computation.42 | convolution fusion | flops 939524096 | bytes 15958016 | tf_op jit(solution)/shard_map/dot_general | solution.py:28
  105.2 1.5 pad_maximum_fusion.3
  106.8 13.2 %collective-permute-done.3 = bf16[2,32,2304]{2,1,0:T(8,128)(2,1)S(1)} collective-permute-done((bf16[2,32,2304]{2,1,0:T(8,128)(2,1)S(1)}, bf16[2,32,2304]{2,1,0:T(8,128)(2,1)S(1)}, u32[]{:S(2)}, u32[]{:S(2)}) %collective-permute-start.3) | collective-permute-done | bytes 294944 | tf_op jit(solution)/shard_map/ppermute | solution.py:10
  120.1 3.6 fusion.21
  123.7 9.7 %fusion.20 = f32[64,4096]{1,0:T(8,128)S(1)} fusion(bf16[64,1792]{1,0:T(8,128)(2,1)S(1)} %bitcast.184, bf16[4096,1792]{1,0:T(8,128)(2,1)} %param.4), kind=kOutput, calls=%fused_computation.44 | convolution fusion | flops 939524096 | bytes 15958016 | tf_op jit(solution)/shard_map/dot_general | solution.py:28
  133.4 1.5 pad_maximum_fusion.4
  135.1 13.5 %collective-permute-done.4 = bf16[2,32,2304]{2,1,0:T(8,128)(2,1)S(1)} collective-permute-done((bf16[2,32,2304]{2,1,0:T(8,128)(2,1)S(1)}, bf16[2,32,2304]{2,1,0:T(8,128)(2,1)S(1)}, u32[]{:S(2)}, u32[]{:S(2)}) %collective-permute-start.4) | collective-permute-done | bytes 294944 | tf_op jit(solution)/shard_map/ppermute | solution.py:10
  148.6 3.6 fusion.23
  152.2 9.7 %fusion.22 = f32[64,4096]{1,0:T(8,128)S(1)} fusion(bf16[64,1792]{1,0:T(8,128)(2,1)S(1)} %bitcast.185, bf16[4096,1792]{1,0:T(8,128)(2,1)} %param.4), kind=kOutput, calls=%fused_computation.46 | convolution fusion | flops 939524096 | bytes 15958016 | tf_op jit(solution)/shard_map/dot_general | solution.py:28
  162.0 1.4 pad_maximum_fusion.5
  163.6 9.2 %collective-permute-done.5 = bf16[2,32,2304]{2,1,0:T(8,128)(2,1)S(1)} collective-permute-done((bf16[2,32,2304]{2,1,0:T(8,128)(2,1)S(1)}, bf16[2,32,2304]{2,1,0:T(8,128)(2,1)S(1)}, u32[]{:S(2)}, u32[]{:S(2)}) %collective-permute-start.5) | collective-permute-done | bytes 294944 | tf_op jit(solution)/shard_map/ppermute | solution.py:10
  172.8 3.6 fusion.25
  176.3 9.7 %fusion.24 = f32[64,4096]{1,0:T(8,128)S(1)} fusion(bf16[64,1792]{1,0:T(8,128)(2,1)S(1)} %bitcast.186, bf16[4096,1792]{1,0:T(8,128)(2,1)} %param.4), kind=kOutput, calls=%fused_computation.48 | convolution fusion | flops 939524096 | bytes 15958016 | tf_op jit(solution)/shard_map/dot_general | solution.py:28
  186.1 1.5 pad_maximum_fusion.6
  187.7 0.3 collective-permute-start.6
  188.0 11.8 %collective-permute-done.6 = bf16[2,32,2304]{2,1,0:T(8,128)(2,1)S(1)} collective-permute-done((bf16[2,32,2304]{2,1,0:T(8,128)(2,1)S(1)}, bf16[2,32,2304]{2,1,0:T(8,128)(2,1)S(1)}, u32[]{:S(2)}, u32[]{:S(2)}) %collective-permute-start.6) | collective-permute-done | bytes 294944 | tf_op jit(solution)/shard_map/ppermute | solution.py:10
  199.7 3.6 fusion.27
  203.3 9.8 %fusion.26 = f32[64,4096]{1,0:T(8,128)S(1)} fusion(bf16[64,1792]{1,0:T(8,128)(2,1)S(1)} %bitcast.180, bf16[4096,1792]{1,0:T(8,128)(2,1)} %param.4), kind=kOutput, calls=%fused_computation.50 | convolution fusion | flops 939524096 | bytes 15958016 | tf_op jit(solution)/shard_map/dot_general | solution.py:28
  213.1 1.5 pad_maximum_fusion.7
  214.8 0.9 fusion.13
  215.7 0.9 fusion.12
  216.6 4.5 reduce-scatter.13.cloned.1.call-done
  221.1 0.9 fusion.11
  222.0 65.7 %reduce-scatter.15.cloned.1.call-done = f32[256,128]{0,1:T(8,128)} async-done(((f32[4096,128]{0,1:T(8,128)}), f32[256,128]{0,1:T(8,128)}) %reduce-scatter.15.cloned.1.call-update) | async-done | bytes 131088 | tf_op jit(solution)/shard_map/reduce_scatter | solution.py:44
  287.7 0.9 fusion.10
  288.6 63.8 %reduce-scatter.17.cloned.1.call-done = f32[256,128]{0,1:T(8,128)} async-done(((f32[4096,128]{0,1:T(8,128)}), f32[256,128]{0,1:T(8,128)}) %reduce-scatter.17.cloned.1.call-update) | async-done | bytes 131088 | tf_op jit(solution)/shard_map/reduce_scatter | solution.py:44
  352.4 0.9 fusion.9
  353.3 64.5 %reduce-scatter.19.cloned.1.call-done = f32[256,128]{0,1:T(8,128)} async-done(((f32[4096,128]{0,1:T(8,128)}), f32[256,128]{0,1:T(8,128)}) %reduce-scatter.19.cloned.1.call-update) | async-done | bytes 131088 | tf_op jit(solution)/shard_map/reduce_scatter | solution.py:44
  417.7 0.9 fusion.8
  418.6 64.6 %reduce-scatter.21.cloned.1.call-done = f32[256,128]{0,1:T(8,128)} async-done(((f32[4096,128]{0,1:T(8,128)}), f32[256,128]{0,1:T(8,128)}) %reduce-scatter.21.cloned.1.call-update) | async-done | bytes 131088 | tf_op jit(solution)/shard_map/reduce_scatter | solution.py:44
  483.3 0.9 fusion.7
  484.2 64.6 %reduce-scatter.23.cloned.1.call-done = f32[256,128]{0,1:T(8,128)} async-done(((f32[4096,128]{0,1:T(8,128)}), f32[256,128]{0,1:T(8,128)}) %reduce-scatter.23.cloned.1.call-update) | async-done | bytes 131088 | tf_op jit(solution)/shard_map/reduce_scatter | solution.py:44
  548.8 0.9 fusion.6
  549.7 0.6 bitcast_dynamic-update-slice_fusion
  (53 shorter events, 1.5 us)
Async XLA Ops:
  6.5 3.6 copy-start.1
  6.5 208.2 %reduce-scatter.9.cloned.1.call-start = ((), (), s32[]{:S(2)}) async-start(), calls=%async_computation.8 | async-start | bytes 2228224 | tf_op jit(solution)/shard_map/reduce_scatter | solution.py:44
  20.0 1.6 copy-start
  21.5 194.2 %reduce-scatter.11.cloned.1.call-start = ((), (), s32[]{:S(2)}) async-start(), calls=%async_computation.9 | async-start | bytes 2228224 | tf_op jit(solution)/shard_map/reduce_scatter | solution.py:44
  21.6 13.9 %collective-permute-start = (bf16[2,32,2304]{2,1,0:T(8,128)(2,1)S(1)}, bf16[2,32,2304]{2,1,0:T(8,128)(2,1)S(1)}, u32[]{:S(2)}, u32[]{:S(2)}) collective-permute-start(bf16[2,32,2304]{2,1,0:T(8,128)(2,1)S(1)} %pad_maximum_fusion.8), channel_id=1, source_target_pairs={{0,16},{16,32},{32,48},{48,64},{64,80},{80,96},{96,112},{112,0},{1... | collective-permute-start | bytes 884744 | tf_op jit(solution)/shard_map/ppermute | solution.py:10
  50.4 170.8 %reduce-scatter.13.cloned.1.call-start = ((), (), s32[]{:S(2)}) async-start(), calls=%async_computation.10 | async-start | bytes 2228224 | tf_op jit(solution)/shard_map/reduce_scatter | solution.py:44
  50.4 13.6 %collective-permute-start.1 = (bf16[2,32,2304]{2,1,0:T(8,128)(2,1)S(1)}, bf16[2,32,2304]{2,1,0:T(8,128)(2,1)S(1)}, u32[]{:S(2)}, u32[]{:S(2)}) collective-permute-start(bf16[2,32,2304]{2,1,0:T(8,128)(2,1)S(1)} %collective-permute-done), channel_id=1, source_target_pairs={{0,16},{16,32},{32,48},{48,64},{64,80},{80,96},{96,112},{112,0},{1... | collective-permute-start | bytes 884744 | tf_op jit(solution)/shard_map/ppermute | solution.py:10
  78.9 208.8 %reduce-scatter.15.cloned.1.call-start = ((), (), s32[]{:S(2)}) async-start(), calls=%async_computation.11 | async-start | bytes 2228224 | tf_op jit(solution)/shard_map/reduce_scatter | solution.py:44
  78.9 13.0 %collective-permute-start.2 = (bf16[2,32,2304]{2,1,0:T(8,128)(2,1)S(1)}, bf16[2,32,2304]{2,1,0:T(8,128)(2,1)S(1)}, u32[]{:S(2)}, u32[]{:S(2)}) collective-permute-start(bf16[2,32,2304]{2,1,0:T(8,128)(2,1)S(1)} %collective-permute-done.1), channel_id=1, source_target_pairs={{0,16},{16,32},{32,48},{48,64},{64,80},{80,96},{96,112},{112,0},{1... | collective-permute-start | bytes 884744 | tf_op jit(solution)/shard_map/ppermute | solution.py:10
  106.7 245.6 %reduce-scatter.17.cloned.1.call-start = ((), (), s32[]{:S(2)}) async-start(), calls=%async_computation.12 | async-start | bytes 2228224 | tf_op jit(solution)/shard_map/reduce_scatter | solution.py:44
  106.8 13.3 %collective-permute-start.3 = (bf16[2,32,2304]{2,1,0:T(8,128)(2,1)S(1)}, bf16[2,32,2304]{2,1,0:T(8,128)(2,1)S(1)}, u32[]{:S(2)}, u32[]{:S(2)}) collective-permute-start(bf16[2,32,2304]{2,1,0:T(8,128)(2,1)S(1)} %collective-permute-done.2), channel_id=1, source_target_pairs={{0,16},{16,32},{32,48},{48,64},{64,80},{80,96},{96,112},{112,0},{1... | collective-permute-start | bytes 884744 | tf_op jit(solution)/shard_map/ppermute | solution.py:10
  135.0 282.8 %reduce-scatter.19.cloned.1.call-start = ((), (), s32[]{:S(2)}) async-start(), calls=%async_computation.13 | async-start | bytes 2228224 | tf_op jit(solution)/shard_map/reduce_scatter | solution.py:44
  135.0 13.6 %collective-permute-start.4 = (bf16[2,32,2304]{2,1,0:T(8,128)(2,1)S(1)}, bf16[2,32,2304]{2,1,0:T(8,128)(2,1)S(1)}, u32[]{:S(2)}, u32[]{:S(2)}) collective-permute-start(bf16[2,32,2304]{2,1,0:T(8,128)(2,1)S(1)} %collective-permute-done.3), channel_id=1, source_target_pairs={{0,16},{16,32},{32,48},{48,64},{64,80},{80,96},{96,112},{112,0},{1... | collective-permute-start | bytes 884744 | tf_op jit(solution)/shard_map/ppermute | solution.py:10
  163.4 319.8 %reduce-scatter.21.cloned.1.call-start = ((), (), s32[]{:S(2)}) async-start(), calls=%async_computation.14 | async-start | bytes 2228224 | tf_op jit(solution)/shard_map/reduce_scatter | solution.py:44
  163.5 9.3 %collective-permute-start.5 = (bf16[2,32,2304]{2,1,0:T(8,128)(2,1)S(1)}, bf16[2,32,2304]{2,1,0:T(8,128)(2,1)S(1)}, u32[]{:S(2)}, u32[]{:S(2)}) collective-permute-start(bf16[2,32,2304]{2,1,0:T(8,128)(2,1)S(1)} %collective-permute-done.4), channel_id=1, source_target_pairs={{0,16},{16,32},{32,48},{48,64},{64,80},{80,96},{96,112},{112,0},{1... | collective-permute-start | bytes 884744 | tf_op jit(solution)/shard_map/ppermute | solution.py:10
  187.6 361.2 %reduce-scatter.23.cloned.1.call-start = ((), (), s32[]{:S(2)}) async-start(), calls=%async_computation.15 | async-start | bytes 2228224 | tf_op jit(solution)/shard_map/reduce_scatter | solution.py:44
  187.7 12.1 %collective-permute-start.6 = (bf16[2,32,2304]{2,1,0:T(8,128)(2,1)S(1)}, bf16[2,32,2304]{2,1,0:T(8,128)(2,1)S(1)}, u32[]{:S(2)}, u32[]{:S(2)}) collective-permute-start(bf16[2,32,2304]{2,1,0:T(8,128)(2,1)S(1)} %collective-permute-done.5), channel_id=1, source_target_pairs={{0,16},{16,32},{32,48},{48,64},{64,80},{80,96},{96,112},{112,0},{1... | collective-permute-start | bytes 884744 | tf_op jit(solution)/shard_map/ppermute | solution.py:10
  484.2 65.5 %copy-start.2 = (f32[16,256]{1,0:T(8,128)}, f32[16,256]{1,0:T(8,128)S(1)}, u32[]{:S(2)}) copy-start(f32[16,256]{1,0:T(8,128)S(1)} %bitcast_dynamic-update-slice_fusion.1) | copy-start | bytes 49156
Sparse Core Ops, SparseCore 0:
  21.7 64.8 reduce-scatter.8
  89.0 64.5 reduce-scatter.10
  156.0 65.0 reduce-scatter.12
  223.4 64.2 reduce-scatter.14
  289.9 62.3 reduce-scatter.16
  354.6 63.0 reduce-scatter.18
  420.1 63.1 reduce-scatter.20
  485.7 63.0 reduce-scatter.22
where the time goes:
time: 561 us; the launch traced here: 557 us
  waiting for transfers between devices  413 us (74%)
  matrix products  106 us (19%)
  other arithmetic  17.8 us (3%)
  between operations  13.9 us (2%)
    reduce_scatter x8, waiting for transfers between devices, local(): summed = lax.psum_scatter(terms, 'feat', scatter_dimension=0, tiled=True)  328 us
    ppermute x7, waiting for transfers between devices, passed_along(): return lax.ppermute(value, axis, pairs)  85.2 us
    dot_general x8, matrix products, local(): lax.dot_general(activations, in_side, (((1,), (1,)), ((), ())), preferred...  77.8 us
    dot_general x8, matrix products, local(): lax.dot_general(out_grads, out_side, (((1,), (1,)), ((), ())), preferred_...  28.6 us
  transfers between devices with their start and end apart: 15, of which 13 were waited for; matrix products, arithmetic and copies ran while one was open for 20% of the time, Pallas kernels for 0%

commit v1 on v0

v1 whole, which is shorter than its diff:
```python
import functools

import jax
import jax.numpy as jnp
from jax import lax
from jax.experimental import pallas as pl
from jax.experimental.pallas import tpu as pltpu
from jax.sharding import PartitionSpec as P

RANK = 32
BLOCK = 256
SPAN = 173.25
VMEM = 24 * 2**20
NT = (((1,), (1,)), ((), ()))

G1, G0, X = 2, 1, 0
ORDERS = ((X, G0, G1), (G0, G1, X), (G1, X, G0))


def gray(y):
    return y ^ (y >> 1)


def block_of(feat, j, core_bit):
    y = gray(gray(feat >> 2) ^ (j >> 1))
    return (y << 2) | ((((feat >> 1) & 1) ^ (j & 1)) << 1) | ((feat & 1) ^ core_bit)


def feat_pairs(bit):
    if bit == "core":
        return [(s, s ^ 1) for s in range(16)]
    if bit == X:
        return [(s, s ^ 2) for s in range(16)]
    flip = 1 if bit == G0 else 2
    return [(s, (gray(gray(s >> 2) ^ flip) << 2) | (s & 3)) for s in range(16)]


def send_feat(value, bit):
    return lax.ppermute(value, "feat", feat_pairs(bit))


def encode(value):
    rows, cols = value.shape
    grouped = jnp.abs(value).reshape(rows // RANK, RANK, cols)
    top = jnp.max(grouped, axis=1, keepdims=True)
    scale = (top * 1.01 + 1e-35).astype(jnp.bfloat16).astype(jnp.float32)
    part = grouped * (1.0 / scale) + 1e-30
    root = (part * lax.rsqrt(part)).reshape(rows, cols)
    code = jnp.exp(root * SPAN - SPAN / 2)
    return jnp.where(value < 0, -code, code).astype(jnp.bfloat16), scale.reshape(rows // RANK, cols)


def decode(code, scale):
    rows, cols = code.shape
    code = code.astype(jnp.float32)
    root = jnp.log(jnp.abs(code)) * (1.0 / SPAN) + 0.5
    size = (root * root).reshape(rows // RANK, RANK, cols) * scale.reshape(rows // RANK, 1, cols)
    size = size.reshape(rows, cols)
    return jnp.where(code < 0, -size, size)


def put(ref, pos, value):
    rows, cols = value.shape
    code, scale = encode(value)
    ref[pos, :rows, :] = code
    row = lax.broadcasted_iota(jnp.int32, (16, cols), 0)
    packed = jnp.zeros((16, cols), jnp.float32)
    for g in range(rows // RANK):
        packed = jnp.where(row == g, scale[g : g + 1, :], packed)
    ref[pos, rows : rows + 16, :] = packed.astype(jnp.bfloat16)


def get(ref, pos):
    rows = ref.shape[1] - 16
    scale = ref[pos, rows : rows + 16, :].astype(jnp.float32)[: rows // RANK, :]
    return decode(ref[pos, :rows, :], scale)


def project(act_ref, grad_ref, factor_refs):
    n_in = act_ref.shape[1]
    q_in = jnp.concatenate([f[:, :n_in] for f in factor_refs], axis=0)
    q_out = jnp.concatenate([f[:, n_in:] for f in factor_refs], axis=0)
    p_in = lax.dot_general(q_in, act_ref[...], NT, preferred_element_type=jnp.float32)
    p_out = lax.dot_general(q_out, grad_ref[...], NT, preferred_element_type=jnp.float32)
    return p_in, p_out


def away_kernel(blocks, feat_ref, act_ref, grad_ref, *refs):
    out_ref = refs[blocks]
    p_in, p_out = project(act_ref, grad_ref, refs[:blocks])
    half = p_in.shape[0]
    out_ref[0, :half, :] = p_in
    out_ref[0, half:, :] = p_out


def home_kernel(blocks, cuts, feat_ref, act_ref, grad_ref, *refs):
    factors, got_ref, outs = refs[:blocks], refs[blocks], refs[blocks + 1 :]
    j = pl.program_id(0)
    p_in, p_out = project(act_ref, grad_ref, factors)
    total = jnp.concatenate([p_in, p_out], axis=0) + got_ref[0]
    for t, order in enumerate(ORDERS):
        send_ref, keep_ref = outs[2 * t], outs[2 * t + 1]
        part = total[cuts[t] : cuts[t + 1]]
        bits = [(j >> d) & 1 for d in order]
        pos = bits[1] * 2 + bits[2]

        @pl.when(bits[0] == 1)
        def _(send_ref=send_ref, part=part, pos=pos):
            put(send_ref, pos, part)

        @pl.when(bits[0] == 0)
        def _(keep_ref=keep_ref, part=part, pos=pos):
            keep_ref[pos] = part


def step_kernel(count, *refs):
    half = count // 2
    keeps, gots, outs = refs[:3], refs[3:6], refs[6:]
    for t in range(3):
        send_ref, keep_ref = outs[2 * t], outs[2 * t + 1]
        for pos in range(half):
            put(send_ref, pos, keeps[t][half + pos] + get(gots[t], half + pos))
        for pos in range(half):
            keep_ref[pos] = keeps[t][pos] + get(gots[t], pos)


def last_kernel(chunks, tok_ref, *refs):
    out_ref = refs[-1]
    tok = tok_ref[0]
    for c, owners in enumerate(chunks):
        keeps, gots = refs[6 * c : 6 * c + 3], refs[6 * c + 3 : 6 * c + 6]
        total = jnp.concatenate([k[0] + get(g, 0) for k, g in zip(keeps, gots)], axis=0)
        half = total.shape[0] // 2
        product = (total[:half] * total[half:]).reshape(half // RANK, RANK, BLOCK)
        score = jnp.sum(product, axis=1)
        per = score.shape[0] // len(owners)
        for i, (flip, turn) in enumerate(owners):
            owner = ((tok & 4) ^ flip) | ((tok + turn) & 3)
            for k in range(per):
                out_ref[pl.ds(owner * per + k, 1), :] = score[i * per + k : i * per + k + 1, :]


def params():
    return pltpu.CompilerParams(vmem_limit_bytes=VMEM)


def cuts_of(chunk_index, rows):
    groups = rows // RANK
    sizes = [groups // 3 + (1 if (i + chunk_index) % 3 < groups % 3 else 0) for i in range(3)]
    cuts = [0]
    for size in sizes:
        cuts.append(cuts[-1] + size * RANK)
    return cuts


def away(feat, acts, grads, factors):
    rows = 2 * sum(f.shape[0] for f in factors)
    k_in, k_out = acts.shape[1], grads.shape[1]
    spec = lambda k: pl.BlockSpec((BLOCK, k), lambda j, feat: (block_of(feat[0], j, 1), 0))
    fixed = [pl.BlockSpec(f.shape, lambda j, feat: (0, 0)) for f in factors]
    return pl.pallas_call(
        functools.partial(away_kernel, len(factors)),
        grid_spec=pltpu.PrefetchScalarGridSpec(
            num_scalar_prefetch=1,
            grid=(8,),
            in_specs=[spec(k_in), spec(k_out), *fixed],
            out_specs=pl.BlockSpec((1, rows, BLOCK), lambda j, feat: (j, 0, 0)),
        ),
        out_shape=jax.ShapeDtypeStruct((8, rows, BLOCK), jnp.float32),
        compiler_params=params(),
        cost_estimate=pl.CostEstimate(
            flops=8 * BLOCK * rows * (k_in + k_out), transcendentals=0,
            bytes_accessed=8 * BLOCK * (2 * (k_in + k_out) + 4 * rows)),
    )(feat, acts, grads, *factors)


def home(feat, acts, grads, factors, got, cuts):
    rows = got.shape[1]
    k_in, k_out = acts.shape[1], grads.shape[1]
    spec = lambda k: pl.BlockSpec((BLOCK, k), lambda j, feat: (block_of(feat[0], j, 0), 0))
    fixed = [pl.BlockSpec(f.shape, lambda j, feat: (0, 0)) for f in factors]
    shapes = []
    for t in range(3):
        n = cuts[t + 1] - cuts[t]
        shapes += [jax.ShapeDtypeStruct((4, n + 16, BLOCK), jnp.bfloat16),
                   jax.ShapeDtypeStruct((4, n, BLOCK), jnp.float32)]
    return pl.pallas_call(
        functools.partial(home_kernel, len(factors), cuts),
        grid_spec=pltpu.PrefetchScalarGridSpec(
            num_scalar_prefetch=1,
            grid=(8,),
            in_specs=[spec(k_in), spec(k_out), *fixed,
                      pl.BlockSpec((1, rows, BLOCK), lambda j, feat: (j, 0, 0))],
            out_specs=[pl.BlockSpec(s.shape, lambda j, feat: (0, 0, 0)) for s in shapes],
        ),
        out_shape=shapes,
        compiler_params=params(),
        cost_estimate=pl.CostEstimate(
            flops=8 * BLOCK * rows * (k_in + k_out), transcendentals=8 * BLOCK * rows,
            bytes_accessed=8 * BLOCK * (2 * (k_in + k_out) + 8 * rows)),
    )(feat, acts, grads, *factors, got)


def step(count, keeps, gots):
    half = count // 2
    shapes = []
    for keep in keeps:
        n = keep.shape[1]
        shapes += [jax.ShapeDtypeStruct((half, n + 16, BLOCK), jnp.bfloat16),
                   jax.ShapeDtypeStruct((half, n, BLOCK), jnp.float32)]
    rows = sum(k.shape[1] for k in keeps)
    return pl.pallas_call(
        functools.partial(step_kernel, count),
        out_shape=shapes,
        compiler_params=params(),
        cost_estimate=pl.CostEstimate(
            flops=count * rows * BLOCK * 20, transcendentals=2 * count * rows * BLOCK,
            bytes_accessed=count * rows * BLOCK * 10),
    )(*keeps, *gots)


def local(activations, out_grads, query_in, query_out):
    per, rank, k_in = query_in.shape
    feat = jnp.reshape(lax.axis_index("feat"), (1,)).astype(jnp.int32)
    tok = jnp.reshape(lax.axis_index("tok"), (1,)).astype(jnp.int32)
    up = [(s, (s & 4) | ((s + 1) & 3)) for s in range(8)]
    down = [(s, (s & 4) | ((s + 3) & 3)) for s in range(8)]
    across = [(s, s ^ 4) for s in range(8)]
    send_tok = lambda value, pairs: lax.ppermute(value, "tok", pairs)

    own = jnp.concatenate([query_in, query_out], axis=2).reshape(per * rank, -1)
    far = send_tok(own, across)
    own_up, own_down = send_tok(own, up), send_tok(own, down)
    far_up, far_down = send_tok(far, up), send_tok(far, down)
    own_two = send_tok(own_up, up)
    far_two = send_tok(far_down, down)
    chunks = [
        ((own, far), ((0, 0), (4, 0))),
        ((own_up, own_down), ((0, 3), (0, 1))),
        ((far_up, far_down), ((4, 3), (4, 1))),
        ((own_two, far_two), ((0, 2), (4, 2))),
    ]
    ends = []
    for c, (factors, _) in enumerate(chunks):
        rows = 2 * sum(f.shape[0] for f in factors)
        cuts = cuts_of(c, rows)
        got = send_feat(away(feat, activations, out_grads, factors), "core")
        outs = home(feat, activations, out_grads, factors, got, cuts)
        for stage, count in enumerate((4, 2)):
            gots = [send_feat(outs[2 * t], ORDERS[t][stage]) for t in range(3)]
            outs = step(count, outs[1::2], gots)
        gots = [send_feat(outs[2 * t], ORDERS[t][2]) for t in range(3)]
        ends += [*outs[1::2], *gots]
    total = per * lax.axis_size("tok")
    return pl.pallas_call(
        functools.partial(last_kernel, [owners for _, owners in chunks]),
        in_specs=[pl.BlockSpec(memory_space=pltpu.SMEM)] + [pl.BlockSpec(memory_space=pltpu.VMEM)] * len(ends),
        out_shape=jax.ShapeDtypeStruct((total, BLOCK), jnp.float32),
        compiler_params=params(),
    )(tok, *ends)


def solution(mesh):
    in_specs = (P("tok", "feat"), P("tok", "feat"), P("tok", None, "feat"), P("tok", None, "feat"))
    out_specs = P(None, ("tok", "feat"))
    return jax.shard_map(local, mesh=mesh, in_specs=in_specs, out_specs=out_specs, check_vma=False)
```

time: 561 us -> 143 us (0.25)
  the two profiles are of different devices: /device:TPU:1 before, /device:TPU:0 now
where the time goes in v1:
time: 143 us; the launch traced here: 142 us
  starting transfers between devices  58.1 us (41%)
  Pallas kernels  52.1 us (36%)
  local copies, waits for them, and re-layouts  17.3 us (12%)
  waiting for transfers between devices  13.8 us (10%)
    ppermute x40, starting transfers between devices, send_feat(): return lax.ppermute(value, 'feat', feat_pairs(bit))  42.8 us
    pallas_call x4, Pallas kernels, home(): pl.pallas_call(functools.partial(home_kernel, len(factors), cuts), grid_s...  25.5 us
    pallas_call x4, Pallas kernels, away(): pl.pallas_call(functools.partial(away_kernel, len(factors)), grid_spec=pl...  20.1 us
    unnamed x44, local copies, waits for them, and re-layouts  17.3 us
    ppermute x7, starting transfers between devices, local(): send_tok = lambda value, pairs: lax.ppermute(value, 'tok', pairs)  15.2 us
    ppermute x40, waiting for transfers between devices, send_feat(): return lax.ppermute(value, 'feat', feat_pairs(bit))  8.18 us
    ppermute x7, waiting for transfers between devices, local(): send_tok = lambda value, pairs: lax.ppermute(value, 'tok', pairs)  5.59 us
    pallas_call x8, Pallas kernels, step(): pl.pallas_call(functools.partial(step_kernel, count), out_shape=shapes, c...  5.45 us
  transfers between devices with their start and end apart: 47, of which 6 were waited for; matrix products, arithmetic and copies ran while one was open for 0% of the time, Pallas kernels for 36%

profile of v1, /device:TPU:0, one launch (start us, length us, event | category | flops | bytes accessed | tf_op | source)
XLA Modules:
  0.0 142.5 jit_solution(8696949835551491685)
XLA Ops:
  0.0 1.0 pad_maximum_fusion
  1.0 3.2 %collective-permute-start = (bf16[64,2304]{1,0:T(8,128)(2,1)S(1)}, bf16[64,2304]{1,0:T(8,128)(2,1)S(1)}, u32[]{:S(2)}, u32[]{:S(2)}) collective-permute-start(bf16[64,2304]{1,0:T(8,128)(2,1)S(1)} %bitcast.5), channel_id=1, source_target_pairs={{0,64},{16,80},{32,96},{48,112},{64,0},{80,16},{96,32},{112,48},{1... | collective-permute-start | bytes 884744 | tf_op jit(solution)/shard_map/ppermute | solution.py:229
  4.2 1.9 %collective-permute-start.11 = (bf16[64,2304]{1,0:T(8,128)(2,1)S(1)}, bf16[64,2304]{1,0:T(8,128)(2,1)S(1)}, u32[]{:S(2)}, u32[]{:S(2)}) collective-permute-start(bf16[64,2304]{1,0:T(8,128)(2,1)S(1)} %bitcast.6), channel_id=1, source_target_pairs={{0,16},{16,32},{32,48},{48,0},{64,80},{80,96},{96,112},{112,64},{1... | collective-permute-start | bytes 884744 | tf_op jit(solution)/shard_map/ppermute | solution.py:229
  6.1 2.1 %collective-permute-start.12 = (bf16[64,2304]{1,0:T(8,128)(2,1)S(1)}, bf16[64,2304]{1,0:T(8,128)(2,1)S(1)}, u32[]{:S(2)}, u32[]{:S(2)}) collective-permute-start(bf16[64,2304]{1,0:T(8,128)(2,1)S(1)} %bitcast.7), channel_id=1, source_target_pairs={{0,48},{16,0},{32,16},{48,32},{64,112},{80,64},{96,80},{112,96},{1... | collective-permute-start | bytes 884744 | tf_op jit(solution)/shard_map/ppermute | solution.py:229
  8.2 3.0 %collective-permute-done.refs_1_ = bf16[64,2304]{1,0:T(8,128)(2,1)S(1)} collective-permute-done((bf16[64,2304]{1,0:T(8,128)(2,1)S(1)}, bf16[64,2304]{1,0:T(8,128)(2,1)S(1)}, u32[]{:S(2)}, u32[]{:S(2)}) %collective-permute-start) | collective-permute-done | bytes 294944 | tf_op jit(solution)/shard_map/ppermute | solution.py:229
  11.2 5.3 %copy-done = bf16[4096,1792]{1,0:T(8,128)(2,1)S(1)} copy-done((bf16[4096,1792]{1,0:T(8,128)(2,1)S(1)}, bf16[4096,1792]{1,0:T(8,128)(2,1)}, u32[]{:S(2)}) %copy-start) | copy-done | bytes 14680088
  16.5 2.2 %copy-done.1 = bf16[4096,512]{1,0:T(8,128)(2,1)S(1)} copy-done((bf16[4096,512]{1,0:T(8,128)(2,1)S(1)}, bf16[4096,512]{1,0:T(8,128)(2,1)}, u32[]{:S(2)}) %copy-start.1) | copy-done | bytes 4194328
  18.7 4.4 %shard_map.46 = f32[8,256,256]{2,1,0:T(8,128)S(1)} custom-call(s32[1]{0:T(128)} %bitcast.1.feat_ref, bf16[4096,1792]{1,0:T(8,128)(2,1)S(1)} %copy-done, bf16[4096,512]{1,0:T(8,128)(2,1)S(1)} %copy-done.1, bf16[64,2304]{1,0:T(8,128)(2,1)S(1)} %bitcast.8, bf16[64,2304]{1,0:T(8,128)(2,1)S(1)} %collective-permute-done.refs_1_), custom_call_target="tpu_custom_call" | custom-call | flops 1207959552 | bytes 11534336 | tf_op jit(solution)/shard_map/pallas_call | solution.py:161
  23.2 4.3 %collective-permute-start.24 = (bf16[64,2304]{1,0:T(8,128)(2,1)S(1)}, bf16[64,2304]{1,0:T(8,128)(2,1)S(1)}, u32[]{:S(2)}, u32[]{:S(2)}) collective-permute-start(bf16[64,2304]{1,0:T(8,128)(2,1)S(1)} %collective-permute-done.refs_1_), channel_id=1, source_target_pairs={{0,48},{16,0},{32,16},{48,32},{64,112},{80,64},{96,80},{112,96},{1... | collective-permute-start | bytes 884744 | tf_op jit(solution)/shard_map/ppermute | solution.py:229
  27.6 4.5 %shard_map.50 = f32[8,256,256]{2,1,0:T(8,128)S(1)} custom-call(s32[1]{0:T(128)} %bitcast.1.feat_ref, bf16[4096,1792]{1,0:T(8,128)(2,1)S(1)} %copy-done, bf16[4096,512]{1,0:T(8,128)(2,1)S(1)} %copy-done.1, bf16[64,2304]{1,0:T(8,128)(2,1)S(1)} %collective-permute-done.11.refs_0_, bf16[64,2304]{1,0:T(8,128)(2,1)S(1)} %collective-permute-done.12.refs_1_), custom_call_target="tpu_custom_call" | custom-call | flops 1207959552 | bytes 11534336 | tf_op jit(solution)/shard_map/pallas_call | solution.py:161
  32.3 2.1 %collective-permute-done.24.refs_1_ = bf16[64,2304]{1,0:T(8,128)(2,1)S(1)} collective-permute-done((bf16[64,2304]{1,0:T(8,128)(2,1)S(1)}, bf16[64,2304]{1,0:T(8,128)(2,1)S(1)}, u32[]{:S(2)}, u32[]{:S(2)}) %collective-permute-start.24) | collective-permute-done | bytes 294944 | tf_op jit(solution)/shard_map/ppermute | solution.py:229
  34.4 3.7 %collective-permute-start.36 = (bf16[64,2304]{1,0:T(8,128)(2,1)S(1)}, bf16[64,2304]{1,0:T(8,128)(2,1)S(1)}, u32[]{:S(2)}, u32[]{:S(2)}) collective-permute-start(bf16[64,2304]{1,0:T(8,128)(2,1)S(1)} %collective-permute-done.24.refs_1_), channel_id=1, source_target_pairs={{0,48},{16,0},{32,16},{48,32},{64,112},{80,64},{96,80},{112,96},{1... | collective-permute-start | bytes 884744 | tf_op jit(solution)/shard_map/ppermute | solution.py:229
  38.6 5.6 %shard_map.54 = f32[8,256,256]{2,1,0:T(8,128)} custom-call(s32[1]{0:T(128)} %bitcast.1.feat_ref, bf16[4096,1792]{1,0:T(8,128)(2,1)S(1)} %copy-done, bf16[4096,512]{1,0:T(8,128)(2,1)S(1)} %copy-done.1, bf16[64,2304]{1,0:T(8,128)(2,1)S(1)} %collective-permute-done.23.refs_0_, bf16[64,2304]{1,0:T(8,128)(2,1)S(1)} %collective-permute-done.24.refs_1_), custom_call_target="tpu_custom_call" | custom-call | flops 1207959552 | bytes 11534336 | tf_op jit(solution)/shard_map/pallas_call | solution.py:161
  44.2 5.6 %shard_map.58 = f32[8,256,256]{2,1,0:T(8,128)} custom-call(s32[1]{0:T(128)} %bitcast.1.feat_ref, bf16[4096,1792]{1,0:T(8,128)(2,1)S(1)} %copy-done, bf16[4096,512]{1,0:T(8,128)(2,1)S(1)} %copy-done.1, bf16[64,2304]{1,0:T(8,128)(2,1)S(1)} %collective-permute-done.35.refs_0_, bf16[64,2304]{1,0:T(8,128)(2,1)S(1)} %collective-permute-done.36.refs_1_), custom_call_target="tpu_custom_call" | custom-call | flops 1207959552 | bytes 11534336 | tf_op jit(solution)/shard_map/pallas_call | solution.py:161
  50.3 6.4 %shard_map.47 = (bf16[4,112,256]{2,1,0:T(8,128)(2,1)}, f32[4,96,256]{2,1,0:T(8,128)S(1)}, bf16[4,112,256]{2,1,0:T(8,128)(2,1)}, f32[4,96,256]{2,1,0:T(8,128)S(1)...) custom-call(s32[1]{0:T(128)} %bitcast.1.feat_ref, bf16[4096,1792]{1,0:T(8,128)(2,1)S(1)} %copy-done, ...), custom_call_target="tpu_custom_call" | custom-call | flops 1207959552 | bytes 13631488 | tf_op jit(solution)/shard_map/pallas_call | solution.py:187
  58.8 1.5 %collective-permute-start.2 = (bf16[4,112,256]{2,1,0:T(8,128)(2,1)}, bf16[4,112,256]{2,1,0:T(8,128)(2,1)S(1)}, u32[]{:S(2)}, u32[]{:S(2)}) collective-permute-start(bf16[4,112,256]{2,1,0:T(8,128)(2,1)} %get-tuple-element.80), channel_id=1, source_target_pairs={{0,2},{1,3},{2,0},{3,1},{4,6},{5,7},{6,4},{7,5},{8,10},{9,11},{10,... | collective-permute-start | bytes 688136 | tf_op jit(solution)/shard_map/ppermute | solution.py:39
  60.3 1.6 %collective-permute-start.3 = (bf16[4,112,256]{2,1,0:T(8,128)(2,1)}, bf16[4,112,256]{2,1,0:T(8,128)(2,1)}, u32[]{:S(2)}, u32[]{:S(2)}) collective-permute-start(bf16[4,112,256]{2,1,0:T(8,128)(2,1)} %get-tuple-element.81), channel_id=1, source_target_pairs={{0,4},{1,5},{2,6},{3,7},{4,0},{5,1},{6,2},{7,3},{8,12},{9,13},{10,... | collective-permute-start | bytes 688136 | tf_op jit(solution)/shard_map/ppermute | solution.py:39
  61.9 1.4 copy-done.2
  63.3 2.2 %collective-permute-start.4 = (bf16[4,80,256]{2,1,0:T(8,128)(2,1)}, bf16[4,80,256]{2,1,0:T(8,128)(2,1)}, u32[]{:S(2)}, u32[]{:S(2)}) collective-permute-start(bf16[4,80,256]{2,1,0:T(8,128)(2,1)} %get-tuple-element.82), channel_id=1, source_target_pairs={{0,12},{1,13},{2,14},{3,15},{4,8},{5,9},{6,10},{7,11},{8,4},{9,5},... | collective-permute-start | bytes 491528 | tf_op jit(solution)/shard_map/ppermute | solution.py:39
  65.5 1.6 %copy-done.3 = f32[8,256,256]{2,1,0:T(8,128)S(1)} copy-done((f32[8,256,256]{2,1,0:T(8,128)S(1)}, f32[8,256,256]{2,1,0:T(8,128)}, u32[]{:S(2)}) %copy-start.3) | copy-done | bytes 2097176
  67.1 1.0 copy-done.7
  68.1 6.3 %shard_map.51 = (bf16[4,112,256]{2,1,0:T(8,128)(2,1)S(1)}, f32[4,96,256]{2,1,0:T(8,128)S(1)}, bf16[4,80,256]{2,1,0:T(8,128)(2,1)}, f32[4,64,256]{2,1,0:T(8,128)S...) custom-call(s32[1]{0:T(128)} %bitcast.1.feat_ref, bf16[4096,1792]{1,0:T(8,128)(2,1)S(1)} %copy-done, ...), custom_call_target="tpu_custom_call" | custom-call | flops 1207959552 | bytes 13631488 | tf_op jit(solution)/shard_map/pallas_call | solution.py:187
  75.6 1.6 %collective-permute-start.16 = (bf16[4,112,256]{2,1,0:T(8,128)(2,1)}, bf16[4,112,256]{2,1,0:T(8,128)(2,1)S(1)}, u32[]{:S(2)}, u32[]{:S(2)}) collective-permute-start(bf16[4,112,256]{2,1,0:T(8,128)(2,1)} %get-tuple-element.100), channel_id=1, source_target_pairs={{0,12},{1,13},{2,14},{3,15},{4,8},{5,9},{6,10},{7,11},{8,4},{9,5},... | collective-permute-start | bytes 688136 | tf_op jit(solution)/shard_map/ppermute | solution.py:39
  77.2 1.0 copy-done.13
  78.2 0.9 copy-done.15
  79.2 0.9 copy-done.17
  80.1 1.8 %shard_map.48 = (bf16[2,112,256]{2,1,0:T(8,128)(2,1)S(1)}, f32[2,96,256]{2,1,0:T(8,128)S(1)}, bf16[2,112,256]{2,1,0:T(8,128)(2,1)S(1)}, f32[2,96,256]{2,1,0:T(8,...) custom-call(f32[4,96,256]{2,1,0:T(8,128)S(1)} %copy-done.11, f32[4,96,256]{2,1,0:T(8,128)S(1)} %copy-done.13, ...), custom_call_target="tpu_custom_call" | custom-call | flops 5242880 | bytes 2621440 | tf_op jit(solution)/shard_map/pallas_call | solution.py:212
  82.7 1.5 %collective-permute-start.7 = (bf16[2,80,256]{2,1,0:T(8,128)(2,1)S(1)}, bf16[2,80,256]{2,1,0:T(8,128)(2,1)S(1)}, u32[]{:S(2)}, u32[]{:S(2)}) collective-permute-start(bf16[2,80,256]{2,1,0:T(8,128)(2,1)S(1)} %get-tuple-element.88), channel_id=1, source_target_pairs={{0,2},{1,3},{2,0},{3,1},{4,6},{5,7},{6,4},{7,5},{8,10},{9,11},{10,... | collective-permute-start | bytes 245768 | tf_op jit(solution)/shard_map/ppermute | solution.py:39
  85.0 1.8 %collective-permute-start.18 = (bf16[2,80,256]{2,1,0:T(8,128)(2,1)S(1)}, bf16[2,80,256]{2,1,0:T(8,128)(2,1)S(1)}, u32[]{:S(2)}, u32[]{:S(2)}) collective-permute-start(bf16[2,80,256]{2,1,0:T(8,128)(2,1)S(1)} %get-tuple-element.105), channel_id=1, source_target_pairs={{0,12},{1,13},{2,14},{3,15},{4,8},{5,9},{6,10},{7,11},{8,4},{9,5},... | collective-permute-start | bytes 245768 | tf_op jit(solution)/shard_map/ppermute | solution.py:39
  86.8 7.3 %shard_map.55 = (bf16[4,80,256]{2,1,0:T(8,128)(2,1)S(1)}, f32[4,64,256]{2,1,0:T(8,128)S(1)}, bf16[4,112,256]{2,1,0:T(8,128)(2,1)S(1)}, f32[4,96,256]{2,1,0:T(8,1...) custom-call(s32[1]{0:T(128)} %bitcast.1.feat_ref, bf16[4096,1792]{1,0:T(8,128)(2,1)S(1)} %bitcast.4, ...), custom_call_target="tpu_custom_call" | custom-call | flops 1207959552 | bytes 13631488 | tf_op jit(solution)/shard_map/pallas_call | solution.py:187
  94.8 1.6 %collective-permute-start.28 = (bf16[4,112,256]{2,1,0:T(8,128)(2,1)S(1)}, bf16[4,112,256]{2,1,0:T(8,128)(2,1)S(1)}, u32[]{:S(2)}, u32[]{:S(2)}) collective-permute-start(bf16[4,112,256]{2,1,0:T(8,128)(2,1)S(1)} %get-tuple-element.118), channel_id=1, source_target_pairs={{0,12},{1,13},{2,14},{3,15},{4,8},{5,9},{6,10},{7,11},{8,4},{9,5},... | collective-permute-start | bytes 688136 | tf_op jit(solution)/shard_map/ppermute | solution.py:39
  97.1 1.7 %collective-permute-start.6 = (bf16[2,112,256]{2,1,0:T(8,128)(2,1)S(1)}, bf16[2,112,256]{2,1,0:T(8,128)(2,1)S(1)}, u32[]{:S(2)}, u32[]{:S(2)}) collective-permute-start(bf16[2,112,256]{2,1,0:T(8,128)(2,1)S(1)} %get-tuple-element.87), channel_id=1, source_target_pairs={{0,12},{1,13},{2,14},{3,15},{4,8},{5,9},{6,10},{7,11},{8,4},{9,5},... | collective-permute-start | bytes 344072 | tf_op jit(solution)/shard_map/ppermute | solution.py:39
  99.3 5.5 %shard_map.59 = (bf16[4,112,256]{2,1,0:T(8,128)(2,1)S(1)}, f32[4,96,256]{2,1,0:T(8,128)S(1)}, bf16[4,112,256]{2,1,0:T(8,128)(2,1)S(1)}, f32[4,96,256]{2,1,0:T(8,...) custom-call(s32[1]{0:T(128)} %bitcast.1.feat_ref, bf16[4096,1792]{1,0:T(8,128)(2,1)S(1)} %bitcast.4, ...), custom_call_target="tpu_custom_call" | custom-call | flops 1207959552 | bytes 13631488 | tf_op jit(solution)/shard_map/pallas_call | solution.py:187
  104.9 1.6 %collective-permute-start.38 = (bf16[4,112,256]{2,1,0:T(8,128)(2,1)S(1)}, bf16[4,112,256]{2,1,0:T(8,128)(2,1)S(1)}, u32[]{:S(2)}, u32[]{:S(2)}) collective-permute-start(bf16[4,112,256]{2,1,0:T(8,128)(2,1)S(1)} %get-tuple-element.134), channel_id=1, source_target_pairs={{0,2},{1,3},{2,0},{3,1},{4,6},{5,7},{6,4},{7,5},{8,10},{9,11},{10,... | collective-permute-start | bytes 688136 | tf_op jit(solution)/shard_map/ppermute | solution.py:39
  107.1 1.6 %collective-permute-start.40 = (bf16[4,80,256]{2,1,0:T(8,128)(2,1)S(1)}, bf16[4,80,256]{2,1,0:T(8,128)(2,1)S(1)}, u32[]{:S(2)}, u32[]{:S(2)}) collective-permute-start(bf16[4,80,256]{2,1,0:T(8,128)(2,1)S(1)} %get-tuple-element.136), channel_id=1, source_target_pairs={{0,12},{1,13},{2,14},{3,15},{4,8},{5,9},{6,10},{7,11},{8,4},{9,5},... | collective-permute-start | bytes 491528 | tf_op jit(solution)/shard_map/ppermute | solution.py:39
  110.9 4.1 %collective-permute-done.17.refs_3_ = bf16[2,112,256]{2,1,0:T(8,128)(2,1)S(1)} collective-permute-done((bf16[2,112,256]{2,1,0:T(8,128)(2,1)S(1)}, bf16[2,112,256]{2,1,0:T(8,128)(2,1)S(1)}, u32[]{:S(2)}, u32[]{:S(2)}) %collective-permute-start.17) | collective-permute-done | bytes 114720 | tf_op jit(solution)/shard_map/ppermute | solution.py:39
  116.0 1.5 %collective-permute-start.10 = (bf16[1,80,256]{2,1,0:T(8,128)(2,1)S(1)}, bf16[1,80,256]{2,1,0:T(8,128)(2,1)S(1)}, u32[]{:S(2)}, u32[]{:S(2)}) collective-permute-start(bf16[1,80,256]{2,1,0:T(8,128)(2,1)S(1)} %get-tuple-element.94), channel_id=1, source_target_pairs={{0,4},{1,5},{2,6},{3,7},{4,0},{5,1},{6,2},{7,3},{8,12},{9,13},{10,... | collective-permute-start | bytes 122888 | tf_op jit(solution)/shard_map/ppermute | solution.py:39
  118.5 1.8 %collective-permute-start.30 = (bf16[2,112,256]{2,1,0:T(8,128)(2,1)S(1)}, bf16[2,112,256]{2,1,0:T(8,128)(2,1)S(1)}, u32[]{:S(2)}, u32[]{:S(2)}) collective-permute-start(bf16[2,112,256]{2,1,0:T(8,128)(2,1)S(1)} %get-tuple-element.123), channel_id=1, source_target_pairs={{0,12},{1,13},{2,14},{3,15},{4,8},{5,9},{6,10},{7,11},{8,4},{9,5},... | collective-permute-start | bytes 344072 | tf_op jit(solution)/shard_map/ppermute | solution.py:39
  120.3 1.3 collective-permute-start.31
  123.3 1.4 %collective-permute-start.42 = (bf16[2,112,256]{2,1,0:T(8,128)(2,1)S(1)}, bf16[2,112,256]{2,1,0:T(8,128)(2,1)S(1)}, u32[]{:S(2)}, u32[]{:S(2)}) collective-permute-start(bf16[2,112,256]{2,1,0:T(8,128)(2,1)S(1)} %get-tuple-element.141), channel_id=1, source_target_pairs={{0,12},{1,13},{2,14},{3,15},{4,8},{5,9},{6,10},{7,11},{8,4},{9,5},... | collective-permute-start | bytes 344072 | tf_op jit(solution)/shard_map/ppermute | solution.py:39
  124.7 1.8 %collective-permute-start.8 = (bf16[1,112,256]{2,1,0:T(8,128)(2,1)S(1)}, bf16[1,112,256]{2,1,0:T(8,128)(2,1)S(1)}, u32[]{:S(2)}, u32[]{:S(2)}) collective-permute-start(bf16[1,112,256]{2,1,0:T(8,128)(2,1)S(1)} %get-tuple-element.92), channel_id=1, source_target_pairs={{0,12},{1,13},{2,14},{3,15},{4,8},{5,9},{6,10},{7,11},{8,4},{9,5},... | collective-permute-start | bytes 172040 | tf_op jit(solution)/shard_map/ppermute | solution.py:39
  126.5 1.5 %collective-permute-start.9 = (bf16[1,112,256]{2,1,0:T(8,128)(2,1)S(1)}, bf16[1,112,256]{2,1,0:T(8,128)(2,1)S(1)}, u32[]{:S(2)}, u32[]{:S(2)}) collective-permute-start(bf16[1,112,256]{2,1,0:T(8,128)(2,1)S(1)} %get-tuple-element.93), channel_id=1, source_target_pairs={{0,2},{1,3},{2,0},{3,1},{4,6},{5,7},{6,4},{7,5},{8,10},{9,11},{10,... | collective-permute-start | bytes 172040 | tf_op jit(solution)/shard_map/ppermute | solution.py:39
  128.0 1.7 %collective-permute-start.20 = (bf16[1,112,256]{2,1,0:T(8,128)(2,1)S(1)}, bf16[1,112,256]{2,1,0:T(8,128)(2,1)S(1)}, u32[]{:S(2)}, u32[]{:S(2)}) collective-permute-start(bf16[1,112,256]{2,1,0:T(8,128)(2,1)S(1)} %get-tuple-element.110), channel_id=1, source_target_pairs={{0,12},{1,13},{2,14},{3,15},{4,8},{5,9},{6,10},{7,11},{8,4},{9,5},... | collective-permute-start | bytes 172040 | tf_op jit(solution)/shard_map/ppermute | solution.py:39
  130.9 1.6 %collective-permute-start.32 = (bf16[1,80,256]{2,1,0:T(8,128)(2,1)S(1)}, bf16[1,80,256]{2,1,0:T(8,128)(2,1)S(1)}, u32[]{:S(2)}, u32[]{:S(2)}) collective-permute-start(bf16[1,80,256]{2,1,0:T(8,128)(2,1)S(1)} %get-tuple-element.128), channel_id=1, source_target_pairs={{0,12},{1,13},{2,14},{3,15},{4,8},{5,9},{6,10},{7,11},{8,4},{9,5},... | collective-permute-start | bytes 122888 | tf_op jit(solution)/shard_map/ppermute | solution.py:39
  134.1 1.4 %collective-permute-start.44 = (bf16[1,112,256]{2,1,0:T(8,128)(2,1)S(1)}, bf16[1,112,256]{2,1,0:T(8,128)(2,1)S(1)}, u32[]{:S(2)}, u32[]{:S(2)}) collective-permute-start(bf16[1,112,256]{2,1,0:T(8,128)(2,1)S(1)} %get-tuple-element.146), channel_id=1, source_target_pairs={{0,12},{1,13},{2,14},{3,15},{4,8},{5,9},{6,10},{7,11},{8,4},{9,5},... | collective-permute-start | bytes 172040 | tf_op jit(solution)/shard_map/ppermute | solution.py:39
  135.6 1.7 %collective-permute-start.45 = (bf16[1,112,256]{2,1,0:T(8,128)(2,1)S(1)}, bf16[1,112,256]{2,1,0:T(8,128)(2,1)S(1)}, u32[]{:S(2)}, u32[]{:S(2)}) collective-permute-start(bf16[1,112,256]{2,1,0:T(8,128)(2,1)S(1)} %get-tuple-element.147), channel_id=1, source_target_pairs={{0,2},{1,3},{2,0},{3,1},{4,6},{5,7},{6,4},{7,5},{8,10},{9,11},{10,... | collective-permute-start | bytes 172040 | tf_op jit(solution)/shard_map/ppermute | solution.py:39
  138.2 3.1 %collective-permute-done.46.refs_23_ = bf16[1,80,256]{2,1,0:T(8,128)(2,1)S(1)} collective-permute-done((bf16[1,80,256]{2,1,0:T(8,128)(2,1)S(1)}, bf16[1,80,256]{2,1,0:T(8,128)(2,1)S(1)}, u32[]{:S(2)}, u32[]{:S(2)}) %collective-permute-start.46) | collective-permute-done | bytes 40992 | tf_op jit(solution)/shard_map/ppermute | solution.py:39
  141.3 1.1 shard_map.62
  (109 shorter events, 18.8 us)
Async XLA Ops:
  1.0 10.2 %collective-permute-start = (bf16[64,2304]{1,0:T(8,128)(2,1)S(1)}, bf16[64,2304]{1,0:T(8,128)(2,1)S(1)}, u32[]{:S(2)}, u32[]{:S(2)}) collective-permute-start(bf16[64,2304]{1,0:T(8,128)(2,1)S(1)} %bitcast.5), channel_id=1, source_target_pairs={{0,64},{16,80},{32,96},{48,112},{64,0},{80,16},{96,32},{112,48},{1... | collective-permute-start | bytes 884744 | tf_op jit(solution)/shard_map/ppermute | solution.py:229
  4.2 23.3 %collective-permute-start.11 = (bf16[64,2304]{1,0:T(8,128)(2,1)S(1)}, bf16[64,2304]{1,0:T(8,128)(2,1)S(1)}, u32[]{:S(2)}, u32[]{:S(2)}) collective-permute-start(bf16[64,2304]{1,0:T(8,128)(2,1)S(1)} %bitcast.6), channel_id=1, source_target_pairs={{0,16},{16,32},{32,48},{48,0},{64,80},{80,96},{96,112},{112,64},{1... | collective-permute-start | bytes 884744 | tf_op jit(solution)/shard_map/ppermute | solution.py:229
  6.1 21.4 %collective-permute-start.12 = (bf16[64,2304]{1,0:T(8,128)(2,1)S(1)}, bf16[64,2304]{1,0:T(8,128)(2,1)S(1)}, u32[]{:S(2)}, u32[]{:S(2)}) collective-permute-start(bf16[64,2304]{1,0:T(8,128)(2,1)S(1)} %bitcast.7), channel_id=1, source_target_pairs={{0,48},{16,0},{32,16},{48,32},{64,112},{80,64},{96,80},{112,96},{1... | collective-permute-start | bytes 884744 | tf_op jit(solution)/shard_map/ppermute | solution.py:229
  23.1 27.1 %collective-permute-start.1 = (f32[8,256,256]{2,1,0:T(8,128)S(1)}, f32[8,256,256]{2,1,0:T(8,128)S(1)}, u32[]{:S(2)}, u32[]{:S(2)}) collective-permute-start(f32[8,256,256]{2,1,0:T(8,128)S(1)} %shard_map.46), channel_id=1, source_target_pairs={{0,1},{1,0},{2,3},{3,2},{4,5},{5,4},{6,7},{7,6},{8,9},{9,8},{10,11... | collective-permute-start | bytes 6291464 | tf_op jit(solution)/shard_map/ppermute | solution.py:39
  23.2 11.2 %collective-permute-start.24 = (bf16[64,2304]{1,0:T(8,128)(2,1)S(1)}, bf16[64,2304]{1,0:T(8,128)(2,1)S(1)}, u32[]{:S(2)}, u32[]{:S(2)}) collective-permute-start(bf16[64,2304]{1,0:T(8,128)(2,1)S(1)} %collective-permute-done.refs_1_), channel_id=1, source_target_pairs={{0,48},{16,0},{32,16},{48,32},{64,112},{80,64},{96,80},{112,96},{1... | collective-permute-start | bytes 884744 | tf_op jit(solution)/shard_map/ppermute | solution.py:229
  27.5 11.1 %collective-permute-start.23 = (bf16[64,2304]{1,0:T(8,128)(2,1)S(1)}, bf16[64,2304]{1,0:T(8,128)(2,1)S(1)}, u32[]{:S(2)}, u32[]{:S(2)}) collective-permute-start(bf16[64,2304]{1,0:T(8,128)(2,1)S(1)} %collective-permute-done.refs_1_), channel_id=1, source_target_pairs={{0,16},{16,32},{32,48},{48,0},{64,80},{80,96},{96,112},{112,64},{1... | collective-permute-start | bytes 884744 | tf_op jit(solution)/shard_map/ppermute | solution.py:229
  32.0 29.9 %collective-permute-start.13 = (f32[8,256,256]{2,1,0:T(8,128)S(1)}, f32[8,256,256]{2,1,0:T(8,128)S(1)}, u32[]{:S(2)}, u32[]{:S(2)}) collective-permute-start(f32[8,256,256]{2,1,0:T(8,128)S(1)} %shard_map.50), channel_id=1, source_target_pairs={{0,1},{1,0},{2,3},{3,2},{4,5},{5,4},{6,7},{7,6},{8,9},{9,8},{10,11... | collective-permute-start | bytes 6291464 | tf_op jit(solution)/shard_map/ppermute | solution.py:39
  32.3 11.9 %collective-permute-start.35 = (bf16[64,2304]{1,0:T(8,128)(2,1)S(1)}, bf16[64,2304]{1,0:T(8,128)(2,1)S(1)}, u32[]{:S(2)}, u32[]{:S(2)}) collective-permute-start(bf16[64,2304]{1,0:T(8,128)(2,1)S(1)} %collective-permute-done.11.refs_0_), channel_id=1, source_target_pairs={{0,16},{16,32},{32,48},{48,0},{64,80},{80,96},{96,112},{112,64},{1... | collective-permute-start | bytes 884744 | tf_op jit(solution)/shard_map/ppermute | solution.py:229
  34.4 9.8 %collective-permute-start.36 = (bf16[64,2304]{1,0:T(8,128)(2,1)S(1)}, bf16[64,2304]{1,0:T(8,128)(2,1)S(1)}, u32[]{:S(2)}, u32[]{:S(2)}) collective-permute-start(bf16[64,2304]{1,0:T(8,128)(2,1)S(1)} %collective-permute-done.24.refs_1_), channel_id=1, source_target_pairs={{0,48},{16,0},{32,16},{48,32},{64,112},{80,64},{96,80},{112,96},{1... | collective-permute-start | bytes 884744 | tf_op jit(solution)/shard_map/ppermute | solution.py:229
  44.1 42.6 %collective-permute-start.25 = (f32[8,256,256]{2,1,0:T(8,128)}, f32[8,256,256]{2,1,0:T(8,128)}, u32[]{:S(2)}, u32[]{:S(2)}) collective-permute-start(f32[8,256,256]{2,1,0:T(8,128)} %shard_map.54), channel_id=1, source_target_pairs={{0,1},{1,0},{2,3},{3,2},{4,5},{5,4},{6,7},{7,6},{8,9},{9,8},{10,11... | collective-permute-start | bytes 6291464 | tf_op jit(solution)/shard_map/ppermute | solution.py:39
  49.8 49.0 %collective-permute-start.37 = (f32[8,256,256]{2,1,0:T(8,128)}, f32[8,256,256]{2,1,0:T(8,128)S(1)}, u32[]{:S(2)}, u32[]{:S(2)}) collective-permute-start(f32[8,256,256]{2,1,0:T(8,128)} %shard_map.58), channel_id=1, source_target_pairs={{0,1},{1,0},{2,3},{3,2},{4,5},{5,4},{6,7},{7,6},{8,9},{9,8},{10,11... | collective-permute-start | bytes 6291464 | tf_op jit(solution)/shard_map/ppermute | solution.py:39
  50.3 36.5 %slice-start.1 = ((s8[14680064]{0:T(1024)(128)(4,1)}), s8[4194304]{0:T(1024)(128)(4,1)S(1)}, s32[]{:S(2)}) async-start(s8[14680064]{0:T(1024)(128)(4,1)} %bitcast.3), calls=%async_computation.1 | async-start | bytes 8388608
  58.8 16.1 %collective-permute-start.2 = (bf16[4,112,256]{2,1,0:T(8,128)(2,1)}, bf16[4,112,256]{2,1,0:T(8,128)(2,1)S(1)}, u32[]{:S(2)}, u32[]{:S(2)}) collective-permute-start(bf16[4,112,256]{2,1,0:T(8,128)(2,1)} %get-tuple-element.80), channel_id=1, source_target_pairs={{0,2},{1,3},{2,0},{3,1},{4,6},{5,7},{6,4},{7,5},{8,10},{9,11},{10,... | collective-permute-start | bytes 688136 | tf_op jit(solution)/shard_map/ppermute | solution.py:39
  60.3 16.9 %collective-permute-start.3 = (bf16[4,112,256]{2,1,0:T(8,128)(2,1)}, bf16[4,112,256]{2,1,0:T(8,128)(2,1)}, u32[]{:S(2)}, u32[]{:S(2)}) collective-permute-start(bf16[4,112,256]{2,1,0:T(8,128)(2,1)} %get-tuple-element.81), channel_id=1, source_target_pairs={{0,4},{1,5},{2,6},{3,7},{4,0},{5,1},{6,2},{7,3},{8,12},{9,13},{10,... | collective-permute-start | bytes 688136 | tf_op jit(solution)/shard_map/ppermute | solution.py:39
  63.3 11.0 %collective-permute-start.4 = (bf16[4,80,256]{2,1,0:T(8,128)(2,1)}, bf16[4,80,256]{2,1,0:T(8,128)(2,1)}, u32[]{:S(2)}, u32[]{:S(2)}) collective-permute-start(bf16[4,80,256]{2,1,0:T(8,128)(2,1)} %get-tuple-element.82), channel_id=1, source_target_pairs={{0,12},{1,13},{2,14},{3,15},{4,8},{5,9},{6,10},{7,11},{8,4},{9,5},... | collective-permute-start | bytes 491528 | tf_op jit(solution)/shard_map/ppermute | solution.py:39
  74.4 9.8 %collective-permute-start.14 = (bf16[4,112,256]{2,1,0:T(8,128)(2,1)S(1)}, bf16[4,112,256]{2,1,0:T(8,128)(2,1)S(1)}, u32[]{:S(2)}, u32[]{:S(2)}) collective-permute-start(bf16[4,112,256]{2,1,0:T(8,128)(2,1)S(1)} %get-tuple-element.98), channel_id=1, source_target_pairs={{0,2},{1,3},{2,0},{3,1},{4,6},{5,7},{6,4},{7,5},{8,10},{9,11},{10,... | collective-permute-start | bytes 688136 | tf_op jit(solution)/shard_map/ppermute | solution.py:39
  75.6 8.6 %collective-permute-start.16 = (bf16[4,112,256]{2,1,0:T(8,128)(2,1)}, bf16[4,112,256]{2,1,0:T(8,128)(2,1)S(1)}, u32[]{:S(2)}, u32[]{:S(2)}) collective-permute-start(bf16[4,112,256]{2,1,0:T(8,128)(2,1)} %get-tuple-element.100), channel_id=1, source_target_pairs={{0,12},{1,13},{2,14},{3,15},{4,8},{5,9},{6,10},{7,11},{8,4},{9,5},... | collective-permute-start | bytes 688136 | tf_op jit(solution)/shard_map/ppermute | solution.py:39
  77.2 5.5 %collective-permute-start.15 = (bf16[4,80,256]{2,1,0:T(8,128)(2,1)}, bf16[4,80,256]{2,1,0:T(8,128)(2,1)S(1)}, u32[]{:S(2)}, u32[]{:S(2)}) collective-permute-start(bf16[4,80,256]{2,1,0:T(8,128)(2,1)} %get-tuple-element.99), channel_id=1, source_target_pairs={{0,4},{1,5},{2,6},{3,7},{4,0},{5,1},{6,2},{7,3},{8,12},{9,13},{10,... | collective-permute-start | bytes 491528 | tf_op jit(solution)/shard_map/ppermute | solution.py:39
  82.7 13.6 %collective-permute-start.7 = (bf16[2,80,256]{2,1,0:T(8,128)(2,1)S(1)}, bf16[2,80,256]{2,1,0:T(8,128)(2,1)S(1)}, u32[]{:S(2)}, u32[]{:S(2)}) collective-permute-start(bf16[2,80,256]{2,1,0:T(8,128)(2,1)S(1)} %get-tuple-element.88), channel_id=1, source_target_pairs={{0,2},{1,3},{2,0},{3,1},{4,6},{5,7},{6,4},{7,5},{8,10},{9,11},{10,... | collective-permute-start | bytes 245768 | tf_op jit(solution)/shard_map/ppermute | solution.py:39
  85.0 12.2 %collective-permute-start.18 = (bf16[2,80,256]{2,1,0:T(8,128)(2,1)S(1)}, bf16[2,80,256]{2,1,0:T(8,128)(2,1)S(1)}, u32[]{:S(2)}, u32[]{:S(2)}) collective-permute-start(bf16[2,80,256]{2,1,0:T(8,128)(2,1)S(1)} %get-tuple-element.105), channel_id=1, source_target_pairs={{0,12},{1,13},{2,14},{3,15},{4,8},{5,9},{6,10},{7,11},{8,4},{9,5},... | collective-permute-start | bytes 245768 | tf_op jit(solution)/shard_map/ppermute | solution.py:39
  94.1 14.6 %collective-permute-start.27 = (bf16[4,112,256]{2,1,0:T(8,128)(2,1)S(1)}, bf16[4,112,256]{2,1,0:T(8,128)(2,1)S(1)}, u32[]{:S(2)}, u32[]{:S(2)}) collective-permute-start(bf16[4,112,256]{2,1,0:T(8,128)(2,1)S(1)} %get-tuple-element.117), channel_id=1, source_target_pairs={{0,4},{1,5},{2,6},{3,7},{4,0},{5,1},{6,2},{7,3},{8,12},{9,13},{10,... | collective-permute-start | bytes 688136 | tf_op jit(solution)/shard_map/ppermute | solution.py:39
  94.8 14.7 %collective-permute-start.28 = (bf16[4,112,256]{2,1,0:T(8,128)(2,1)S(1)}, bf16[4,112,256]{2,1,0:T(8,128)(2,1)S(1)}, u32[]{:S(2)}, u32[]{:S(2)}) collective-permute-start(bf16[4,112,256]{2,1,0:T(8,128)(2,1)S(1)} %get-tuple-element.118), channel_id=1, source_target_pairs={{0,12},{1,13},{2,14},{3,15},{4,8},{5,9},{6,10},{7,11},{8,4},{9,5},... | collective-permute-start | bytes 688136 | tf_op jit(solution)/shard_map/ppermute | solution.py:39
  96.3 8.5 %collective-permute-start.5 = (bf16[2,112,256]{2,1,0:T(8,128)(2,1)S(1)}, bf16[2,112,256]{2,1,0:T(8,128)(2,1)S(1)}, u32[]{:S(2)}, u32[]{:S(2)}) collective-permute-start(bf16[2,112,256]{2,1,0:T(8,128)(2,1)S(1)} %get-tuple-element.86), channel_id=1, source_target_pairs={{0,4},{1,5},{2,6},{3,7},{4,0},{5,1},{6,2},{7,3},{8,12},{9,13},{10,... | collective-permute-start | bytes 344072 | tf_op jit(solution)/shard_map/ppermute | solution.py:39
  97.1 9.3 %collective-permute-start.6 = (bf16[2,112,256]{2,1,0:T(8,128)(2,1)S(1)}, bf16[2,112,256]{2,1,0:T(8,128)(2,1)S(1)}, u32[]{:S(2)}, u32[]{:S(2)}) collective-permute-start(bf16[2,112,256]{2,1,0:T(8,128)(2,1)S(1)} %get-tuple-element.87), channel_id=1, source_target_pairs={{0,12},{1,13},{2,14},{3,15},{4,8},{5,9},{6,10},{7,11},{8,4},{9,5},... | collective-permute-start | bytes 344072 | tf_op jit(solution)/shard_map/ppermute | solution.py:39
  98.8 8.3 %collective-permute-start.26 = (bf16[4,80,256]{2,1,0:T(8,128)(2,1)S(1)}, bf16[4,80,256]{2,1,0:T(8,128)(2,1)S(1)}, u32[]{:S(2)}, u32[]{:S(2)}) collective-permute-start(bf16[4,80,256]{2,1,0:T(8,128)(2,1)S(1)} %get-tuple-element.116), channel_id=1, source_target_pairs={{0,2},{1,3},{2,0},{3,1},{4,6},{5,7},{6,4},{7,5},{8,10},{9,11},{10,... | collective-permute-start | bytes 491528 | tf_op jit(solution)/shard_map/ppermute | solution.py:39
  104.9 13.6 %collective-permute-start.38 = (bf16[4,112,256]{2,1,0:T(8,128)(2,1)S(1)}, bf16[4,112,256]{2,1,0:T(8,128)(2,1)S(1)}, u32[]{:S(2)}, u32[]{:S(2)}) collective-permute-start(bf16[4,112,256]{2,1,0:T(8,128)(2,1)S(1)} %get-tuple-element.134), channel_id=1, source_target_pairs={{0,2},{1,3},{2,0},{3,1},{4,6},{5,7},{6,4},{7,5},{8,10},{9,11},{10,... | collective-permute-start | bytes 688136 | tf_op jit(solution)/shard_map/ppermute | solution.py:39
  106.4 13.9 %collective-permute-start.39 = (bf16[4,112,256]{2,1,0:T(8,128)(2,1)S(1)}, bf16[4,112,256]{2,1,0:T(8,128)(2,1)S(1)}, u32[]{:S(2)}, u32[]{:S(2)}) collective-permute-start(bf16[4,112,256]{2,1,0:T(8,128)(2,1)S(1)} %get-tuple-element.135), channel_id=1, source_target_pairs={{0,4},{1,5},{2,6},{3,7},{4,0},{5,1},{6,2},{7,3},{8,12},{9,13},{10,... | collective-permute-start | bytes 688136 | tf_op jit(solution)/shard_map/ppermute | solution.py:39
  107.1 10.8 %collective-permute-start.40 = (bf16[4,80,256]{2,1,0:T(8,128)(2,1)S(1)}, bf16[4,80,256]{2,1,0:T(8,128)(2,1)S(1)}, u32[]{:S(2)}, u32[]{:S(2)}) collective-permute-start(bf16[4,80,256]{2,1,0:T(8,128)(2,1)S(1)} %get-tuple-element.136), channel_id=1, source_target_pairs={{0,12},{1,13},{2,14},{3,15},{4,8},{5,9},{6,10},{7,11},{8,4},{9,5},... | collective-permute-start | bytes 491528 | tf_op jit(solution)/shard_map/ppermute | solution.py:39
  108.6 6.4 %collective-permute-start.17 = (bf16[2,112,256]{2,1,0:T(8,128)(2,1)S(1)}, bf16[2,112,256]{2,1,0:T(8,128)(2,1)S(1)}, u32[]{:S(2)}, u32[]{:S(2)}) collective-permute-start(bf16[2,112,256]{2,1,0:T(8,128)(2,1)S(1)} %get-tuple-element.104), channel_id=1, source_target_pairs={{0,4},{1,5},{2,6},{3,7},{4,0},{5,1},{6,2},{7,3},{8,12},{9,13},{10,... | collective-permute-start | bytes 344072 | tf_op jit(solution)/shard_map/ppermute | solution.py:39
  109.4 6.6 %collective-permute-start.19 = (bf16[2,112,256]{2,1,0:T(8,128)(2,1)S(1)}, bf16[2,112,256]{2,1,0:T(8,128)(2,1)S(1)}, u32[]{:S(2)}, u32[]{:S(2)}) collective-permute-start(bf16[2,112,256]{2,1,0:T(8,128)(2,1)S(1)} %get-tuple-element.106), channel_id=1, source_target_pairs={{0,2},{1,3},{2,0},{3,1},{4,6},{5,7},{6,4},{7,5},{8,10},{9,11},{10,... | collective-permute-start | bytes 344072 | tf_op jit(solution)/shard_map/ppermute | solution.py:39
  115.0 8.2 %collective-permute-start.29 = (bf16[2,80,256]{2,1,0:T(8,128)(2,1)S(1)}, bf16[2,80,256]{2,1,0:T(8,128)(2,1)S(1)}, u32[]{:S(2)}, u32[]{:S(2)}) collective-permute-start(bf16[2,80,256]{2,1,0:T(8,128)(2,1)S(1)} %get-tuple-element.122), channel_id=1, source_target_pairs={{0,4},{1,5},{2,6},{3,7},{4,0},{5,1},{6,2},{7,3},{8,12},{9,13},{10,... | collective-permute-start | bytes 245768 | tf_op jit(solution)/shard_map/ppermute | solution.py:39
  116.0 6.3 %collective-permute-start.10 = (bf16[1,80,256]{2,1,0:T(8,128)(2,1)S(1)}, bf16[1,80,256]{2,1,0:T(8,128)(2,1)S(1)}, u32[]{:S(2)}, u32[]{:S(2)}) collective-permute-start(bf16[1,80,256]{2,1,0:T(8,128)(2,1)S(1)} %get-tuple-element.94), channel_id=1, source_target_pairs={{0,4},{1,5},{2,6},{3,7},{4,0},{5,1},{6,2},{7,3},{8,12},{9,13},{10,... | collective-permute-start | bytes 122888 | tf_op jit(solution)/shard_map/ppermute | solution.py:39
  117.9 4.5 %collective-permute-start.21 = (bf16[1,80,256]{2,1,0:T(8,128)(2,1)S(1)}, bf16[1,80,256]{2,1,0:T(8,128)(2,1)S(1)}, u32[]{:S(2)}, u32[]{:S(2)}) collective-permute-start(bf16[1,80,256]{2,1,0:T(8,128)(2,1)S(1)} %get-tuple-element.111), channel_id=1, source_target_pairs={{0,2},{1,3},{2,0},{3,1},{4,6},{5,7},{6,4},{7,5},{8,10},{9,11},{10,... | collective-permute-start | bytes 122888 | tf_op jit(solution)/shard_map/ppermute | solution.py:39
  118.5 6.2 %collective-permute-start.30 = (bf16[2,112,256]{2,1,0:T(8,128)(2,1)S(1)}, bf16[2,112,256]{2,1,0:T(8,128)(2,1)S(1)}, u32[]{:S(2)}, u32[]{:S(2)}) collective-permute-start(bf16[2,112,256]{2,1,0:T(8,128)(2,1)S(1)} %get-tuple-element.123), channel_id=1, source_target_pairs={{0,12},{1,13},{2,14},{3,15},{4,8},{5,9},{6,10},{7,11},{8,4},{9,5},... | collective-permute-start | bytes 344072 | tf_op jit(solution)/shard_map/ppermute | solution.py:39
  120.3 6.2 %collective-permute-start.31 = (bf16[2,112,256]{2,1,0:T(8,128)(2,1)S(1)}, bf16[2,112,256]{2,1,0:T(8,128)(2,1)S(1)}, u32[]{:S(2)}, u32[]{:S(2)}) collective-permute-start(bf16[2,112,256]{2,1,0:T(8,128)(2,1)S(1)} %get-tuple-element.124), channel_id=1, source_target_pairs={{0,2},{1,3},{2,0},{3,1},{4,6},{5,7},{6,4},{7,5},{8,10},{9,11},{10,... | collective-permute-start | bytes 344072 | tf_op jit(solution)/shard_map/ppermute | solution.py:39
  122.3 7.4 %collective-permute-start.41 = (bf16[2,112,256]{2,1,0:T(8,128)(2,1)S(1)}, bf16[2,112,256]{2,1,0:T(8,128)(2,1)S(1)}, u32[]{:S(2)}, u32[]{:S(2)}) collective-permute-start(bf16[2,112,256]{2,1,0:T(8,128)(2,1)S(1)} %get-tuple-element.140), channel_id=1, source_target_pairs={{0,4},{1,5},{2,6},{3,7},{4,0},{5,1},{6,2},{7,3},{8,12},{9,13},{10,... | collective-permute-start | bytes 344072 | tf_op jit(solution)/shard_map/ppermute | solution.py:39
  122.4 5.6 %collective-permute-start.43 = (bf16[2,80,256]{2,1,0:T(8,128)(2,1)S(1)}, bf16[2,80,256]{2,1,0:T(8,128)(2,1)S(1)}, u32[]{:S(2)}, u32[]{:S(2)}) collective-permute-start(bf16[2,80,256]{2,1,0:T(8,128)(2,1)S(1)} %get-tuple-element.142), channel_id=1, source_target_pairs={{0,2},{1,3},{2,0},{3,1},{4,6},{5,7},{6,4},{7,5},{8,10},{9,11},{10,... | collective-permute-start | bytes 245768 | tf_op jit(solution)/shard_map/ppermute | solution.py:39
  123.3 7.7 %collective-permute-start.42 = (bf16[2,112,256]{2,1,0:T(8,128)(2,1)S(1)}, bf16[2,112,256]{2,1,0:T(8,128)(2,1)S(1)}, u32[]{:S(2)}, u32[]{:S(2)}) collective-permute-start(bf16[2,112,256]{2,1,0:T(8,128)(2,1)S(1)} %get-tuple-element.141), channel_id=1, source_target_pairs={{0,12},{1,13},{2,14},{3,15},{4,8},{5,9},{6,10},{7,11},{8,4},{9,5},... | collective-permute-start | bytes 344072 | tf_op jit(solution)/shard_map/ppermute | solution.py:39
  124.7 8.2 %collective-permute-start.8 = (bf16[1,112,256]{2,1,0:T(8,128)(2,1)S(1)}, bf16[1,112,256]{2,1,0:T(8,128)(2,1)S(1)}, u32[]{:S(2)}, u32[]{:S(2)}) collective-permute-start(bf16[1,112,256]{2,1,0:T(8,128)(2,1)S(1)} %get-tuple-element.92), channel_id=1, source_target_pairs={{0,12},{1,13},{2,14},{3,15},{4,8},{5,9},{6,10},{7,11},{8,4},{9,5},... | collective-permute-start | bytes 172040 | tf_op jit(solution)/shard_map/ppermute | solution.py:39
  126.5 7.0 %collective-permute-start.9 = (bf16[1,112,256]{2,1,0:T(8,128)(2,1)S(1)}, bf16[1,112,256]{2,1,0:T(8,128)(2,1)S(1)}, u32[]{:S(2)}, u32[]{:S(2)}) collective-permute-start(bf16[1,112,256]{2,1,0:T(8,128)(2,1)S(1)} %get-tuple-element.93), channel_id=1, source_target_pairs={{0,2},{1,3},{2,0},{3,1},{4,6},{5,7},{6,4},{7,5},{8,10},{9,11},{10,... | collective-permute-start | bytes 172040 | tf_op jit(solution)/shard_map/ppermute | solution.py:39
  128.0 6.1 %collective-permute-start.20 = (bf16[1,112,256]{2,1,0:T(8,128)(2,1)S(1)}, bf16[1,112,256]{2,1,0:T(8,128)(2,1)S(1)}, u32[]{:S(2)}, u32[]{:S(2)}) collective-permute-start(bf16[1,112,256]{2,1,0:T(8,128)(2,1)S(1)} %get-tuple-element.110), channel_id=1, source_target_pairs={{0,12},{1,13},{2,14},{3,15},{4,8},{5,9},{6,10},{7,11},{8,4},{9,5},... | collective-permute-start | bytes 172040 | tf_op jit(solution)/shard_map/ppermute | solution.py:39
  129.7 5.9 %collective-permute-start.22 = (bf16[1,112,256]{2,1,0:T(8,128)(2,1)S(1)}, bf16[1,112,256]{2,1,0:T(8,128)(2,1)S(1)}, u32[]{:S(2)}, u32[]{:S(2)}) collective-permute-start(bf16[1,112,256]{2,1,0:T(8,128)(2,1)S(1)} %get-tuple-element.112), channel_id=1, source_target_pairs={{0,4},{1,5},{2,6},{3,7},{4,0},{5,1},{6,2},{7,3},{8,12},{9,13},{10,... | collective-permute-start | bytes 172040 | tf_op jit(solution)/shard_map/ppermute | solution.py:39
  130.9 6.4 %collective-permute-start.32 = (bf16[1,80,256]{2,1,0:T(8,128)(2,1)S(1)}, bf16[1,80,256]{2,1,0:T(8,128)(2,1)S(1)}, u32[]{:S(2)}, u32[]{:S(2)}) collective-permute-start(bf16[1,80,256]{2,1,0:T(8,128)(2,1)S(1)} %get-tuple-element.128), channel_id=1, source_target_pairs={{0,12},{1,13},{2,14},{3,15},{4,8},{5,9},{6,10},{7,11},{8,4},{9,5},... | collective-permute-start | bytes 122888 | tf_op jit(solution)/shard_map/ppermute | solution.py:39
  133.0 5.2 %collective-permute-start.33 = (bf16[1,112,256]{2,1,0:T(8,128)(2,1)S(1)}, bf16[1,112,256]{2,1,0:T(8,128)(2,1)S(1)}, u32[]{:S(2)}, u32[]{:S(2)}) collective-permute-start(bf16[1,112,256]{2,1,0:T(8,128)(2,1)S(1)} %get-tuple-element.129), channel_id=1, source_target_pairs={{0,2},{1,3},{2,0},{3,1},{4,6},{5,7},{6,4},{7,5},{8,10},{9,11},{10,... | collective-permute-start | bytes 172040 | tf_op jit(solution)/shard_map/ppermute | solution.py:39
  133.5 4.7 %collective-permute-start.34 = (bf16[1,112,256]{2,1,0:T(8,128)(2,1)S(1)}, bf16[1,112,256]{2,1,0:T(8,128)(2,1)S(1)}, u32[]{:S(2)}, u32[]{:S(2)}) collective-permute-start(bf16[1,112,256]{2,1,0:T(8,128)(2,1)S(1)} %get-tuple-element.130), channel_id=1, source_target_pairs={{0,4},{1,5},{2,6},{3,7},{4,0},{5,1},{6,2},{7,3},{8,12},{9,13},{10,... | collective-permute-start | bytes 172040 | tf_op jit(solution)/shard_map/ppermute | solution.py:39
  134.1 7.2 %collective-permute-start.44 = (bf16[1,112,256]{2,1,0:T(8,128)(2,1)S(1)}, bf16[1,112,256]{2,1,0:T(8,128)(2,1)S(1)}, u32[]{:S(2)}, u32[]{:S(2)}) collective-permute-start(bf16[1,112,256]{2,1,0:T(8,128)(2,1)S(1)} %get-tuple-element.146), channel_id=1, source_target_pairs={{0,12},{1,13},{2,14},{3,15},{4,8},{5,9},{6,10},{7,11},{8,4},{9,5},... | collective-permute-start | bytes 172040 | tf_op jit(solution)/shard_map/ppermute | solution.py:39
  135.6 5.8 %collective-permute-start.45 = (bf16[1,112,256]{2,1,0:T(8,128)(2,1)S(1)}, bf16[1,112,256]{2,1,0:T(8,128)(2,1)S(1)}, u32[]{:S(2)}, u32[]{:S(2)}) collective-permute-start(bf16[1,112,256]{2,1,0:T(8,128)(2,1)S(1)} %get-tuple-element.147), channel_id=1, source_target_pairs={{0,2},{1,3},{2,0},{3,1},{4,6},{5,7},{6,4},{7,5},{8,10},{9,11},{10,... | collective-permute-start | bytes 172040 | tf_op jit(solution)/shard_map/ppermute | solution.py:39
  137.3 4.0 %collective-permute-start.46 = (bf16[1,80,256]{2,1,0:T(8,128)(2,1)S(1)}, bf16[1,80,256]{2,1,0:T(8,128)(2,1)S(1)}, u32[]{:S(2)}, u32[]{:S(2)}) collective-permute-start(bf16[1,80,256]{2,1,0:T(8,128)(2,1)S(1)} %get-tuple-element.148), channel_id=1, source_target_pairs={{0,4},{1,5},{2,6},{3,7},{4,0},{5,1},{6,2},{7,3},{8,12},{9,13},{10,... | collective-permute-start | bytes 122888 | tf_op jit(solution)/shard_map/ppermute | solution.py:39
  (21 other events, 157.1 us)

commit v2 on v0

v2 whole, which is shorter than its diff:
```python
import functools

import jax
import jax.numpy as jnp
from jax import lax
from jax.experimental import pallas as pl
from jax.experimental.pallas import tpu as pltpu
from jax.sharding import PartitionSpec as P

RANK = 32
BLOCK = 256
SPAN = 125.0
UNIT = (1.4426950408889634 / SPAN) ** 2
VMEM = 16 * 2**20
NT = (((1,), (1,)), ((), ()))
IN_VMEM = pl.BlockSpec(memory_space=pltpu.VMEM)
IN_SMEM = pl.BlockSpec(memory_space=pltpu.SMEM)

G1, G0, X = 2, 1, 0
ORDERS = (
    ((G0, X, G1), (G1, G0, X)),
    ((X, G1, G0), (G1, X, G0)),
    ((G0, X, G1), (X, G0, G1)),
)
CHUNKS = (
    ("own_up", "own_down", "own", "far"),
    ("own_two", "far_down", "far_up"),
    ("far_two",),
)
PLAN = (
    ("home", 0), ("away", 1), ("home", 1), ("step", 0, 1), ("away", 2), ("step", 0, 2), ("home", 2),
    ("step", 1, 1), ("step", 2, 1), ("step", 1, 2), ("step", 2, 2),
)
OWNERS = {
    "own": (0, 0), "far": (4, 0), "own_up": (0, 3), "own_down": (0, 1),
    "far_up": (4, 3), "far_down": (4, 1), "own_two": (0, 2), "far_two": (4, 2),
}


def gray(y):
    return y ^ (y >> 1)


def block_of(feat, orders, j, away):
    core = feat & 1
    spread = [sum(((j >> (2 - i)) & 1) << bit for i, bit in enumerate(order)) for order in orders]
    flips = spread[0] + (core ^ away) * (spread[1] - spread[0])
    y = gray(gray(feat >> 2) ^ (flips >> 1))
    return (y << 2) | ((((feat >> 1) & 1) ^ (flips & 1)) << 1) | (core ^ away)


def partner(device, bit):
    if bit == X:
        return device ^ 2
    flip = 1 if bit == G0 else 2
    return (gray(gray(device >> 2) ^ flip) << 2) | (device & 3)


def halve(value, orders, stage):
    return lax.ppermute(value, "feat", [(s, partner(s, orders[s & 1][stage])) for s in range(16)])


def put(ref, pos, value):
    rows, cols = value.shape
    grouped = value.reshape(rows // RANK, RANK, cols)
    top = jnp.max(jnp.abs(grouped), axis=1, keepdims=True)
    scale = (top * 1.01 + 1e-35).astype(jnp.bfloat16).astype(jnp.float32)
    part = grouped * (1.0 / scale)
    root = part * lax.rsqrt(jnp.abs(part) + 1e-30)
    ref[pos, :rows, :] = jnp.exp2(root * SPAN).reshape(rows, cols).astype(jnp.bfloat16)
    row = lax.broadcasted_iota(jnp.int32, (16, cols), 0)
    packed = jnp.zeros((16, cols), jnp.float32)
    for g in range(rows // RANK):
        packed = jnp.where(row == g, scale[g], packed)
    ref[pos, rows : rows + 16, :] = packed.astype(jnp.bfloat16)


def get(ref, pos):
    rows, cols = ref.shape[1] - 16, ref.shape[2]
    scale = ref[pos, rows : rows + 16, :].astype(jnp.float32)[: rows // RANK, :]
    root = jnp.log(ref[pos, :rows, :].astype(jnp.float32)).reshape(rows // RANK, RANK, cols)
    return (root * jnp.abs(root) * (scale * UNIT).reshape(rows // RANK, 1, cols)).reshape(rows, cols)


def gather_factors(factors, q_ref):
    row = 0
    for f in factors:
        q_ref[row : row + f.shape[0], :] = f[...]
        row += f.shape[0]


def project(act_ref, grad_ref, q_ref, block):
    n_in = act_ref.shape[1]
    rows = pl.ds(pl.multiple_of(block * BLOCK, BLOCK), BLOCK)
    p_in = lax.dot_general(q_ref[:, :n_in], act_ref[rows, :], NT, preferred_element_type=jnp.float32)
    p_out = lax.dot_general(q_ref[:, n_in:], grad_ref[rows, :], NT, preferred_element_type=jnp.float32)
    return p_in, p_out


def load_kernel(parts, act_ref, grad_ref, act_out, grad_out, sems):
    copies = []
    for src, dst in ((act_ref, act_out), (grad_ref, grad_out)):
        share = src.shape[0] // parts
        for i in range(parts):
            rows = pl.ds(i * share, share)
            copies.append(pltpu.make_async_copy(src.at[rows, :], dst.at[rows, :], sems.at[len(copies)]))
    for copy in copies:
        copy.start()
    for copy in copies:
        copy.wait()


def load(arrays):
    parts = 8
    return pl.pallas_call(
        functools.partial(load_kernel, parts),
        in_specs=[pl.BlockSpec(memory_space=pltpu.HBM)] * 2,
        out_specs=[IN_VMEM] * 2,
        out_shape=[pltpu.VMEM(x.shape, x.dtype) for x in arrays],
        scratch_shapes=[pltpu.SemaphoreType.DMA((2 * parts,))],
        compiler_params=pltpu.CompilerParams(vmem_limit_bytes=VMEM),
        cost_estimate=pl.CostEstimate(flops=0, transcendentals=0, bytes_accessed=sum(x.size * 2 for x in arrays)),
    )(*(pltpu.with_memory_space_constraint(x, pltpu.HBM) for x in arrays))


def away_kernel(blocks, orders, feat_ref, act_ref, grad_ref, *refs):
    out_ref, q_ref = refs[blocks:]
    gather_factors(refs[:blocks], q_ref)
    for j in range(8):
        p_in, p_out = project(act_ref, grad_ref, q_ref, block_of(feat_ref[0], orders, j, 1))
        put(out_ref, j, jnp.concatenate([p_in, p_out], axis=0))


def home_kernel(blocks, orders, feat_ref, act_ref, grad_ref, *refs):
    got_ref, send_ref, keep_ref, q_ref = refs[blocks:]
    gather_factors(refs[:blocks], q_ref)
    for j in (4, 5, 6, 7, 0, 1, 2, 3):
        p_in, p_out = project(act_ref, grad_ref, q_ref, block_of(feat_ref[0], orders, j, 0))
        total = jnp.concatenate([p_in, p_out], axis=0) + get(got_ref, j)
        if j >= 4:
            put(send_ref, j - 4, total)
        else:
            keep_ref[j] = total


def step_kernel(keep_ref, got_ref, send_ref, left_ref):
    half = left_ref.shape[0]
    for pos in range(half):
        put(send_ref, pos, keep_ref[half + pos] + get(got_ref, half + pos))
    for pos in range(half):
        left_ref[pos] = keep_ref[pos] + get(got_ref, pos)


def last_kernel(tok_ref, *refs):
    out_ref = refs[-1]
    tok = tok_ref[0]
    for c, names in enumerate(CHUNKS):
        keep_ref, got_ref = refs[2 * c : 2 * c + 2]
        total = keep_ref[0] + get(got_ref, 0)
        half = total.shape[0] // 2
        product = (total[:half] * total[half:]).reshape(half // RANK, RANK, BLOCK)
        score = jnp.sum(product, axis=1)
        per = score.shape[0] // len(names)
        for i, name in enumerate(names):
            flip, turn = OWNERS[name]
            owner = ((tok & 4) ^ flip) | ((tok + turn) & 3)
            for k in range(per):
                out_ref[pl.ds(owner * per + k, 1), :] = score[i * per + k : i * per + k + 1, :]


def call(kernel, shapes, operands, flops=0, transcendentals=0, scalars=1, scratch=(), after=None):
    moved = sum(o.size * o.dtype.itemsize for o in operands)
    specs = [IN_SMEM] * scalars + [IN_VMEM] * (len(operands) - scalars)
    if after is not None:
        inner, place = kernel, len(operands)
        kernel = lambda *refs: inner(*refs[:place], *refs[place + 1 :])
        operands, specs = (*operands, after), [*specs, pl.BlockSpec(memory_space=pl.ANY)]
    return pl.pallas_call(
        kernel,
        in_specs=specs,
        out_specs=jax.tree.map(lambda _: IN_VMEM, shapes),
        out_shape=shapes,
        scratch_shapes=scratch,
        compiler_params=pltpu.CompilerParams(vmem_limit_bytes=VMEM),
        cost_estimate=pl.CostEstimate(flops=flops, transcendentals=transcendentals, bytes_accessed=moved),
    )(*operands)


def sends(count, rows):
    return [jax.ShapeDtypeStruct((count, rows + 16, BLOCK), jnp.bfloat16),
            jax.ShapeDtypeStruct((count, rows, BLOCK), jnp.float32)]


def local(activations, out_grads, query_in, query_out):
    per, rank, k_in = query_in.shape
    feat = jnp.reshape(lax.axis_index("feat"), (1,)).astype(jnp.int32)
    tok = jnp.reshape(lax.axis_index("tok"), (1,)).astype(jnp.int32)
    pairs = {
        "up": [(s, (s & 4) | ((s + 1) & 3)) for s in range(8)],
        "down": [(s, (s & 4) | ((s + 3) & 3)) for s in range(8)],
        "across": [(s, s ^ 4) for s in range(8)],
    }
    move = lambda value, way: lax.ppermute(value, "tok", pairs[way])

    own = jnp.concatenate([query_in, query_out], axis=2).reshape(per * rank, -1)
    factor = {"own": own, "own_up": move(own, "up"), "own_down": move(own, "down"), "far": move(own, "across")}
    acts, grads = load((activations, out_grads))
    turn = {"after": None}
    got, keep = {}, {}

    def away(c):
        blocks = [factor[name] for name in CHUNKS[c]]
        side, width = sum(b.shape[0] for b in blocks), own.shape[1]
        scratch = [pltpu.VMEM((side, width), jnp.bfloat16)]
        send = call(functools.partial(away_kernel, len(blocks), ORDERS[c]), sends(8, 2 * side)[0],
                    (feat, acts, grads, *blocks), 2 * 8 * BLOCK * side * width, 0, 1, scratch, **turn)
        turn["after"] = send
        got[c] = lax.ppermute(send, "feat", [(s, s ^ 1) for s in range(16)])

    def home(c):
        blocks = [factor[name] for name in CHUNKS[c]]
        side, width = sum(b.shape[0] for b in blocks), own.shape[1]
        scratch = [pltpu.VMEM((side, width), jnp.bfloat16)]
        send, keep[c] = call(functools.partial(home_kernel, len(blocks), ORDERS[c]), sends(4, 2 * side),
                             (feat, acts, grads, *blocks, got[c]), 2 * 8 * BLOCK * side * width, 0, 1, scratch, **turn)
        turn["after"] = send
        got[c] = halve(send, ORDERS[c], 0)

    def step(c, stage):
        count, rows = keep[c].shape[:2]
        send, keep[c] = call(step_kernel, sends(count // 2, rows), (keep[c], got[c]),
                             20 * count * rows * BLOCK, 0, 0, **turn)
        turn["after"] = send
        got[c] = halve(send, ORDERS[c], stage)

    away(0)
    own_up, far, _ = lax.optimization_barrier((factor["own_up"], factor["far"], turn["after"]))
    factor["own_two"] = move(own_up, "up")
    factor["far_down"] = move(far, "down")
    factor["far_up"] = move(own_up, "across")
    factor["far_two"] = move(factor["own_two"], "across")
    for item in PLAN:
        kind, c = item[0], item[1]
        if kind == "away":
            away(c)
        elif kind == "home":
            home(c)
        else:
            step(c, item[2])
    ends = [x for c in range(len(CHUNKS)) for x in (keep[c], got[c])]
    return call(last_kernel, jax.ShapeDtypeStruct((per * lax.axis_size("tok"), BLOCK), jnp.float32), (tok, *ends))


def solution(mesh):
    in_specs = (P("tok", "feat"), P("tok", "feat"), P("tok", None, "feat"), P("tok", None, "feat"))
    out_specs = P(None, ("tok", "feat"))
    return jax.shard_map(local, mesh=mesh, in_specs=in_specs, out_specs=out_specs, check_vma=False)
```

time: 561 us -> 91.8 us (0.16)
  waiting for transfers between devices: 413 us -> 28.2 us
  matrix products: 106 us -> 0 us
  Pallas kernels: 0 us -> 30.7 us
  starting transfers between devices: 3.68 us -> 31.5 us
  other arithmetic: 17.8 us -> 1 us
  between operations: 13.9 us -> 0.14 us
    reduce_scatter x8 -> x0, waiting for transfers between devices: 328 us -> none  [local(): summed = lax.psum_scatter(terms, 'feat', scatter_dimension=0, tiled=True)]
    dot_general x16 -> x0, matrix products: 106 us -> none  [the longest x8 77.8 us: local(): lax.dot_general(activations, in_side, (((1,), (1,)), ((), ())), preferred...]
    ppermute x7 -> x19, waiting for transfers between devices: 85.2 us -> 28.2 us  [the longest x9 25 us: halve(): lax.ppermute(value, 'feat', [(s, partner(s, orders[s & 1][stage])) for s...]
    pallas_call x0 -> x14, Pallas kernels: none -> 30.7 us  [the longest x13 24.2 us: call(): pl.pallas_call(kernel, in_specs=specs, out_specs=jax.tree.map(lambda _: I...]
    ppermute x7 -> x19, starting transfers between devices: 3.39 us -> 31.5 us  [the longest x7 15.7 us: local(): move = lambda value, way: lax.ppermute(value, 'tok', pairs[way])]
    another operation x8 -> x0, other arithmetic: 10.6 us -> none  [local(): jnp.stack([in_terms.reshape(row_count, -1, rank_size), out_terms.reshape(...]
    reduce_sum x8 -> x0, other arithmetic: 7.17 us -> none  [local(): jnp.sum(grouped[:, :, 0, :] * grouped[:, :, 1, :], axis=2)]
  transfers between devices with their start and end apart: 15 -> 19, of which waited for: 13 -> 7; matrix products, arithmetic and copies ran while one was open for 20% -> 0% of each run, Pallas kernels for 0% -> 24%
where the time goes in v2:
time: 91.8 us; the launch traced here: 91.5 us
  starting transfers between devices  31.5 us (34%)
  Pallas kernels  30.7 us (33%)
  waiting for transfers between devices  28.2 us (31%)
  other arithmetic  1 us (1%)
    ppermute x9, waiting for transfers between devices, halve(): lax.ppermute(value, 'feat', [(s, partner(s, orders[s & 1][stage])) for s...  25 us
    pallas_call x13, Pallas kernels, call(): pl.pallas_call(kernel, in_specs=specs, out_specs=jax.tree.map(lambda _: I...  24.2 us
    ppermute x7, starting transfers between devices, local(): move = lambda value, way: lax.ppermute(value, 'tok', pairs[way])  15.7 us
    ppermute x9, starting transfers between devices, halve(): lax.ppermute(value, 'feat', [(s, partner(s, orders[s & 1][stage])) for s...  12.4 us
    pallas_call x1, Pallas kernels, load(): pl.pallas_call(functools.partial(load_kernel, parts), in_specs=[pl.BlockS...  6.48 us
    ppermute x3, starting transfers between devices, away(): got[c] = lax.ppermute(send, 'feat', [(s, s ^ 1) for s in range(16)])  3.4 us
    ppermute x7, waiting for transfers between devices, local(): move = lambda value, way: lax.ppermute(value, 'tok', pairs[way])  3.23 us
  transfers between devices with their start and end apart: 19, of which 7 were waited for; matrix products, arithmetic and copies ran while one was open for 0% of the time, Pallas kernels for 24%

profile of v2, /device:TPU:1, one launch (start us, length us, event | category | flops | bytes accessed | tf_op | source)
XLA Modules:
  0.0 91.5 jit_solution(11935437126590349601)
XLA Ops:
  0.0 1.0 %pad_maximum_fusion = bf16[2,32,2304]{2,1,0:T(8,128)(2,1)S(1)} fusion(bf16[2,32,512]{2,1,0:T(8,128)(2,1)} %param.7, bf16[2,32,1792]{2,1,0:T(8,128)(2,1)} %param.6), kind=kLoop, calls=%fused_computation | loop fusion | flops 589824 | bytes 589824 | tf_op jit(solution)/shard_map/concatenate | solution.py:205
  1.0 2.5 %collective-permute-start = (bf16[64,2304]{1,0:T(8,128)(2,1)S(1)}, bf16[64,2304]{1,0:T(8,128)(2,1)S(1)}, u32[]{:S(2)}, u32[]{:S(2)}) collective-permute-start(bf16[64,2304]{1,0:T(8,128)(2,1)S(1)} %bitcast.3), channel_id=1, source_target_pairs={{0,16},{16,32},{32,48},{48,0},{64,80},{80,96},{96,112},{112,64},{1... | collective-permute-start | bytes 884744 | tf_op jit(solution)/shard_map/ppermute | solution.py:203
  3.5 2.2 %collective-permute-start.1 = (bf16[64,2304]{1,0:T(8,128)(2,1)S(1)}, bf16[64,2304]{1,0:T(8,128)(2,1)S(1)}, u32[]{:S(2)}, u32[]{:S(2)}) collective-permute-start(bf16[64,2304]{1,0:T(8,128)(2,1)S(1)} %bitcast.4), channel_id=1, source_target_pairs={{0,48},{16,0},{32,16},{48,32},{64,112},{80,64},{96,80},{112,96},{1... | collective-permute-start | bytes 884744 | tf_op jit(solution)/shard_map/ppermute | solution.py:203
  5.7 2.7 %collective-permute-start.2 = (bf16[64,2304]{1,0:T(8,128)(2,1)S(1)}, bf16[64,2304]{1,0:T(8,128)(2,1)S(1)}, u32[]{:S(2)}, u32[]{:S(2)}) collective-permute-start(bf16[64,2304]{1,0:T(8,128)(2,1)S(1)} %bitcast.5), channel_id=1, source_target_pairs={{0,64},{16,80},{32,96},{48,112},{64,0},{80,16},{96,32},{112,48},{1... | collective-permute-start | bytes 884744 | tf_op jit(solution)/shard_map/ppermute | solution.py:203
  8.5 6.5 %shard_map.46 = (bf16[4096,1792]{1,0:T(8,128)(2,1)S(1)}, bf16[4096,512]{1,0:T(8,128)(2,1)S(1)}) custom-call(bf16[4096,1792]{1,0:T(8,128)(2,1)} %act_ref.1, bf16[4096,512]{1,0:T(8,128)(2,1)} %grad_ref.1), custom_call_target="tpu_custom_call" | custom-call | bytes 18874368 | tf_op jit(solution)/shard_map/pallas_call | solution.py:115
  15.0 0.0 collective-permute-done.refs_0_.refs_3_
  15.0 0.0 collective-permute-done.2.refs_3_.refs_6_
  15.0 3.5 %shard_map.47.refs_8_ = bf16[8,528,256]{2,1,0:T(8,128)(2,1)S(1)} custom-call(s32[1]{0:T(128)} %bitcast.1.feat_ref.refs_0_, bf16[4096,1792]{1,0:T(8,128)(2,1)S(1)} %get-tuple-element.27.act_ref.refs_1_, bf16[4096,512]{1,0:T(8,128)(2,1)S(1)} %get-tuple-element.28.grad_ref.refs_2_, bf16[64,2304]{1,0:T(8,128)(2,1)S(1)} %collective-permute-done.refs_0_.refs_3_, ...), custom_call_target="tpu_custom_call" | custom-call | flops 2415919104 | bytes 20054020 | tf_op jit(solution)/shard_map/pallas_call | solution.py:178
  18.5 1.7 %collective-permute-start.3 = (bf16[8,528,256]{2,1,0:T(8,128)(2,1)S(1)}, bf16[8,528,256]{2,1,0:T(8,128)(2,1)S(1)}, u32[]{:S(2)}, u32[]{:S(2)}) collective-permute-start(bf16[8,528,256]{2,1,0:T(8,128)(2,1)S(1)} %shard_map.47.refs_8_), channel_id=1, source_target_pairs={{0,1},{1,0},{2,3},{3,2},{4,5},{5,4},{6,7},{7,6},{8,9},{9,8},{10,11... | collective-permute-start | bytes 6488072 | tf_op jit(solution)/shard_map/ppermute | solution.py:218
  20.2 0.0 collective-permute-start.5
  20.2 2.7 %collective-permute-start.6 = (bf16[64,2304]{1,0:T(8,128)(2,1)S(1)}, bf16[64,2304]{1,0:T(8,128)(2,1)S(1)}, u32[]{:S(2)}, u32[]{:S(2)}) collective-permute-start(bf16[64,2304]{1,0:T(8,128)(2,1)S(1)} %collective-permute-done.2.refs_3_.refs_6_), channel_id=1, source_target_pairs={{0,48},{16,0},{32,16},{48,32},{64,112},{80,64},{96,80},{112,96},{1... | collective-permute-start | bytes 884744 | tf_op jit(solution)/shard_map/ppermute | solution.py:203
  22.9 2.7 %collective-permute-start.7 = (bf16[64,2304]{1,0:T(8,128)(2,1)S(1)}, bf16[64,2304]{1,0:T(8,128)(2,1)S(1)}, u32[]{:S(2)}, u32[]{:S(2)}) collective-permute-start(bf16[64,2304]{1,0:T(8,128)(2,1)S(1)} %collective-permute-done.refs_0_.refs_3_), channel_id=1, source_target_pairs={{0,64},{16,80},{32,96},{48,112},{64,0},{80,16},{96,32},{112,48},{1... | collective-permute-start | bytes 884744 | tf_op jit(solution)/shard_map/ppermute | solution.py:203
  25.6 0.0 collective-permute-done.3.refs_7_
  25.6 3.5 %shard_map.48 = (bf16[4,528,256]{2,1,0:T(8,128)(2,1)S(1)}, f32[4,512,256]{2,1,0:T(8,128)S(1)}) custom-call(s32[1]{0:T(128)} %bitcast.1.feat_ref.refs_0_, bf16[4096,1792]{1,0:T(8,128)(2,1)S(1)} %get-tuple-element.27.act_ref.refs_1_, bf16[4096,512]{1,0:T(8,128)(2,1)S(1)} %get-tuple-element.28.grad_ref.refs_2_, ...), custom_call_target="tpu_custom_call" | custom-call | flops 2415919104 | bytes 22216708 | tf_op jit(solution)/shard_map/pallas_call | solution.py:178
  29.1 0.9 collective-permute-done.5.refs_3_
  30.0 2.3 %collective-permute-done.7.refs_5_ = bf16[64,2304]{1,0:T(8,128)(2,1)S(1)} collective-permute-done((bf16[64,2304]{1,0:T(8,128)(2,1)S(1)}, bf16[64,2304]{1,0:T(8,128)(2,1)S(1)}, u32[]{:S(2)}, u32[]{:S(2)}) %collective-permute-start.7) | collective-permute-done | bytes 294944 | tf_op jit(solution)/shard_map/ppermute | solution.py:203
  32.3 3.5 %shard_map.49.refs_7_ = bf16[8,400,256]{2,1,0:T(8,128)(2,1)S(1)} custom-call(s32[1]{0:T(128)} %bitcast.1.feat_ref.refs_0_, bf16[4096,1792]{1,0:T(8,128)(2,1)S(1)} %get-tuple-element.27.act_ref.refs_1_, bf16[4096,512]{1,0:T(8,128)(2,1)S(1)} %get-tuple-element.28.grad_ref.refs_2_, bf16[64,2304]{1,0:T(8,128)(2,1)S(1)} %collective-permute-done.5.refs_3_, ...), custom_call_target="tpu_custom_call" | custom-call | flops 1811939328 | bytes 19759108 | tf_op jit(solution)/shard_map/pallas_call | solution.py:178
  35.9 1.6 %collective-permute-start.8 = (bf16[8,400,256]{2,1,0:T(8,128)(2,1)S(1)}, bf16[8,400,256]{2,1,0:T(8,128)(2,1)S(1)}, u32[]{:S(2)}, u32[]{:S(2)}) collective-permute-start(bf16[8,400,256]{2,1,0:T(8,128)(2,1)S(1)} %shard_map.49.refs_7_), channel_id=1, source_target_pairs={{0,1},{1,0},{2,3},{3,2},{4,5},{5,4},{6,7},{7,6},{8,9},{9,8},{10,11... | collective-permute-start | bytes 4915208 | tf_op jit(solution)/shard_map/ppermute | solution.py:218
  37.4 2.7 %collective-permute-start.4 = (bf16[4,528,256]{2,1,0:T(8,128)(2,1)S(1)}, bf16[4,528,256]{2,1,0:T(8,128)(2,1)S(1)}, u32[]{:S(2)}, u32[]{:S(2)}) collective-permute-start(bf16[4,528,256]{2,1,0:T(8,128)(2,1)S(1)} %get-tuple-element.30.refs_6_), channel_id=1, source_target_pairs={{0,4},{1,13},{2,6},{3,15},{4,0},{5,9},{6,2},{7,11},{8,12},{9,5},{1... | collective-permute-start | bytes 3244040 | tf_op jit(solution)/shard_map/ppermute | solution.py:60
  40.2 2.8 %collective-permute-start.10 = (bf16[64,2304]{1,0:T(8,128)(2,1)S(1)}, bf16[64,2304]{1,0:T(8,128)(2,1)S(1)}, u32[]{:S(2)}, u32[]{:S(2)}) collective-permute-start(bf16[64,2304]{1,0:T(8,128)(2,1)S(1)} %collective-permute-done.5.refs_3_), channel_id=1, source_target_pairs={{0,64},{16,80},{32,96},{48,112},{64,0},{80,16},{96,32},{112,48},{1... | collective-permute-start | bytes 884744 | tf_op jit(solution)/shard_map/ppermute | solution.py:203
  42.9 3.6 %shard_map.50 = (bf16[4,400,256]{2,1,0:T(8,128)(2,1)S(1)}, f32[4,384,256]{2,1,0:T(8,128)S(1)}) custom-call(s32[1]{0:T(128)} %bitcast.1.feat_ref.refs_0_, bf16[4096,1792]{1,0:T(8,128)(2,1)S(1)} %get-tuple-element.27.act_ref.refs_1_, bf16[4096,512]{1,0:T(8,128)(2,1)S(1)} %get-tuple-element.28.grad_ref.refs_2_, ...), custom_call_target="tpu_custom_call" | custom-call | flops 1811939328 | bytes 21397508 | tf_op jit(solution)/shard_map/pallas_call | solution.py:178
  46.5 0.4 collective-permute-start.12
  47.0 5.7 %collective-permute-done.4.refs_1_ = bf16[4,528,256]{2,1,0:T(8,128)(2,1)S(1)} collective-permute-done((bf16[4,528,256]{2,1,0:T(8,128)(2,1)S(1)}, bf16[4,528,256]{2,1,0:T(8,128)(2,1)S(1)}, u32[]{:S(2)}, u32[]{:S(2)}) %collective-permute-start.4) | collective-permute-done | bytes 1081376 | tf_op jit(solution)/shard_map/ppermute | solution.py:60
  52.7 1.1 %shard_map.51 = (bf16[2,528,256]{2,1,0:T(8,128)(2,1)S(1)}, f32[2,512,256]{2,1,0:T(8,128)S(1)}) custom-call(f32[4,512,256]{2,1,0:T(8,128)S(1)} %get-tuple-element.29.refs_0_, bf16[4,528,256]{2,1,0:T(8,128)(2,1)S(1)} %collective-permute-done.4.refs_1_, bf16[4,400,256]{2,1,0:T(8,128)(2,1)S(1)} %get-tuple-element.33.refs_2_), custom_call_target="tpu_custom_call" | custom-call | flops 10485760 | bytes 3178496 | tf_op jit(solution)/shard_map/pallas_call | solution.py:178
  53.8 3.0 %shard_map.52.refs_2_ = bf16[8,144,256]{2,1,0:T(8,128)(2,1)S(1)} custom-call(s32[1]{0:T(128)} %bitcast.1.feat_ref.refs_0_, bf16[4096,1792]{1,0:T(8,128)(2,1)S(1)} %get-tuple-element.27.act_ref.refs_1_, bf16[4096,512]{1,0:T(8,128)(2,1)S(1)} %get-tuple-element.28.grad_ref.refs_2_, bf16[64,2304]{1,0:T(8,128)(2,1)S(1)} %collective-permute-done.10.refs_3_, ...), custom_call_target="tpu_custom_call" | custom-call | flops 603979776 | bytes 19169284 | tf_op jit(solution)/shard_map/pallas_call | solution.py:178
  56.8 0.1 collective-permute-start.13
  56.9 1.3 %collective-permute-start.9 = (bf16[2,528,256]{2,1,0:T(8,128)(2,1)S(1)}, bf16[2,528,256]{2,1,0:T(8,128)(2,1)S(1)}, u32[]{:S(2)}, u32[]{:S(2)}) collective-permute-start(bf16[2,528,256]{2,1,0:T(8,128)(2,1)S(1)} %get-tuple-element.35.refs_4_), channel_id=1, source_target_pairs={{0,2},{1,5},{2,0},{3,7},{4,6},{5,1},{6,4},{7,3},{8,10},{9,13},{10,... | collective-permute-start | bytes 1622024 | tf_op jit(solution)/shard_map/ppermute | solution.py:60
  58.2 7.3 %collective-permute-done.9.refs_1_ = bf16[2,528,256]{2,1,0:T(8,128)(2,1)S(1)} collective-permute-done((bf16[2,528,256]{2,1,0:T(8,128)(2,1)S(1)}, bf16[2,528,256]{2,1,0:T(8,128)(2,1)S(1)}, u32[]{:S(2)}, u32[]{:S(2)}) %collective-permute-start.9) | collective-permute-done | bytes 540704 | tf_op jit(solution)/shard_map/ppermute | solution.py:60
  65.5 0.5 shard_map.53
  66.0 0.0 collective-permute-done.13.refs_4_
  66.0 3.0 %shard_map.54 = (bf16[4,144,256]{2,1,0:T(8,128)(2,1)S(1)}, f32[4,128,256]{2,1,0:T(8,128)S(1)}) custom-call(s32[1]{0:T(128)} %bitcast.1.feat_ref.refs_0_, bf16[4096,1792]{1,0:T(8,128)(2,1)S(1)} %get-tuple-element.27.act_ref.refs_1_, bf16[4096,512]{1,0:T(8,128)(2,1)S(1)} %get-tuple-element.28.grad_ref.refs_2_, ...), custom_call_target="tpu_custom_call" | custom-call | flops 603979776 | bytes 19759108 | tf_op jit(solution)/shard_map/pallas_call | solution.py:178
  69.0 0.8 shard_map.55
  69.8 1.3 %collective-permute-start.14 = (bf16[2,400,256]{2,1,0:T(8,128)(2,1)S(1)}, bf16[2,400,256]{2,1,0:T(8,128)(2,1)S(1)}, u32[]{:S(2)}, u32[]{:S(2)}) collective-permute-start(bf16[2,400,256]{2,1,0:T(8,128)(2,1)S(1)} %get-tuple-element.41.refs_2_), channel_id=1, source_target_pairs={{0,12},{1,3},{2,14},{3,1},{4,8},{5,7},{6,10},{7,5},{8,4},{9,11},{1... | collective-permute-start | bytes 1228808 | tf_op jit(solution)/shard_map/ppermute | solution.py:60
  71.1 0.2 collective-permute-start.15
  71.4 1.2 %collective-permute-start.11 = (bf16[1,528,256]{2,1,0:T(8,128)(2,1)S(1)}, bf16[1,528,256]{2,1,0:T(8,128)(2,1)S(1)}, u32[]{:S(2)}, u32[]{:S(2)}) collective-permute-start(bf16[1,528,256]{2,1,0:T(8,128)(2,1)S(1)} %get-tuple-element.37.refs_5_), channel_id=1, source_target_pairs={{0,12},{1,3},{2,14},{3,1},{4,8},{5,7},{6,10},{7,5},{8,4},{9,11},{1... | collective-permute-start | bytes 811016 | tf_op jit(solution)/shard_map/ppermute | solution.py:60
  72.6 7.6 %collective-permute-done.15.refs_1_ = bf16[4,144,256]{2,1,0:T(8,128)(2,1)S(1)} collective-permute-done((bf16[4,144,256]{2,1,0:T(8,128)(2,1)S(1)}, bf16[4,144,256]{2,1,0:T(8,128)(2,1)S(1)}, u32[]{:S(2)}, u32[]{:S(2)}) %collective-permute-start.15) | collective-permute-done | bytes 294944 | tf_op jit(solution)/shard_map/ppermute | solution.py:60
  80.2 0.3 shard_map.56
  80.4 1.3 %collective-permute-start.17 = (bf16[2,144,256]{2,1,0:T(8,128)(2,1)S(1)}, bf16[2,144,256]{2,1,0:T(8,128)(2,1)S(1)}, u32[]{:S(2)}, u32[]{:S(2)}) collective-permute-start(bf16[2,144,256]{2,1,0:T(8,128)(2,1)S(1)} %get-tuple-element.43.refs_2_), channel_id=1, source_target_pairs={{0,2},{1,5},{2,0},{3,7},{4,6},{5,1},{6,4},{7,3},{8,10},{9,13},{10,... | collective-permute-start | bytes 442376 | tf_op jit(solution)/shard_map/ppermute | solution.py:60
  81.7 0.0 collective-permute-done.14.refs_1_
  81.7 0.4 shard_map.57
  82.1 0.4 collective-permute-start.16
  82.5 2.3 %collective-permute-done.17.refs_1_ = bf16[2,144,256]{2,1,0:T(8,128)(2,1)S(1)} collective-permute-done((bf16[2,144,256]{2,1,0:T(8,128)(2,1)S(1)}, bf16[2,144,256]{2,1,0:T(8,128)(2,1)S(1)}, u32[]{:S(2)}, u32[]{:S(2)}) %collective-permute-start.17) | collective-permute-done | bytes 147488 | tf_op jit(solution)/shard_map/ppermute | solution.py:60
  84.8 0.1 shard_map.58
  84.9 3.6 %collective-permute-start.18 = (bf16[1,144,256]{2,1,0:T(8,128)(2,1)S(1)}, bf16[1,144,256]{2,1,0:T(8,128)(2,1)S(1)}, u32[]{:S(2)}, u32[]{:S(2)}) collective-permute-start(bf16[1,144,256]{2,1,0:T(8,128)(2,1)S(1)} %get-tuple-element.48), channel_id=1, source_target_pairs={{0,12},{1,13},{2,14},{3,15},{4,8},{5,9},{6,10},{7,11},{8,4},{9,5},... | collective-permute-start | bytes 221192 | tf_op jit(solution)/shard_map/ppermute | solution.py:60
  88.5 0.0 collective-permute-done.11.refs_1_
  88.5 2.0 %collective-permute-done.18.refs_5_ = bf16[1,144,256]{2,1,0:T(8,128)(2,1)S(1)} collective-permute-done((bf16[1,144,256]{2,1,0:T(8,128)(2,1)S(1)}, bf16[1,144,256]{2,1,0:T(8,128)(2,1)S(1)}, u32[]{:S(2)}, u32[]{:S(2)}) %collective-permute-start.18) | collective-permute-done | bytes 73760 | tf_op jit(solution)/shard_map/ppermute | solution.py:60
  90.6 0.0 collective-permute-done.16.refs_3_
  90.6 1.0 %shard_map.59 = f32[16,256]{1,0:T(8,128)} custom-call(s32[1]{0:T(128)} %bitcast.tok_ref, f32[1,512,256]{2,1,0:T(8,128)S(1)} %get-tuple-element.36.refs_0_, bf16[1,528,256]{2,1,0:T(8,128)(2,1)S(1)} %collective-permute-done.11.refs_1_, f32[1,384,256]{2,1,0:T(8,128)S(1)} %get-tuple-element.44.refs_2_, bf16[1,400,256]{2,1,0:T(8,128)(2,1)S(1)} %collective-permute-done.16.refs_3_, ...), custom_call_target="tpu_custom_call" | custom-call | bytes 1597444 | tf_op jit(solution)/shard_map/pallas_call | solution.py:178
  (5 shorter events, 0.0 us)
Async XLA Ops:
  1.0 14.0 %collective-permute-start = (bf16[64,2304]{1,0:T(8,128)(2,1)S(1)}, bf16[64,2304]{1,0:T(8,128)(2,1)S(1)}, u32[]{:S(2)}, u32[]{:S(2)}) collective-permute-start(bf16[64,2304]{1,0:T(8,128)(2,1)S(1)} %bitcast.3), channel_id=1, source_target_pairs={{0,16},{16,32},{32,48},{48,0},{64,80},{80,96},{96,112},{112,64},{1... | collective-permute-start | bytes 884744 | tf_op jit(solution)/shard_map/ppermute | solution.py:203
  3.5 11.4 %collective-permute-start.1 = (bf16[64,2304]{1,0:T(8,128)(2,1)S(1)}, bf16[64,2304]{1,0:T(8,128)(2,1)S(1)}, u32[]{:S(2)}, u32[]{:S(2)}) collective-permute-start(bf16[64,2304]{1,0:T(8,128)(2,1)S(1)} %bitcast.4), channel_id=1, source_target_pairs={{0,48},{16,0},{32,16},{48,32},{64,112},{80,64},{96,80},{112,96},{1... | collective-permute-start | bytes 884744 | tf_op jit(solution)/shard_map/ppermute | solution.py:203
  5.7 9.3 %collective-permute-start.2 = (bf16[64,2304]{1,0:T(8,128)(2,1)S(1)}, bf16[64,2304]{1,0:T(8,128)(2,1)S(1)}, u32[]{:S(2)}, u32[]{:S(2)}) collective-permute-start(bf16[64,2304]{1,0:T(8,128)(2,1)S(1)} %bitcast.5), channel_id=1, source_target_pairs={{0,64},{16,80},{32,96},{48,112},{64,0},{80,16},{96,32},{112,48},{1... | collective-permute-start | bytes 884744 | tf_op jit(solution)/shard_map/ppermute | solution.py:203
  18.5 7.2 %collective-permute-start.3 = (bf16[8,528,256]{2,1,0:T(8,128)(2,1)S(1)}, bf16[8,528,256]{2,1,0:T(8,128)(2,1)S(1)}, u32[]{:S(2)}, u32[]{:S(2)}) collective-permute-start(bf16[8,528,256]{2,1,0:T(8,128)(2,1)S(1)} %shard_map.47.refs_8_), channel_id=1, source_target_pairs={{0,1},{1,0},{2,3},{3,2},{4,5},{5,4},{6,7},{7,6},{8,9},{9,8},{10,11... | collective-permute-start | bytes 6488072 | tf_op jit(solution)/shard_map/ppermute | solution.py:218
  20.2 9.8 %collective-permute-start.5 = (bf16[64,2304]{1,0:T(8,128)(2,1)S(1)}, bf16[64,2304]{1,0:T(8,128)(2,1)S(1)}, u32[]{:S(2)}, u32[]{:S(2)}) collective-permute-start(bf16[64,2304]{1,0:T(8,128)(2,1)S(1)} %collective-permute-done.refs_0_.refs_3_), channel_id=1, source_target_pairs={{0,16},{16,32},{32,48},{48,0},{64,80},{80,96},{96,112},{112,64},{1... | collective-permute-start | bytes 884744 | tf_op jit(solution)/shard_map/ppermute | solution.py:203
  20.2 9.8 %collective-permute-start.6 = (bf16[64,2304]{1,0:T(8,128)(2,1)S(1)}, bf16[64,2304]{1,0:T(8,128)(2,1)S(1)}, u32[]{:S(2)}, u32[]{:S(2)}) collective-permute-start(bf16[64,2304]{1,0:T(8,128)(2,1)S(1)} %collective-permute-done.2.refs_3_.refs_6_), channel_id=1, source_target_pairs={{0,48},{16,0},{32,16},{48,32},{64,112},{80,64},{96,80},{112,96},{1... | collective-permute-start | bytes 884744 | tf_op jit(solution)/shard_map/ppermute | solution.py:203
  22.9 9.4 %collective-permute-start.7 = (bf16[64,2304]{1,0:T(8,128)(2,1)S(1)}, bf16[64,2304]{1,0:T(8,128)(2,1)S(1)}, u32[]{:S(2)}, u32[]{:S(2)}) collective-permute-start(bf16[64,2304]{1,0:T(8,128)(2,1)S(1)} %collective-permute-done.refs_0_.refs_3_), channel_id=1, source_target_pairs={{0,64},{16,80},{32,96},{48,112},{64,0},{80,16},{96,32},{112,48},{1... | collective-permute-start | bytes 884744 | tf_op jit(solution)/shard_map/ppermute | solution.py:203
  35.9 7.1 %collective-permute-start.8 = (bf16[8,400,256]{2,1,0:T(8,128)(2,1)S(1)}, bf16[8,400,256]{2,1,0:T(8,128)(2,1)S(1)}, u32[]{:S(2)}, u32[]{:S(2)}) collective-permute-start(bf16[8,400,256]{2,1,0:T(8,128)(2,1)S(1)} %shard_map.49.refs_7_), channel_id=1, source_target_pairs={{0,1},{1,0},{2,3},{3,2},{4,5},{5,4},{6,7},{7,6},{8,9},{9,8},{10,11... | collective-permute-start | bytes 4915208 | tf_op jit(solution)/shard_map/ppermute | solution.py:218
  37.4 15.3 %collective-permute-start.4 = (bf16[4,528,256]{2,1,0:T(8,128)(2,1)S(1)}, bf16[4,528,256]{2,1,0:T(8,128)(2,1)S(1)}, u32[]{:S(2)}, u32[]{:S(2)}) collective-permute-start(bf16[4,528,256]{2,1,0:T(8,128)(2,1)S(1)} %get-tuple-element.30.refs_6_), channel_id=1, source_target_pairs={{0,4},{1,13},{2,6},{3,15},{4,0},{5,9},{6,2},{7,11},{8,12},{9,5},{1... | collective-permute-start | bytes 3244040 | tf_op jit(solution)/shard_map/ppermute | solution.py:60
  40.2 13.6 %collective-permute-start.10 = (bf16[64,2304]{1,0:T(8,128)(2,1)S(1)}, bf16[64,2304]{1,0:T(8,128)(2,1)S(1)}, u32[]{:S(2)}, u32[]{:S(2)}) collective-permute-start(bf16[64,2304]{1,0:T(8,128)(2,1)S(1)} %collective-permute-done.5.refs_3_), channel_id=1, source_target_pairs={{0,64},{16,80},{32,96},{48,112},{64,0},{80,16},{96,32},{112,48},{1... | collective-permute-start | bytes 884744 | tf_op jit(solution)/shard_map/ppermute | solution.py:203
  46.5 22.5 %collective-permute-start.12 = (bf16[4,400,256]{2,1,0:T(8,128)(2,1)S(1)}, bf16[4,400,256]{2,1,0:T(8,128)(2,1)S(1)}, u32[]{:S(2)}, u32[]{:S(2)}) collective-permute-start(bf16[4,400,256]{2,1,0:T(8,128)(2,1)S(1)} %get-tuple-element.33.refs_2_), channel_id=1, source_target_pairs={{0,2},{1,13},{2,0},{3,15},{4,6},{5,9},{6,4},{7,11},{8,10},{9,5},{1... | collective-permute-start | bytes 2457608 | tf_op jit(solution)/shard_map/ppermute | solution.py:60
  56.8 9.2 %collective-permute-start.13 = (bf16[8,144,256]{2,1,0:T(8,128)(2,1)S(1)}, bf16[8,144,256]{2,1,0:T(8,128)(2,1)S(1)}, u32[]{:S(2)}, u32[]{:S(2)}) collective-permute-start(bf16[8,144,256]{2,1,0:T(8,128)(2,1)S(1)} %shard_map.52.refs_2_), channel_id=1, source_target_pairs={{0,1},{1,0},{2,3},{3,2},{4,5},{5,4},{6,7},{7,6},{8,9},{9,8},{10,11... | collective-permute-start | bytes 1769480 | tf_op jit(solution)/shard_map/ppermute | solution.py:218
  56.9 8.6 %collective-permute-start.9 = (bf16[2,528,256]{2,1,0:T(8,128)(2,1)S(1)}, bf16[2,528,256]{2,1,0:T(8,128)(2,1)S(1)}, u32[]{:S(2)}, u32[]{:S(2)}) collective-permute-start(bf16[2,528,256]{2,1,0:T(8,128)(2,1)S(1)} %get-tuple-element.35.refs_4_), channel_id=1, source_target_pairs={{0,2},{1,5},{2,0},{3,7},{4,6},{5,1},{6,4},{7,3},{8,10},{9,13},{10,... | collective-permute-start | bytes 1622024 | tf_op jit(solution)/shard_map/ppermute | solution.py:60
  69.8 11.9 %collective-permute-start.14 = (bf16[2,400,256]{2,1,0:T(8,128)(2,1)S(1)}, bf16[2,400,256]{2,1,0:T(8,128)(2,1)S(1)}, u32[]{:S(2)}, u32[]{:S(2)}) collective-permute-start(bf16[2,400,256]{2,1,0:T(8,128)(2,1)S(1)} %get-tuple-element.41.refs_2_), channel_id=1, source_target_pairs={{0,12},{1,3},{2,14},{3,1},{4,8},{5,7},{6,10},{7,5},{8,4},{9,11},{1... | collective-permute-start | bytes 1228808 | tf_op jit(solution)/shard_map/ppermute | solution.py:60
  71.1 9.0 %collective-permute-start.15 = (bf16[4,144,256]{2,1,0:T(8,128)(2,1)S(1)}, bf16[4,144,256]{2,1,0:T(8,128)(2,1)S(1)}, u32[]{:S(2)}, u32[]{:S(2)}) collective-permute-start(bf16[4,144,256]{2,1,0:T(8,128)(2,1)S(1)} %get-tuple-element.39.refs_2_), channel_id=1, source_target_pairs={{0,4},{1,3},{2,6},{3,1},{4,0},{5,7},{6,2},{7,5},{8,12},{9,11},{10,... | collective-permute-start | bytes 884744 | tf_op jit(solution)/shard_map/ppermute | solution.py:60
  71.4 17.1 %collective-permute-start.11 = (bf16[1,528,256]{2,1,0:T(8,128)(2,1)S(1)}, bf16[1,528,256]{2,1,0:T(8,128)(2,1)S(1)}, u32[]{:S(2)}, u32[]{:S(2)}) collective-permute-start(bf16[1,528,256]{2,1,0:T(8,128)(2,1)S(1)} %get-tuple-element.37.refs_5_), channel_id=1, source_target_pairs={{0,12},{1,3},{2,14},{3,1},{4,8},{5,7},{6,10},{7,5},{8,4},{9,11},{1... | collective-permute-start | bytes 811016 | tf_op jit(solution)/shard_map/ppermute | solution.py:60
  80.4 4.4 %collective-permute-start.17 = (bf16[2,144,256]{2,1,0:T(8,128)(2,1)S(1)}, bf16[2,144,256]{2,1,0:T(8,128)(2,1)S(1)}, u32[]{:S(2)}, u32[]{:S(2)}) collective-permute-start(bf16[2,144,256]{2,1,0:T(8,128)(2,1)S(1)} %get-tuple-element.43.refs_2_), channel_id=1, source_target_pairs={{0,2},{1,5},{2,0},{3,7},{4,6},{5,1},{6,4},{7,3},{8,10},{9,13},{10,... | collective-permute-start | bytes 442376 | tf_op jit(solution)/shard_map/ppermute | solution.py:60
  82.1 8.5 %collective-permute-start.16 = (bf16[1,400,256]{2,1,0:T(8,128)(2,1)S(1)}, bf16[1,400,256]{2,1,0:T(8,128)(2,1)S(1)}, u32[]{:S(2)}, u32[]{:S(2)}) collective-permute-start(bf16[1,400,256]{2,1,0:T(8,128)(2,1)S(1)} %get-tuple-element.45.refs_2_), channel_id=1, source_target_pairs={{0,4},{1,5},{2,6},{3,7},{4,0},{5,1},{6,2},{7,3},{8,12},{9,13},{10,... | collective-permute-start | bytes 614408 | tf_op jit(solution)/shard_map/ppermute | solution.py:60
  84.9 5.6 %collective-permute-start.18 = (bf16[1,144,256]{2,1,0:T(8,128)(2,1)S(1)}, bf16[1,144,256]{2,1,0:T(8,128)(2,1)S(1)}, u32[]{:S(2)}, u32[]{:S(2)}) collective-permute-start(bf16[1,144,256]{2,1,0:T(8,128)(2,1)S(1)} %get-tuple-element.48), channel_id=1, source_target_pairs={{0,12},{1,13},{2,14},{3,15},{4,8},{5,9},{6,10},{7,11},{8,4},{9,5},... | collective-permute-start | bytes 221192 | tf_op jit(solution)/shard_map/ppermute | solution.py:60

commit v3 on v2

--- a/solution.py
+++ b/solution.py
@@ -18,18 +18,19 @@
 
 G1, G0, X = 2, 1, 0
 ORDERS = (
-    ((G0, X, G1), (G1, G0, X)),
+    ((G0, G1, X), (G1, X, G0)),
+    ((X, G0, G1), (G0, G1, X)),
     ((X, G1, G0), (G1, X, G0)),
-    ((G0, X, G1), (X, G0, G1)),
 )
 CHUNKS = (
     ("own_up", "own_down", "own", "far"),
     ("own_two", "far_down", "far_up"),
     ("far_two",),
 )
+COST = 1024
 PLAN = (
-    ("home", 0), ("away", 1), ("home", 1), ("step", 0, 1), ("away", 2), ("step", 0, 2), ("home", 2),
-    ("step", 1, 1), ("step", 2, 1), ("step", 1, 2), ("step", 2, 2),
+    ("away", 0), ("home", 0), ("pass", 2), ("away", 1), ("home", 1), ("away", 2), ("step", 0, 1), ("home", 2),
+    ("step", 1, 1), ("step", 0, 2), ("step", 2, 1), ("step", 1, 2), ("step", 2, 2),
 )
 OWNERS = {
     "own": (0, 0), "far": (4, 0), "own_up": (0, 3), "own_down": (0, 1),
@@ -168,7 +169,7 @@
                 out_ref[pl.ds(owner * per + k, 1), :] = score[i * per + k : i * per + k + 1, :]
 
 
-def call(kernel, shapes, operands, flops=0, transcendentals=0, scalars=1, scratch=(), after=None):
+def call(kernel, shapes, operands, flops=0, transcendentals=0, scalars=1, scratch=(), after=None, name=None):
     moved = sum(o.size * o.dtype.itemsize for o in operands)
     specs = [IN_SMEM] * scalars + [IN_VMEM] * (len(operands) - scalars)
     if after is not None:
@@ -181,8 +182,9 @@
         out_specs=jax.tree.map(lambda _: IN_VMEM, shapes),
         out_shape=shapes,
         scratch_shapes=scratch,
+        name=name,
         compiler_params=pltpu.CompilerParams(vmem_limit_bytes=VMEM),
-        cost_estimate=pl.CostEstimate(flops=flops, transcendentals=transcendentals, bytes_accessed=moved),
+        cost_estimate=pl.CostEstimate(flops=flops, transcendentals=0, bytes_accessed=1024),
     )(*operands)
 
 
@@ -213,7 +215,7 @@
         side, width = sum(b.shape[0] for b in blocks), own.shape[1]
         scratch = [pltpu.VMEM((side, width), jnp.bfloat16)]
         send = call(functools.partial(away_kernel, len(blocks), ORDERS[c]), sends(8, 2 * side)[0],
-                    (feat, acts, grads, *blocks), 2 * 8 * BLOCK * side * width, 0, 1, scratch, **turn)
+                    (feat, acts, grads, *blocks), 1024, 0, 1, scratch, name=f"away_{c}", **turn)
         turn["after"] = send
         got[c] = lax.ppermute(send, "feat", [(s, s ^ 1) for s in range(16)])
 
@@ -222,29 +224,29 @@
         side, width = sum(b.shape[0] for b in blocks), own.shape[1]
         scratch = [pltpu.VMEM((side, width), jnp.bfloat16)]
         send, keep[c] = call(functools.partial(home_kernel, len(blocks), ORDERS[c]), sends(4, 2 * side),
-                             (feat, acts, grads, *blocks, got[c]), 2 * 8 * BLOCK * side * width, 0, 1, scratch, **turn)
+                             (feat, acts, grads, *blocks, got[c]), 1024, 0, 1, scratch, name=f"home_{c}", **turn)
         turn["after"] = send
         got[c] = halve(send, ORDERS[c], 0)
 
     def step(c, stage):
         count, rows = keep[c].shape[:2]
         send, keep[c] = call(step_kernel, sends(count // 2, rows), (keep[c], got[c]),
-                             20 * count * rows * BLOCK, 0, 0, **turn)
+                             COST, 0, 0, name=f"step_{c}_{stage}", **turn)
         turn["after"] = send
         got[c] = halve(send, ORDERS[c], stage)
 
-    away(0)
-    own_up, far, _ = lax.optimization_barrier((factor["own_up"], factor["far"], turn["after"]))
-    factor["own_two"] = move(own_up, "up")
-    factor["far_down"] = move(far, "down")
-    factor["far_up"] = move(own_up, "across")
-    factor["far_two"] = move(factor["own_two"], "across")
+    factor["own_two"] = move(factor["own_up"], "up")
+    factor["far_down"] = move(factor["far"], "down")
+    factor["far_up"] = move(factor["own_up"], "across")
     for item in PLAN:
         kind, c = item[0], item[1]
         if kind == "away":
             away(c)
         elif kind == "home":
             home(c)
+        elif kind == "pass":
+            ahead, _ = lax.optimization_barrier((factor["own_two"], turn["after"]))
+            factor["far_two"] = move(ahead, "across")
         else:
             step(c, item[2])
     ends = [x for c in range(len(CHUNKS)) for x in (keep[c], got[c])]

time: 91.8 us -> 84.2 us (0.917)
  starting transfers between devices: 31.5 us -> 24.3 us
    ppermute x9, waiting for transfers between devices: 25 us -> 18.5 us  [halve(): lax.ppermute(value, 'feat', [(s, partner(s, orders[s & 1][stage])) for s...]
    ppermute x7, waiting for transfers between devices: 3.23 us -> 8.28 us  [local(): move = lambda value, way: lax.ppermute(value, 'tok', pairs[way])]
    ppermute x9, starting transfers between devices: 12.4 us -> 8.95 us  [halve(): lax.ppermute(value, 'feat', [(s, partner(s, orders[s & 1][stage])) for s...]
    ppermute x7, starting transfers between devices: 15.7 us -> 12.6 us  [local(): move = lambda value, way: lax.ppermute(value, 'tok', pairs[way])]
  transfers between devices with their start and end apart: 19 -> 19, of which waited for: 7 -> 9; matrix products, arithmetic and copies ran while one was open for 0% -> 0% of each run, Pallas kernels for 24% -> 27%
where the time goes in v3:
time: 84.2 us; the launch traced here: 83.6 us
  Pallas kernels  30.7 us (36%)
  waiting for transfers between devices  27.5 us (33%)
  starting transfers between devices  24.3 us (29%)
  other arithmetic  1 us (1%)
    pallas_call x13, Pallas kernels, call(): pl.pallas_call(kernel, in_specs=specs, out_specs=jax.tree.map(lambda _: I...  24.2 us
    ppermute x9, waiting for transfers between devices, halve(): lax.ppermute(value, 'feat', [(s, partner(s, orders[s & 1][stage])) for s...  18.5 us
    ppermute x7, starting transfers between devices, local(): move = lambda value, way: lax.ppermute(value, 'tok', pairs[way])  12.6 us
    ppermute x9, starting transfers between devices, halve(): lax.ppermute(value, 'feat', [(s, partner(s, orders[s & 1][stage])) for s...  8.95 us
    ppermute x7, waiting for transfers between devices, local(): move = lambda value, way: lax.ppermute(value, 'tok', pairs[way])  8.28 us
    pallas_call x1, Pallas kernels, load(): pl.pallas_call(functools.partial(load_kernel, parts), in_specs=[pl.BlockS...  6.48 us
    ppermute x3, starting transfers between devices, away(): got[c] = lax.ppermute(send, 'feat', [(s, s ^ 1) for s in range(16)])  2.67 us
  transfers between devices with their start and end apart: 19, of which 9 were waited for; matrix products, arithmetic and copies ran while one was open for 0% of the time, Pallas kernels for 27%

profile of v3, /device:TPU:1, one launch (start us, length us, event | category | flops | bytes accessed | tf_op | source)
XLA Modules:
  0.0 83.6 jit_solution(15421365847844205242)
XLA Ops:
  0.0 1.0 %pad_maximum_fusion = bf16[2,32,2304]{2,1,0:T(8,128)(2,1)S(1)} fusion(bf16[2,32,512]{2,1,0:T(8,128)(2,1)} %param.7, bf16[2,32,1792]{2,1,0:T(8,128)(2,1)} %param.6), kind=kLoop, calls=%fused_computation | loop fusion | flops 589824 | bytes 589824 | tf_op jit(solution)/shard_map/concatenate | solution.py:207
  1.0 2.5 %collective-permute-start = (bf16[64,2304]{1,0:T(8,128)(2,1)S(1)}, bf16[64,2304]{1,0:T(8,128)(2,1)S(1)}, u32[]{:S(2)}, u32[]{:S(2)}) collective-permute-start(bf16[64,2304]{1,0:T(8,128)(2,1)S(1)} %bitcast.3), channel_id=1, source_target_pairs={{0,16},{16,32},{32,48},{48,0},{64,80},{80,96},{96,112},{112,64},{1... | collective-permute-start | bytes 884744 | tf_op jit(solution)/shard_map/ppermute | solution.py:205
  3.5 2.7 %collective-permute-start.2 = (bf16[64,2304]{1,0:T(8,128)(2,1)S(1)}, bf16[64,2304]{1,0:T(8,128)(2,1)S(1)}, u32[]{:S(2)}, u32[]{:S(2)}) collective-permute-start(bf16[64,2304]{1,0:T(8,128)(2,1)S(1)} %bitcast.4), channel_id=1, source_target_pairs={{0,64},{16,80},{32,96},{48,112},{64,0},{80,16},{96,32},{112,48},{1... | collective-permute-start | bytes 884744 | tf_op jit(solution)/shard_map/ppermute | solution.py:205
  6.3 2.2 %collective-permute-start.1 = (bf16[64,2304]{1,0:T(8,128)(2,1)S(1)}, bf16[64,2304]{1,0:T(8,128)(2,1)S(1)}, u32[]{:S(2)}, u32[]{:S(2)}) collective-permute-start(bf16[64,2304]{1,0:T(8,128)(2,1)S(1)} %bitcast.5), channel_id=1, source_target_pairs={{0,48},{16,0},{32,16},{48,32},{64,112},{80,64},{96,80},{112,96},{1... | collective-permute-start | bytes 884744 | tf_op jit(solution)/shard_map/ppermute | solution.py:205
  8.5 6.5 %shard_map.46 = (bf16[4096,1792]{1,0:T(8,128)(2,1)S(1)}, bf16[4096,512]{1,0:T(8,128)(2,1)S(1)}) custom-call(bf16[4096,1792]{1,0:T(8,128)(2,1)} %act_ref.1, bf16[4096,512]{1,0:T(8,128)(2,1)} %grad_ref.1), custom_call_target="tpu_custom_call" | custom-call | bytes 18874368 | tf_op jit(solution)/shard_map/pallas_call | solution.py:116
  15.0 0.0 collective-permute-done.1.refs_1_.refs_4_
  15.0 3.5 %away_0.1.refs_8_ = bf16[8,528,256]{2,1,0:T(8,128)(2,1)S(1)} custom-call(s32[1]{0:T(128)} %bitcast.1.feat_ref.refs_0_, bf16[4096,1792]{1,0:T(8,128)(2,1)S(1)} %get-tuple-element.26.act_ref.refs_1_, bf16[4096,512]{1,0:T(8,128)(2,1)S(1)} %get-tuple-element.27.grad_ref.refs_2_, bf16[64,2304]{1,0:T(8,128)(2,1)S(1)} %collective-permute-done.refs_0_.refs_3_, ...), custom_call_target="tpu_custom_call" | custom-call | flops 1024 | bytes 1024 | tf_op jit(solution)/shard_map/away_0/pallas_call | solution.py:179
  18.5 1.3 %collective-permute-start.3 = (bf16[8,528,256]{2,1,0:T(8,128)(2,1)S(1)}, bf16[8,528,256]{2,1,0:T(8,128)(2,1)S(1)}, u32[]{:S(2)}, u32[]{:S(2)}) collective-permute-start(bf16[8,528,256]{2,1,0:T(8,128)(2,1)S(1)} %away_0.1.refs_8_), channel_id=1, source_target_pairs={{0,1},{1,0},{2,3},{3,2},{4,5},{5,4},{6,7},{7,6},{8,9},{9,8},{10,11... | collective-permute-start | bytes 6488072 | tf_op jit(solution)/shard_map/ppermute | solution.py:220
  19.8 1.1 %collective-permute-start.5 = (bf16[64,2304]{1,0:T(8,128)(2,1)S(1)}, bf16[64,2304]{1,0:T(8,128)(2,1)S(1)}, u32[]{:S(2)}, u32[]{:S(2)}) collective-permute-start(bf16[64,2304]{1,0:T(8,128)(2,1)S(1)} %collective-permute-done.refs_0_.refs_3_), channel_id=1, source_target_pairs={{0,16},{16,32},{32,48},{48,0},{64,80},{80,96},{96,112},{112,64},{1... | collective-permute-start | bytes 884744 | tf_op jit(solution)/shard_map/ppermute | solution.py:205
  20.9 1.5 %collective-permute-start.8 = (bf16[64,2304]{1,0:T(8,128)(2,1)S(1)}, bf16[64,2304]{1,0:T(8,128)(2,1)S(1)}, u32[]{:S(2)}, u32[]{:S(2)}) collective-permute-start(bf16[64,2304]{1,0:T(8,128)(2,1)S(1)} %collective-permute-done.refs_0_.refs_3_), channel_id=1, source_target_pairs={{0,64},{16,80},{32,96},{48,112},{64,0},{80,16},{96,32},{112,48},{1... | collective-permute-start | bytes 884744 | tf_op jit(solution)/shard_map/ppermute | solution.py:205
  22.4 1.0 %collective-permute-start.7 = (bf16[64,2304]{1,0:T(8,128)(2,1)S(1)}, bf16[64,2304]{1,0:T(8,128)(2,1)S(1)}, u32[]{:S(2)}, u32[]{:S(2)}) collective-permute-start(bf16[64,2304]{1,0:T(8,128)(2,1)S(1)} %collective-permute-done.2.refs_3_.refs_6_), channel_id=1, source_target_pairs={{0,48},{16,0},{32,16},{48,32},{64,112},{80,64},{96,80},{112,96},{1... | collective-permute-start | bytes 884744 | tf_op jit(solution)/shard_map/ppermute | solution.py:205
  23.4 0.2 collective-permute-done.3.refs_7_
  23.7 3.5 %home_0.1 = (bf16[4,528,256]{2,1,0:T(8,128)(2,1)S(1)}, f32[4,512,256]{2,1,0:T(8,128)S(1)}) custom-call(s32[1]{0:T(128)} %bitcast.1.feat_ref.refs_0_, bf16[4096,1792]{1,0:T(8,128)(2,1)S(1)} %get-tuple-element.26.act_ref.refs_1_, bf16[4096,512]{1,0:T(8,128)(2,1)S(1)} %get-tuple-element.27.grad_ref.refs_2_, ...), custom_call_target="tpu_custom_call" | custom-call | flops 1024 | bytes 1024 | tf_op jit(solution)/shard_map/home_0/pallas_call | solution.py:179
  27.2 2.8 %collective-permute-done.5.refs_3_ = bf16[64,2304]{1,0:T(8,128)(2,1)S(1)} collective-permute-done((bf16[64,2304]{1,0:T(8,128)(2,1)S(1)}, bf16[64,2304]{1,0:T(8,128)(2,1)S(1)}, u32[]{:S(2)}, u32[]{:S(2)}) %collective-permute-start.5) | collective-permute-done | bytes 294944 | tf_op jit(solution)/shard_map/ppermute | solution.py:205
  30.0 0.7 collective-permute-done.8.refs_5_
  30.7 0.0 collective-permute-done.7.refs_4_
  30.7 3.5 %away_1.1.refs_7_ = bf16[8,400,256]{2,1,0:T(8,128)(2,1)S(1)} custom-call(s32[1]{0:T(128)} %bitcast.1.feat_ref.refs_0_, bf16[4096,1792]{1,0:T(8,128)(2,1)S(1)} %get-tuple-element.26.act_ref.refs_1_, bf16[4096,512]{1,0:T(8,128)(2,1)S(1)} %get-tuple-element.27.grad_ref.refs_2_, bf16[64,2304]{1,0:T(8,128)(2,1)S(1)} %collective-permute-done.5.refs_3_, ...), custom_call_target="tpu_custom_call" | custom-call | flops 1024 | bytes 1024 | tf_op jit(solution)/shard_map/away_1/pallas_call | solution.py:179
  34.2 1.3 %collective-permute-start.9 = (bf16[8,400,256]{2,1,0:T(8,128)(2,1)S(1)}, bf16[8,400,256]{2,1,0:T(8,128)(2,1)S(1)}, u32[]{:S(2)}, u32[]{:S(2)}) collective-permute-start(bf16[8,400,256]{2,1,0:T(8,128)(2,1)S(1)} %away_1.1.refs_7_), channel_id=1, source_target_pairs={{0,1},{1,0},{2,3},{3,2},{4,5},{5,4},{6,7},{7,6},{8,9},{9,8},{10,11... | collective-permute-start | bytes 4915208 | tf_op jit(solution)/shard_map/ppermute | solution.py:220
  35.4 2.7 %collective-permute-start.4 = (bf16[4,528,256]{2,1,0:T(8,128)(2,1)S(1)}, bf16[4,528,256]{2,1,0:T(8,128)(2,1)S(1)}, u32[]{:S(2)}, u32[]{:S(2)}) collective-permute-start(bf16[4,528,256]{2,1,0:T(8,128)(2,1)S(1)} %get-tuple-element.29.refs_6_), channel_id=1, source_target_pairs={{0,4},{1,13},{2,6},{3,15},{4,0},{5,9},{6,2},{7,11},{8,12},{9,5},{1... | collective-permute-start | bytes 3244040 | tf_op jit(solution)/shard_map/ppermute | solution.py:61
  38.2 1.5 %collective-permute-start.6 = (bf16[64,2304]{1,0:T(8,128)(2,1)S(1)}, bf16[64,2304]{1,0:T(8,128)(2,1)S(1)}, u32[]{:S(2)}, u32[]{:S(2)}) collective-permute-start(bf16[64,2304]{1,0:T(8,128)(2,1)S(1)} %collective-permute-done.5.refs_3_), channel_id=1, source_target_pairs={{0,64},{16,80},{32,96},{48,112},{64,0},{80,16},{96,32},{112,48},{1... | collective-permute-start | bytes 884744 | tf_op jit(solution)/shard_map/ppermute | solution.py:205
  39.7 0.0 collective-permute-done.9.refs_6_
  39.7 3.6 %home_1.1 = (bf16[4,400,256]{2,1,0:T(8,128)(2,1)S(1)}, f32[4,384,256]{2,1,0:T(8,128)S(1)}) custom-call(s32[1]{0:T(128)} %bitcast.1.feat_ref.refs_0_, bf16[4096,1792]{1,0:T(8,128)(2,1)S(1)} %get-tuple-element.26.act_ref.refs_1_, bf16[4096,512]{1,0:T(8,128)(2,1)S(1)} %get-tuple-element.27.grad_ref.refs_2_, ...), custom_call_target="tpu_custom_call" | custom-call | flops 1024 | bytes 1024 | tf_op jit(solution)/shard_map/home_1/pallas_call | solution.py:179
  43.3 0.3 collective-permute-start.11
  43.6 4.8 %collective-permute-done.6.refs_3_ = bf16[64,2304]{1,0:T(8,128)(2,1)S(1)} collective-permute-done((bf16[64,2304]{1,0:T(8,128)(2,1)S(1)}, bf16[64,2304]{1,0:T(8,128)(2,1)S(1)}, u32[]{:S(2)}, u32[]{:S(2)}) %collective-permute-start.6) | collective-permute-done | bytes 294944 | tf_op jit(solution)/shard_map/ppermute | solution.py:205
  48.3 3.0 %away_2.1.refs_2_ = bf16[8,144,256]{2,1,0:T(8,128)(2,1)S(1)} custom-call(s32[1]{0:T(128)} %bitcast.1.feat_ref.refs_0_, bf16[4096,1792]{1,0:T(8,128)(2,1)S(1)} %get-tuple-element.26.act_ref.refs_1_, bf16[4096,512]{1,0:T(8,128)(2,1)S(1)} %get-tuple-element.27.grad_ref.refs_2_, bf16[64,2304]{1,0:T(8,128)(2,1)S(1)} %collective-permute-done.6.refs_3_, ...), custom_call_target="tpu_custom_call" | custom-call | flops 1024 | bytes 1024 | tf_op jit(solution)/shard_map/away_2/pallas_call | solution.py:179
  51.4 0.1 collective-permute-start.12
  51.5 0.0 collective-permute-done.4.refs_1_
  51.5 1.1 %step_0_1.1 = (bf16[2,528,256]{2,1,0:T(8,128)(2,1)S(1)}, f32[2,512,256]{2,1,0:T(8,128)S(1)}) custom-call(f32[4,512,256]{2,1,0:T(8,128)S(1)} %get-tuple-element.28.refs_0_, bf16[4,528,256]{2,1,0:T(8,128)(2,1)S(1)} %collective-permute-done.4.refs_1_, bf16[8,144,256]{2,1,0:T(8,128)(2,1)S(1)} %away_2.1.refs_2_), custom_call_target="tpu_custom_call" | custom-call | flops 1024 | bytes 1024 | tf_op jit(solution)/shard_map/step_0_1/pallas_call | solution.py:179
  52.5 0.4 collective-permute-start.10
  52.9 0.5 collective-permute-done.12.refs_4_
  53.4 3.0 %home_2.1 = (bf16[4,144,256]{2,1,0:T(8,128)(2,1)S(1)}, f32[4,128,256]{2,1,0:T(8,128)S(1)}) custom-call(s32[1]{0:T(128)} %bitcast.1.feat_ref.refs_0_, bf16[4096,1792]{1,0:T(8,128)(2,1)S(1)} %get-tuple-element.26.act_ref.refs_1_, bf16[4096,512]{1,0:T(8,128)(2,1)S(1)} %get-tuple-element.27.grad_ref.refs_2_, ...), custom_call_target="tpu_custom_call" | custom-call | flops 1024 | bytes 1024 | tf_op jit(solution)/shard_map/home_2/pallas_call | solution.py:179
  56.4 2.4 %collective-permute-done.11.refs_1_ = bf16[4,400,256]{2,1,0:T(8,128)(2,1)S(1)} collective-permute-done((bf16[4,400,256]{2,1,0:T(8,128)(2,1)S(1)}, bf16[4,400,256]{2,1,0:T(8,128)(2,1)S(1)}, u32[]{:S(2)}, u32[]{:S(2)}) %collective-permute-start.11) | collective-permute-done | bytes 819232 | tf_op jit(solution)/shard_map/ppermute | solution.py:61
  58.8 0.8 step_1_1.1
  59.6 2.8 %collective-permute-start.14 = (bf16[2,400,256]{2,1,0:T(8,128)(2,1)S(1)}, bf16[2,400,256]{2,1,0:T(8,128)(2,1)S(1)}, u32[]{:S(2)}, u32[]{:S(2)}) collective-permute-start(bf16[2,400,256]{2,1,0:T(8,128)(2,1)S(1)} %get-tuple-element.36.refs_2_), channel_id=1, source_target_pairs={{0,4},{1,13},{2,6},{3,15},{4,0},{5,9},{6,2},{7,11},{8,12},{9,5},{1... | collective-permute-start | bytes 1228808 | tf_op jit(solution)/shard_map/ppermute | solution.py:61
  62.4 0.1 collective-permute-start.15
  62.5 0.0 collective-permute-done.10.refs_1_
  62.5 0.5 step_0_2.1
  63.0 0.1 collective-permute-start.13
  63.1 11.2 %collective-permute-done.15.refs_1_ = bf16[4,144,256]{2,1,0:T(8,128)(2,1)S(1)} collective-permute-done((bf16[4,144,256]{2,1,0:T(8,128)(2,1)S(1)}, bf16[4,144,256]{2,1,0:T(8,128)(2,1)S(1)}, u32[]{:S(2)}, u32[]{:S(2)}) %collective-permute-start.15) | collective-permute-done | bytes 294944 | tf_op jit(solution)/shard_map/ppermute | solution.py:61
  74.3 0.3 step_2_1.1
  74.5 0.4 collective-permute-start.17
  74.9 0.4 step_1_2.1
  75.3 1.2 %collective-permute-start.16 = (bf16[1,400,256]{2,1,0:T(8,128)(2,1)S(1)}, bf16[1,400,256]{2,1,0:T(8,128)(2,1)S(1)}, u32[]{:S(2)}, u32[]{:S(2)}) collective-permute-start(bf16[1,400,256]{2,1,0:T(8,128)(2,1)S(1)} %get-tuple-element.43.refs_2_), channel_id=1, source_target_pairs={{0,12},{1,3},{2,14},{3,1},{4,8},{5,7},{6,10},{7,5},{8,4},{9,11},{1... | collective-permute-start | bytes 614408 | tf_op jit(solution)/shard_map/ppermute | solution.py:61
  76.6 2.1 %collective-permute-done.17.refs_1_ = bf16[2,144,256]{2,1,0:T(8,128)(2,1)S(1)} collective-permute-done((bf16[2,144,256]{2,1,0:T(8,128)(2,1)S(1)}, bf16[2,144,256]{2,1,0:T(8,128)(2,1)S(1)}, u32[]{:S(2)}, u32[]{:S(2)}) %collective-permute-start.17) | collective-permute-done | bytes 147488 | tf_op jit(solution)/shard_map/ppermute | solution.py:61
  78.7 0.1 step_2_2.1
  78.9 1.0 %collective-permute-start.18 = (bf16[1,144,256]{2,1,0:T(8,128)(2,1)S(1)}, bf16[1,144,256]{2,1,0:T(8,128)(2,1)S(1)}, u32[]{:S(2)}, u32[]{:S(2)}) collective-permute-start(bf16[1,144,256]{2,1,0:T(8,128)(2,1)S(1)} %get-tuple-element.46), channel_id=1, source_target_pairs={{0,4},{1,5},{2,6},{3,7},{4,0},{5,1},{6,2},{7,3},{8,12},{9,13},{10,... | collective-permute-start | bytes 221192 | tf_op jit(solution)/shard_map/ppermute | solution.py:61
  79.8 2.8 %collective-permute-done.18.refs_5_ = bf16[1,144,256]{2,1,0:T(8,128)(2,1)S(1)} collective-permute-done((bf16[1,144,256]{2,1,0:T(8,128)(2,1)S(1)}, bf16[1,144,256]{2,1,0:T(8,128)(2,1)S(1)}, u32[]{:S(2)}, u32[]{:S(2)}) %collective-permute-start.18) | collective-permute-done | bytes 73760 | tf_op jit(solution)/shard_map/ppermute | solution.py:61
  82.6 1.0 %shard_map.47 = f32[16,256]{1,0:T(8,128)} custom-call(s32[1]{0:T(128)} %bitcast.tok_ref, f32[1,512,256]{2,1,0:T(8,128)S(1)} %get-tuple-element.37.refs_0_, bf16[1,528,256]{2,1,0:T(8,128)(2,1)S(1)} %collective-permute-done.13.refs_1_, f32[1,384,256]{2,1,0:T(8,128)S(1)} %get-tuple-element.42.refs_2_, bf16[1,400,256]{2,1,0:T(8,128)(2,1)S(1)} %collective-permute-done.16.refs_3_, ...), custom_call_target="tpu_custom_call" | custom-call | bytes 1024 | tf_op jit(solution)/shard_map/pallas_call | solution.py:179
  (5 shorter events, 0.0 us)
Async XLA Ops:
  1.0 14.0 %collective-permute-start = (bf16[64,2304]{1,0:T(8,128)(2,1)S(1)}, bf16[64,2304]{1,0:T(8,128)(2,1)S(1)}, u32[]{:S(2)}, u32[]{:S(2)}) collective-permute-start(bf16[64,2304]{1,0:T(8,128)(2,1)S(1)} %bitcast.3), channel_id=1, source_target_pairs={{0,16},{16,32},{32,48},{48,0},{64,80},{80,96},{96,112},{112,64},{1... | collective-permute-start | bytes 884744 | tf_op jit(solution)/shard_map/ppermute | solution.py:205
  3.5 11.5 %collective-permute-start.2 = (bf16[64,2304]{1,0:T(8,128)(2,1)S(1)}, bf16[64,2304]{1,0:T(8,128)(2,1)S(1)}, u32[]{:S(2)}, u32[]{:S(2)}) collective-permute-start(bf16[64,2304]{1,0:T(8,128)(2,1)S(1)} %bitcast.4), channel_id=1, source_target_pairs={{0,64},{16,80},{32,96},{48,112},{64,0},{80,16},{96,32},{112,48},{1... | collective-permute-start | bytes 884744 | tf_op jit(solution)/shard_map/ppermute | solution.py:205
  6.3 8.7 %collective-permute-start.1 = (bf16[64,2304]{1,0:T(8,128)(2,1)S(1)}, bf16[64,2304]{1,0:T(8,128)(2,1)S(1)}, u32[]{:S(2)}, u32[]{:S(2)}) collective-permute-start(bf16[64,2304]{1,0:T(8,128)(2,1)S(1)} %bitcast.5), channel_id=1, source_target_pairs={{0,48},{16,0},{32,16},{48,32},{64,112},{80,64},{96,80},{112,96},{1... | collective-permute-start | bytes 884744 | tf_op jit(solution)/shard_map/ppermute | solution.py:205
  18.5 5.2 %collective-permute-start.3 = (bf16[8,528,256]{2,1,0:T(8,128)(2,1)S(1)}, bf16[8,528,256]{2,1,0:T(8,128)(2,1)S(1)}, u32[]{:S(2)}, u32[]{:S(2)}) collective-permute-start(bf16[8,528,256]{2,1,0:T(8,128)(2,1)S(1)} %away_0.1.refs_8_), channel_id=1, source_target_pairs={{0,1},{1,0},{2,3},{3,2},{4,5},{5,4},{6,7},{7,6},{8,9},{9,8},{10,11... | collective-permute-start | bytes 6488072 | tf_op jit(solution)/shard_map/ppermute | solution.py:220
  19.8 10.2 %collective-permute-start.5 = (bf16[64,2304]{1,0:T(8,128)(2,1)S(1)}, bf16[64,2304]{1,0:T(8,128)(2,1)S(1)}, u32[]{:S(2)}, u32[]{:S(2)}) collective-permute-start(bf16[64,2304]{1,0:T(8,128)(2,1)S(1)} %collective-permute-done.refs_0_.refs_3_), channel_id=1, source_target_pairs={{0,16},{16,32},{32,48},{48,0},{64,80},{80,96},{96,112},{112,64},{1... | collective-permute-start | bytes 884744 | tf_op jit(solution)/shard_map/ppermute | solution.py:205
  20.9 9.7 %collective-permute-start.8 = (bf16[64,2304]{1,0:T(8,128)(2,1)S(1)}, bf16[64,2304]{1,0:T(8,128)(2,1)S(1)}, u32[]{:S(2)}, u32[]{:S(2)}) collective-permute-start(bf16[64,2304]{1,0:T(8,128)(2,1)S(1)} %collective-permute-done.refs_0_.refs_3_), channel_id=1, source_target_pairs={{0,64},{16,80},{32,96},{48,112},{64,0},{80,16},{96,32},{112,48},{1... | collective-permute-start | bytes 884744 | tf_op jit(solution)/shard_map/ppermute | solution.py:205
  22.4 8.2 %collective-permute-start.7 = (bf16[64,2304]{1,0:T(8,128)(2,1)S(1)}, bf16[64,2304]{1,0:T(8,128)(2,1)S(1)}, u32[]{:S(2)}, u32[]{:S(2)}) collective-permute-start(bf16[64,2304]{1,0:T(8,128)(2,1)S(1)} %collective-permute-done.2.refs_3_.refs_6_), channel_id=1, source_target_pairs={{0,48},{16,0},{32,16},{48,32},{64,112},{80,64},{96,80},{112,96},{1... | collective-permute-start | bytes 884744 | tf_op jit(solution)/shard_map/ppermute | solution.py:205
  34.2 5.5 %collective-permute-start.9 = (bf16[8,400,256]{2,1,0:T(8,128)(2,1)S(1)}, bf16[8,400,256]{2,1,0:T(8,128)(2,1)S(1)}, u32[]{:S(2)}, u32[]{:S(2)}) collective-permute-start(bf16[8,400,256]{2,1,0:T(8,128)(2,1)S(1)} %away_1.1.refs_7_), channel_id=1, source_target_pairs={{0,1},{1,0},{2,3},{3,2},{4,5},{5,4},{6,7},{7,6},{8,9},{9,8},{10,11... | collective-permute-start | bytes 4915208 | tf_op jit(solution)/shard_map/ppermute | solution.py:220
  35.4 16.0 %collective-permute-start.4 = (bf16[4,528,256]{2,1,0:T(8,128)(2,1)S(1)}, bf16[4,528,256]{2,1,0:T(8,128)(2,1)S(1)}, u32[]{:S(2)}, u32[]{:S(2)}) collective-permute-start(bf16[4,528,256]{2,1,0:T(8,128)(2,1)S(1)} %get-tuple-element.29.refs_6_), channel_id=1, source_target_pairs={{0,4},{1,13},{2,6},{3,15},{4,0},{5,9},{6,2},{7,11},{8,12},{9,5},{1... | collective-permute-start | bytes 3244040 | tf_op jit(solution)/shard_map/ppermute | solution.py:61
  38.2 10.2 %collective-permute-start.6 = (bf16[64,2304]{1,0:T(8,128)(2,1)S(1)}, bf16[64,2304]{1,0:T(8,128)(2,1)S(1)}, u32[]{:S(2)}, u32[]{:S(2)}) collective-permute-start(bf16[64,2304]{1,0:T(8,128)(2,1)S(1)} %collective-permute-done.5.refs_3_), channel_id=1, source_target_pairs={{0,64},{16,80},{32,96},{48,112},{64,0},{80,16},{96,32},{112,48},{1... | collective-permute-start | bytes 884744 | tf_op jit(solution)/shard_map/ppermute | solution.py:205
  43.3 15.5 %collective-permute-start.11 = (bf16[4,400,256]{2,1,0:T(8,128)(2,1)S(1)}, bf16[4,400,256]{2,1,0:T(8,128)(2,1)S(1)}, u32[]{:S(2)}, u32[]{:S(2)}) collective-permute-start(bf16[4,400,256]{2,1,0:T(8,128)(2,1)S(1)} %get-tuple-element.31.refs_4_), channel_id=1, source_target_pairs={{0,2},{1,5},{2,0},{3,7},{4,6},{5,1},{6,4},{7,3},{8,10},{9,13},{10,... | collective-permute-start | bytes 2457608 | tf_op jit(solution)/shard_map/ppermute | solution.py:61
  51.4 2.1 %collective-permute-start.12 = (bf16[8,144,256]{2,1,0:T(8,128)(2,1)S(1)}, bf16[8,144,256]{2,1,0:T(8,128)(2,1)S(1)}, u32[]{:S(2)}, u32[]{:S(2)}) collective-permute-start(bf16[8,144,256]{2,1,0:T(8,128)(2,1)S(1)} %away_2.1.refs_2_), channel_id=1, source_target_pairs={{0,1},{1,0},{2,3},{3,2},{4,5},{5,4},{6,7},{7,6},{8,9},{9,8},{10,11... | collective-permute-start | bytes 1769480 | tf_op jit(solution)/shard_map/ppermute | solution.py:220
  52.5 9.9 %collective-permute-start.10 = (bf16[2,528,256]{2,1,0:T(8,128)(2,1)S(1)}, bf16[2,528,256]{2,1,0:T(8,128)(2,1)S(1)}, u32[]{:S(2)}, u32[]{:S(2)}) collective-permute-start(bf16[2,528,256]{2,1,0:T(8,128)(2,1)S(1)} %get-tuple-element.33.refs_5_), channel_id=1, source_target_pairs={{0,12},{1,3},{2,14},{3,1},{4,8},{5,7},{6,10},{7,5},{8,4},{9,11},{1... | collective-permute-start | bytes 1622024 | tf_op jit(solution)/shard_map/ppermute | solution.py:61
  59.6 15.4 %collective-permute-start.14 = (bf16[2,400,256]{2,1,0:T(8,128)(2,1)S(1)}, bf16[2,400,256]{2,1,0:T(8,128)(2,1)S(1)}, u32[]{:S(2)}, u32[]{:S(2)}) collective-permute-start(bf16[2,400,256]{2,1,0:T(8,128)(2,1)S(1)} %get-tuple-element.36.refs_2_), channel_id=1, source_target_pairs={{0,4},{1,13},{2,6},{3,15},{4,0},{5,9},{6,2},{7,11},{8,12},{9,5},{1... | collective-permute-start | bytes 1228808 | tf_op jit(solution)/shard_map/ppermute | solution.py:61
  62.4 11.9 %collective-permute-start.15 = (bf16[4,144,256]{2,1,0:T(8,128)(2,1)S(1)}, bf16[4,144,256]{2,1,0:T(8,128)(2,1)S(1)}, u32[]{:S(2)}, u32[]{:S(2)}) collective-permute-start(bf16[4,144,256]{2,1,0:T(8,128)(2,1)S(1)} %get-tuple-element.35.refs_2_), channel_id=1, source_target_pairs={{0,2},{1,13},{2,0},{3,15},{4,6},{5,9},{6,4},{7,11},{8,10},{9,5},{1... | collective-permute-start | bytes 884744 | tf_op jit(solution)/shard_map/ppermute | solution.py:61
  63.0 16.8 %collective-permute-start.13 = (bf16[1,528,256]{2,1,0:T(8,128)(2,1)S(1)}, bf16[1,528,256]{2,1,0:T(8,128)(2,1)S(1)}, u32[]{:S(2)}, u32[]{:S(2)}) collective-permute-start(bf16[1,528,256]{2,1,0:T(8,128)(2,1)S(1)} %get-tuple-element.38.refs_2_), channel_id=1, source_target_pairs={{0,2},{1,5},{2,0},{3,7},{4,6},{5,1},{6,4},{7,3},{8,10},{9,13},{10,... | collective-permute-start | bytes 811016 | tf_op jit(solution)/shard_map/ppermute | solution.py:61
  74.5 4.2 %collective-permute-start.17 = (bf16[2,144,256]{2,1,0:T(8,128)(2,1)S(1)}, bf16[2,144,256]{2,1,0:T(8,128)(2,1)S(1)}, u32[]{:S(2)}, u32[]{:S(2)}) collective-permute-start(bf16[2,144,256]{2,1,0:T(8,128)(2,1)S(1)} %get-tuple-element.41.refs_2_), channel_id=1, source_target_pairs={{0,12},{1,3},{2,14},{3,1},{4,8},{5,7},{6,10},{7,5},{8,4},{9,11},{1... | collective-permute-start | bytes 442376 | tf_op jit(solution)/shard_map/ppermute | solution.py:61
  75.3 7.3 %collective-permute-start.16 = (bf16[1,400,256]{2,1,0:T(8,128)(2,1)S(1)}, bf16[1,400,256]{2,1,0:T(8,128)(2,1)S(1)}, u32[]{:S(2)}, u32[]{:S(2)}) collective-permute-start(bf16[1,400,256]{2,1,0:T(8,128)(2,1)S(1)} %get-tuple-element.43.refs_2_), channel_id=1, source_target_pairs={{0,12},{1,3},{2,14},{3,1},{4,8},{5,7},{6,10},{7,5},{8,4},{9,11},{1... | collective-permute-start | bytes 614408 | tf_op jit(solution)/shard_map/ppermute | solution.py:61
  78.9 3.7 %collective-permute-start.18 = (bf16[1,144,256]{2,1,0:T(8,128)(2,1)S(1)}, bf16[1,144,256]{2,1,0:T(8,128)(2,1)S(1)}, u32[]{:S(2)}, u32[]{:S(2)}) collective-permute-start(bf16[1,144,256]{2,1,0:T(8,128)(2,1)S(1)} %get-tuple-element.46), channel_id=1, source_target_pairs={{0,4},{1,5},{2,6},{3,7},{4,0},{5,1},{6,2},{7,3},{8,12},{9,13},{10,... | collective-permute-start | bytes 221192 | tf_op jit(solution)/shard_map/ppermute | solution.py:61

commit v4 on v3

--- a/solution.py
+++ b/solution.py
@@ -18,19 +18,19 @@
 
 G1, G0, X = 2, 1, 0
 ORDERS = (
-    ((G0, G1, X), (G1, X, G0)),
-    ((X, G0, G1), (G0, G1, X)),
+    ((G0, X, G1), (G1, G0, X)),
     ((X, G1, G0), (G1, X, G0)),
+    ((G0, G1, X), (X, G0, G1)),
 )
 CHUNKS = (
     ("own_up", "own_down", "own", "far"),
     ("own_two", "far_down", "far_up"),
     ("far_two",),
 )
-COST = 1024
+COST_OF = {}
 PLAN = (
-    ("away", 0), ("home", 0), ("pass", 2), ("away", 1), ("home", 1), ("away", 2), ("step", 0, 1), ("home", 2),
-    ("step", 1, 1), ("step", 0, 2), ("step", 2, 1), ("step", 1, 2), ("step", 2, 2),
+    ("away", 0), ("home", 0), ("pass", 2), ("away", 1), ("home", 1), ("away", 2), ("step", 0, 1),
+    ("home", 2), ("step", 1, 1), ("step", 0, 2), ("step", 2, 1), ("step", 1, 2), ("step", 2, 2),
 )
 OWNERS = {
     "own": (0, 0), "far": (4, 0), "own_up": (0, 3), "own_down": (0, 1),
@@ -215,7 +215,7 @@
         side, width = sum(b.shape[0] for b in blocks), own.shape[1]
         scratch = [pltpu.VMEM((side, width), jnp.bfloat16)]
         send = call(functools.partial(away_kernel, len(blocks), ORDERS[c]), sends(8, 2 * side)[0],
-                    (feat, acts, grads, *blocks), 1024, 0, 1, scratch, name=f"away_{c}", **turn)
+                    (feat, acts, grads, *blocks), COST_OF.get(f"away_{c}", 1024), 0, 1, scratch, name=f"away_{c}", **turn)
         turn["after"] = send
         got[c] = lax.ppermute(send, "feat", [(s, s ^ 1) for s in range(16)])
 
@@ -224,14 +224,14 @@
         side, width = sum(b.shape[0] for b in blocks), own.shape[1]
         scratch = [pltpu.VMEM((side, width), jnp.bfloat16)]
         send, keep[c] = call(functools.partial(home_kernel, len(blocks), ORDERS[c]), sends(4, 2 * side),
-                             (feat, acts, grads, *blocks, got[c]), 1024, 0, 1, scratch, name=f"home_{c}", **turn)
+                             (feat, acts, grads, *blocks, got[c]), COST_OF.get(f"home_{c}", 1024), 0, 1, scratch, name=f"home_{c}", **turn)
         turn["after"] = send
         got[c] = halve(send, ORDERS[c], 0)
 
     def step(c, stage):
         count, rows = keep[c].shape[:2]
         send, keep[c] = call(step_kernel, sends(count // 2, rows), (keep[c], got[c]),
-                             COST, 0, 0, name=f"step_{c}_{stage}", **turn)
+                             COST_OF.get(f"step_{c}_{stage}", 1024), 0, 0, name=f"step_{c}_{stage}", **turn)
         turn["after"] = send
         got[c] = halve(send, ORDERS[c], stage)
 

time: 84.2 us -> 81 us (0.962)
  waiting for transfers between devices: 27.5 us -> 22.7 us
  starting transfers between devices: 24.3 us -> 26.4 us
    ppermute x9, waiting for transfers between devices: 18.5 us -> 14.8 us  [halve(): lax.ppermute(value, 'feat', [(s, partner(s, orders[s & 1][stage])) for s...]
    ppermute x9, starting transfers between devices: 8.95 us -> 11.1 us  [halve(): lax.ppermute(value, 'feat', [(s, partner(s, orders[s & 1][stage])) for s...]
    ppermute x7, waiting for transfers between devices: 8.28 us -> 6.87 us  [local(): move = lambda value, way: lax.ppermute(value, 'tok', pairs[way])]
  transfers between devices with their start and end apart: 19 -> 19, of which waited for: 9 -> 9; matrix products, arithmetic and copies ran while one was open for 0% -> 0% of each run, Pallas kernels for 27% -> 28%
where the time goes in v4:
time: 81 us; the launch traced here: 80.8 us
  Pallas kernels  30.7 us (38%)
  starting transfers between devices  26.4 us (33%)
  waiting for transfers between devices  22.7 us (28%)
  other arithmetic  1 us (1%)
    pallas_call x13, Pallas kernels, call(): pl.pallas_call(kernel, in_specs=specs, out_specs=jax.tree.map(lambda _: I...  24.2 us
    ppermute x9, waiting for transfers between devices, halve(): lax.ppermute(value, 'feat', [(s, partner(s, orders[s & 1][stage])) for s...  14.8 us
    ppermute x7, starting transfers between devices, local(): move = lambda value, way: lax.ppermute(value, 'tok', pairs[way])  12.6 us
    ppermute x9, starting transfers between devices, halve(): lax.ppermute(value, 'feat', [(s, partner(s, orders[s & 1][stage])) for s...  11.1 us
    ppermute x7, waiting for transfers between devices, local(): move = lambda value, way: lax.ppermute(value, 'tok', pairs[way])  6.87 us
    pallas_call x1, Pallas kernels, load(): pl.pallas_call(functools.partial(load_kernel, parts), in_specs=[pl.BlockS...  6.48 us
    ppermute x3, starting transfers between devices, away(): got[c] = lax.ppermute(send, 'feat', [(s, s ^ 1) for s in range(16)])  2.67 us
  transfers between devices with their start and end apart: 19, of which 9 were waited for; matrix products, arithmetic and copies ran while one was open for 0% of the time, Pallas kernels for 28%

profile of v4, /device:TPU:1, one launch (start us, length us, event | category | flops | bytes accessed | tf_op | source)
XLA Modules:
  0.0 80.8 jit_solution(230747490986854314)
XLA Ops:
  0.0 1.0 %pad_maximum_fusion = bf16[2,32,2304]{2,1,0:T(8,128)(2,1)S(1)} fusion(bf16[2,32,512]{2,1,0:T(8,128)(2,1)} %param.7, bf16[2,32,1792]{2,1,0:T(8,128)(2,1)} %param.6), kind=kLoop, calls=%fused_computation | loop fusion | flops 589824 | bytes 589824 | tf_op jit(solution)/shard_map/concatenate | solution.py:207
  1.0 2.5 %collective-permute-start = (bf16[64,2304]{1,0:T(8,128)(2,1)S(1)}, bf16[64,2304]{1,0:T(8,128)(2,1)S(1)}, u32[]{:S(2)}, u32[]{:S(2)}) collective-permute-start(bf16[64,2304]{1,0:T(8,128)(2,1)S(1)} %bitcast.3), channel_id=1, source_target_pairs={{0,16},{16,32},{32,48},{48,0},{64,80},{80,96},{96,112},{112,64},{1... | collective-permute-start | bytes 884744 | tf_op jit(solution)/shard_map/ppermute | solution.py:205
  3.5 2.7 %collective-permute-start.2 = (bf16[64,2304]{1,0:T(8,128)(2,1)S(1)}, bf16[64,2304]{1,0:T(8,128)(2,1)S(1)}, u32[]{:S(2)}, u32[]{:S(2)}) collective-permute-start(bf16[64,2304]{1,0:T(8,128)(2,1)S(1)} %bitcast.4), channel_id=1, source_target_pairs={{0,64},{16,80},{32,96},{48,112},{64,0},{80,16},{96,32},{112,48},{1... | collective-permute-start | bytes 884744 | tf_op jit(solution)/shard_map/ppermute | solution.py:205
  6.3 2.2 %collective-permute-start.1 = (bf16[64,2304]{1,0:T(8,128)(2,1)S(1)}, bf16[64,2304]{1,0:T(8,128)(2,1)S(1)}, u32[]{:S(2)}, u32[]{:S(2)}) collective-permute-start(bf16[64,2304]{1,0:T(8,128)(2,1)S(1)} %bitcast.5), channel_id=1, source_target_pairs={{0,48},{16,0},{32,16},{48,32},{64,112},{80,64},{96,80},{112,96},{1... | collective-permute-start | bytes 884744 | tf_op jit(solution)/shard_map/ppermute | solution.py:205
  8.5 6.5 %shard_map.46 = (bf16[4096,1792]{1,0:T(8,128)(2,1)S(1)}, bf16[4096,512]{1,0:T(8,128)(2,1)S(1)}) custom-call(bf16[4096,1792]{1,0:T(8,128)(2,1)} %act_ref.1, bf16[4096,512]{1,0:T(8,128)(2,1)} %grad_ref.1), custom_call_target="tpu_custom_call" | custom-call | bytes 18874368 | tf_op jit(solution)/shard_map/pallas_call | solution.py:116
  15.0 0.0 collective-permute-done.2.refs_3_.refs_6_
  15.0 3.5 %away_0.1.refs_8_ = bf16[8,528,256]{2,1,0:T(8,128)(2,1)S(1)} custom-call(s32[1]{0:T(128)} %bitcast.1.feat_ref.refs_0_, bf16[4096,1792]{1,0:T(8,128)(2,1)S(1)} %get-tuple-element.26.act_ref.refs_1_, bf16[4096,512]{1,0:T(8,128)(2,1)S(1)} %get-tuple-element.27.grad_ref.refs_2_, bf16[64,2304]{1,0:T(8,128)(2,1)S(1)} %collective-permute-done.refs_0_.refs_3_, ...), custom_call_target="tpu_custom_call" | custom-call | flops 1024 | bytes 1024 | tf_op jit(solution)/shard_map/away_0/pallas_call | solution.py:179
  18.5 1.3 %collective-permute-start.3 = (bf16[8,528,256]{2,1,0:T(8,128)(2,1)S(1)}, bf16[8,528,256]{2,1,0:T(8,128)(2,1)S(1)}, u32[]{:S(2)}, u32[]{:S(2)}) collective-permute-start(bf16[8,528,256]{2,1,0:T(8,128)(2,1)S(1)} %away_0.1.refs_8_), channel_id=1, source_target_pairs={{0,1},{1,0},{2,3},{3,2},{4,5},{5,4},{6,7},{7,6},{8,9},{9,8},{10,11... | collective-permute-start | bytes 6488072 | tf_op jit(solution)/shard_map/ppermute | solution.py:220
  19.8 1.1 %collective-permute-start.5 = (bf16[64,2304]{1,0:T(8,128)(2,1)S(1)}, bf16[64,2304]{1,0:T(8,128)(2,1)S(1)}, u32[]{:S(2)}, u32[]{:S(2)}) collective-permute-start(bf16[64,2304]{1,0:T(8,128)(2,1)S(1)} %collective-permute-done.refs_0_.refs_3_), channel_id=1, source_target_pairs={{0,16},{16,32},{32,48},{48,0},{64,80},{80,96},{96,112},{112,64},{1... | collective-permute-start | bytes 884744 | tf_op jit(solution)/shard_map/ppermute | solution.py:205
  20.9 1.5 %collective-permute-start.8 = (bf16[64,2304]{1,0:T(8,128)(2,1)S(1)}, bf16[64,2304]{1,0:T(8,128)(2,1)S(1)}, u32[]{:S(2)}, u32[]{:S(2)}) collective-permute-start(bf16[64,2304]{1,0:T(8,128)(2,1)S(1)} %collective-permute-done.refs_0_.refs_3_), channel_id=1, source_target_pairs={{0,64},{16,80},{32,96},{48,112},{64,0},{80,16},{96,32},{112,48},{1... | collective-permute-start | bytes 884744 | tf_op jit(solution)/shard_map/ppermute | solution.py:205
  22.4 1.0 %collective-permute-start.7 = (bf16[64,2304]{1,0:T(8,128)(2,1)S(1)}, bf16[64,2304]{1,0:T(8,128)(2,1)S(1)}, u32[]{:S(2)}, u32[]{:S(2)}) collective-permute-start(bf16[64,2304]{1,0:T(8,128)(2,1)S(1)} %collective-permute-done.2.refs_3_.refs_6_), channel_id=1, source_target_pairs={{0,48},{16,0},{32,16},{48,32},{64,112},{80,64},{96,80},{112,96},{1... | collective-permute-start | bytes 884744 | tf_op jit(solution)/shard_map/ppermute | solution.py:205
  23.4 0.2 collective-permute-done.3.refs_7_
  23.7 3.5 %home_0.1 = (bf16[4,528,256]{2,1,0:T(8,128)(2,1)S(1)}, f32[4,512,256]{2,1,0:T(8,128)S(1)}) custom-call(s32[1]{0:T(128)} %bitcast.1.feat_ref.refs_0_, bf16[4096,1792]{1,0:T(8,128)(2,1)S(1)} %get-tuple-element.26.act_ref.refs_1_, bf16[4096,512]{1,0:T(8,128)(2,1)S(1)} %get-tuple-element.27.grad_ref.refs_2_, ...), custom_call_target="tpu_custom_call" | custom-call | flops 1024 | bytes 1024 | tf_op jit(solution)/shard_map/home_0/pallas_call | solution.py:179
  27.2 2.8 %collective-permute-done.5.refs_3_ = bf16[64,2304]{1,0:T(8,128)(2,1)S(1)} collective-permute-done((bf16[64,2304]{1,0:T(8,128)(2,1)S(1)}, bf16[64,2304]{1,0:T(8,128)(2,1)S(1)}, u32[]{:S(2)}, u32[]{:S(2)}) %collective-permute-start.5) | collective-permute-done | bytes 294944 | tf_op jit(solution)/shard_map/ppermute | solution.py:205
  30.0 0.7 collective-permute-done.8.refs_5_
  30.7 3.5 %away_1.1.refs_7_ = bf16[8,400,256]{2,1,0:T(8,128)(2,1)S(1)} custom-call(s32[1]{0:T(128)} %bitcast.1.feat_ref.refs_0_, bf16[4096,1792]{1,0:T(8,128)(2,1)S(1)} %get-tuple-element.26.act_ref.refs_1_, bf16[4096,512]{1,0:T(8,128)(2,1)S(1)} %get-tuple-element.27.grad_ref.refs_2_, bf16[64,2304]{1,0:T(8,128)(2,1)S(1)} %collective-permute-done.5.refs_3_, ...), custom_call_target="tpu_custom_call" | custom-call | flops 1024 | bytes 1024 | tf_op jit(solution)/shard_map/away_1/pallas_call | solution.py:179
  34.2 1.3 %collective-permute-start.9 = (bf16[8,400,256]{2,1,0:T(8,128)(2,1)S(1)}, bf16[8,400,256]{2,1,0:T(8,128)(2,1)S(1)}, u32[]{:S(2)}, u32[]{:S(2)}) collective-permute-start(bf16[8,400,256]{2,1,0:T(8,128)(2,1)S(1)} %away_1.1.refs_7_), channel_id=1, source_target_pairs={{0,1},{1,0},{2,3},{3,2},{4,5},{5,4},{6,7},{7,6},{8,9},{9,8},{10,11... | collective-permute-start | bytes 4915208 | tf_op jit(solution)/shard_map/ppermute | solution.py:220
  35.4 2.7 %collective-permute-start.4 = (bf16[4,528,256]{2,1,0:T(8,128)(2,1)S(1)}, bf16[4,528,256]{2,1,0:T(8,128)(2,1)S(1)}, u32[]{:S(2)}, u32[]{:S(2)}) collective-permute-start(bf16[4,528,256]{2,1,0:T(8,128)(2,1)S(1)} %get-tuple-element.29.refs_6_), channel_id=1, source_target_pairs={{0,4},{1,13},{2,6},{3,15},{4,0},{5,9},{6,2},{7,11},{8,12},{9,5},{1... | collective-permute-start | bytes 3244040 | tf_op jit(solution)/shard_map/ppermute | solution.py:61
  38.2 1.5 %collective-permute-start.6 = (bf16[64,2304]{1,0:T(8,128)(2,1)S(1)}, bf16[64,2304]{1,0:T(8,128)(2,1)S(1)}, u32[]{:S(2)}, u32[]{:S(2)}) collective-permute-start(bf16[64,2304]{1,0:T(8,128)(2,1)S(1)} %collective-permute-done.5.refs_3_), channel_id=1, source_target_pairs={{0,64},{16,80},{32,96},{48,112},{64,0},{80,16},{96,32},{112,48},{1... | collective-permute-start | bytes 884744 | tf_op jit(solution)/shard_map/ppermute | solution.py:205
  39.7 0.0 collective-permute-done.9.refs_6_
  39.7 3.6 %home_1.1 = (bf16[4,400,256]{2,1,0:T(8,128)(2,1)S(1)}, f32[4,384,256]{2,1,0:T(8,128)S(1)}) custom-call(s32[1]{0:T(128)} %bitcast.1.feat_ref.refs_0_, bf16[4096,1792]{1,0:T(8,128)(2,1)S(1)} %get-tuple-element.26.act_ref.refs_1_, bf16[4096,512]{1,0:T(8,128)(2,1)S(1)} %get-tuple-element.27.grad_ref.refs_2_, ...), custom_call_target="tpu_custom_call" | custom-call | flops 1024 | bytes 1024 | tf_op jit(solution)/shard_map/home_1/pallas_call | solution.py:179
  43.3 1.7 %collective-permute-start.11 = (bf16[4,400,256]{2,1,0:T(8,128)(2,1)S(1)}, bf16[4,400,256]{2,1,0:T(8,128)(2,1)S(1)}, u32[]{:S(2)}, u32[]{:S(2)}) collective-permute-start(bf16[4,400,256]{2,1,0:T(8,128)(2,1)S(1)} %get-tuple-element.31.refs_4_), channel_id=1, source_target_pairs={{0,2},{1,13},{2,0},{3,15},{4,6},{5,9},{6,4},{7,11},{8,10},{9,5},{1... | collective-permute-start | bytes 2457608 | tf_op jit(solution)/shard_map/ppermute | solution.py:61
  45.0 3.4 %collective-permute-done.6.refs_3_ = bf16[64,2304]{1,0:T(8,128)(2,1)S(1)} collective-permute-done((bf16[64,2304]{1,0:T(8,128)(2,1)S(1)}, bf16[64,2304]{1,0:T(8,128)(2,1)S(1)}, u32[]{:S(2)}, u32[]{:S(2)}) %collective-permute-start.6) | collective-permute-done | bytes 294944 | tf_op jit(solution)/shard_map/ppermute | solution.py:205
  48.3 3.0 %away_2.1.refs_2_ = bf16[8,144,256]{2,1,0:T(8,128)(2,1)S(1)} custom-call(s32[1]{0:T(128)} %bitcast.1.feat_ref.refs_0_, bf16[4096,1792]{1,0:T(8,128)(2,1)S(1)} %get-tuple-element.26.act_ref.refs_1_, bf16[4096,512]{1,0:T(8,128)(2,1)S(1)} %get-tuple-element.27.grad_ref.refs_2_, bf16[64,2304]{1,0:T(8,128)(2,1)S(1)} %collective-permute-done.6.refs_3_, ...), custom_call_target="tpu_custom_call" | custom-call | flops 1024 | bytes 1024 | tf_op jit(solution)/shard_map/away_2/pallas_call | solution.py:179
  51.4 0.1 collective-permute-start.12
  51.5 0.0 collective-permute-done.4.refs_1_
  51.5 1.1 %step_0_1.1 = (bf16[2,528,256]{2,1,0:T(8,128)(2,1)S(1)}, f32[2,512,256]{2,1,0:T(8,128)S(1)}) custom-call(f32[4,512,256]{2,1,0:T(8,128)S(1)} %get-tuple-element.28.refs_0_, bf16[4,528,256]{2,1,0:T(8,128)(2,1)S(1)} %collective-permute-done.4.refs_1_, bf16[8,144,256]{2,1,0:T(8,128)(2,1)S(1)} %away_2.1.refs_2_), custom_call_target="tpu_custom_call" | custom-call | flops 1024 | bytes 1024 | tf_op jit(solution)/shard_map/step_0_1/pallas_call | solution.py:179
  52.5 0.1 collective-permute-start.10
  52.7 0.8 collective-permute-done.12.refs_4_
  53.5 3.0 %home_2.1 = (bf16[4,144,256]{2,1,0:T(8,128)(2,1)S(1)}, f32[4,128,256]{2,1,0:T(8,128)S(1)}) custom-call(s32[1]{0:T(128)} %bitcast.1.feat_ref.refs_0_, bf16[4096,1792]{1,0:T(8,128)(2,1)S(1)} %get-tuple-element.26.act_ref.refs_1_, bf16[4096,512]{1,0:T(8,128)(2,1)S(1)} %get-tuple-element.27.grad_ref.refs_2_, ...), custom_call_target="tpu_custom_call" | custom-call | flops 1024 | bytes 1024 | tf_op jit(solution)/shard_map/home_2/pallas_call | solution.py:179
  56.4 3.1 %collective-permute-done.11.refs_1_ = bf16[4,400,256]{2,1,0:T(8,128)(2,1)S(1)} collective-permute-done((bf16[4,400,256]{2,1,0:T(8,128)(2,1)S(1)}, bf16[4,400,256]{2,1,0:T(8,128)(2,1)S(1)}, u32[]{:S(2)}, u32[]{:S(2)}) %collective-permute-start.11) | collective-permute-done | bytes 819232 | tf_op jit(solution)/shard_map/ppermute | solution.py:61
  59.5 0.8 step_1_1.1
  60.3 0.4 collective-permute-start.14
  60.7 1.2 %collective-permute-start.15 = (bf16[4,144,256]{2,1,0:T(8,128)(2,1)S(1)}, bf16[4,144,256]{2,1,0:T(8,128)(2,1)S(1)}, u32[]{:S(2)}, u32[]{:S(2)}) collective-permute-start(bf16[4,144,256]{2,1,0:T(8,128)(2,1)S(1)} %get-tuple-element.35.refs_2_), channel_id=1, source_target_pairs={{0,4},{1,3},{2,6},{3,1},{4,0},{5,7},{6,2},{7,5},{8,12},{9,11},{10,... | collective-permute-start | bytes 884744 | tf_op jit(solution)/shard_map/ppermute | solution.py:61
  61.8 0.0 collective-permute-done.10.refs_1_
  61.8 0.5 step_0_2.1
  62.4 0.4 collective-permute-start.13
  62.8 7.6 %collective-permute-done.15.refs_1_ = bf16[4,144,256]{2,1,0:T(8,128)(2,1)S(1)} collective-permute-done((bf16[4,144,256]{2,1,0:T(8,128)(2,1)S(1)}, bf16[4,144,256]{2,1,0:T(8,128)(2,1)S(1)}, u32[]{:S(2)}, u32[]{:S(2)}) %collective-permute-start.15) | collective-permute-done | bytes 294944 | tf_op jit(solution)/shard_map/ppermute | solution.py:61
  70.4 0.3 step_2_1.1
  70.6 0.7 collective-permute-start.17
  71.3 0.0 collective-permute-done.14.refs_1_
  71.3 0.4 step_1_2.1
  71.7 1.0 %collective-permute-start.16 = (bf16[1,400,256]{2,1,0:T(8,128)(2,1)S(1)}, bf16[1,400,256]{2,1,0:T(8,128)(2,1)S(1)}, u32[]{:S(2)}, u32[]{:S(2)}) collective-permute-start(bf16[1,400,256]{2,1,0:T(8,128)(2,1)S(1)} %get-tuple-element.43.refs_2_), channel_id=1, source_target_pairs={{0,4},{1,5},{2,6},{3,7},{4,0},{5,1},{6,2},{7,3},{8,12},{9,13},{10,... | collective-permute-start | bytes 614408 | tf_op jit(solution)/shard_map/ppermute | solution.py:61
  72.7 2.3 %collective-permute-done.17.refs_1_ = bf16[2,144,256]{2,1,0:T(8,128)(2,1)S(1)} collective-permute-done((bf16[2,144,256]{2,1,0:T(8,128)(2,1)S(1)}, bf16[2,144,256]{2,1,0:T(8,128)(2,1)S(1)}, u32[]{:S(2)}, u32[]{:S(2)}) %collective-permute-start.17) | collective-permute-done | bytes 147488 | tf_op jit(solution)/shard_map/ppermute | solution.py:61
  75.0 0.1 step_2_2.1
  75.1 3.0 %collective-permute-start.18 = (bf16[1,144,256]{2,1,0:T(8,128)(2,1)S(1)}, bf16[1,144,256]{2,1,0:T(8,128)(2,1)S(1)}, u32[]{:S(2)}, u32[]{:S(2)}) collective-permute-start(bf16[1,144,256]{2,1,0:T(8,128)(2,1)S(1)} %get-tuple-element.46), channel_id=1, source_target_pairs={{0,2},{1,13},{2,0},{3,15},{4,6},{5,9},{6,4},{7,11},{8,10},{9,5},{1... | collective-permute-start | bytes 221192 | tf_op jit(solution)/shard_map/ppermute | solution.py:61
  78.1 1.7 %collective-permute-done.18.refs_5_ = bf16[1,144,256]{2,1,0:T(8,128)(2,1)S(1)} collective-permute-done((bf16[1,144,256]{2,1,0:T(8,128)(2,1)S(1)}, bf16[1,144,256]{2,1,0:T(8,128)(2,1)S(1)}, u32[]{:S(2)}, u32[]{:S(2)}) %collective-permute-start.18) | collective-permute-done | bytes 73760 | tf_op jit(solution)/shard_map/ppermute | solution.py:61
  79.9 1.0 %shard_map.47 = f32[16,256]{1,0:T(8,128)} custom-call(s32[1]{0:T(128)} %bitcast.tok_ref, f32[1,512,256]{2,1,0:T(8,128)S(1)} %get-tuple-element.37.refs_0_, bf16[1,528,256]{2,1,0:T(8,128)(2,1)S(1)} %collective-permute-done.13.refs_1_, f32[1,384,256]{2,1,0:T(8,128)S(1)} %get-tuple-element.42.refs_2_, bf16[1,400,256]{2,1,0:T(8,128)(2,1)S(1)} %collective-permute-done.16.refs_3_, ...), custom_call_target="tpu_custom_call" | custom-call | bytes 1024 | tf_op jit(solution)/shard_map/pallas_call | solution.py:179
  (5 shorter events, 0.0 us)
Async XLA Ops:
  1.0 14.0 %collective-permute-start = (bf16[64,2304]{1,0:T(8,128)(2,1)S(1)}, bf16[64,2304]{1,0:T(8,128)(2,1)S(1)}, u32[]{:S(2)}, u32[]{:S(2)}) collective-permute-start(bf16[64,2304]{1,0:T(8,128)(2,1)S(1)} %bitcast.3), channel_id=1, source_target_pairs={{0,16},{16,32},{32,48},{48,0},{64,80},{80,96},{96,112},{112,64},{1... | collective-permute-start | bytes 884744 | tf_op jit(solution)/shard_map/ppermute | solution.py:205
  3.5 11.5 %collective-permute-start.2 = (bf16[64,2304]{1,0:T(8,128)(2,1)S(1)}, bf16[64,2304]{1,0:T(8,128)(2,1)S(1)}, u32[]{:S(2)}, u32[]{:S(2)}) collective-permute-start(bf16[64,2304]{1,0:T(8,128)(2,1)S(1)} %bitcast.4), channel_id=1, source_target_pairs={{0,64},{16,80},{32,96},{48,112},{64,0},{80,16},{96,32},{112,48},{1... | collective-permute-start | bytes 884744 | tf_op jit(solution)/shard_map/ppermute | solution.py:205
  6.3 8.7 %collective-permute-start.1 = (bf16[64,2304]{1,0:T(8,128)(2,1)S(1)}, bf16[64,2304]{1,0:T(8,128)(2,1)S(1)}, u32[]{:S(2)}, u32[]{:S(2)}) collective-permute-start(bf16[64,2304]{1,0:T(8,128)(2,1)S(1)} %bitcast.5), channel_id=1, source_target_pairs={{0,48},{16,0},{32,16},{48,32},{64,112},{80,64},{96,80},{112,96},{1... | collective-permute-start | bytes 884744 | tf_op jit(solution)/shard_map/ppermute | solution.py:205
  18.5 5.2 %collective-permute-start.3 = (bf16[8,528,256]{2,1,0:T(8,128)(2,1)S(1)}, bf16[8,528,256]{2,1,0:T(8,128)(2,1)S(1)}, u32[]{:S(2)}, u32[]{:S(2)}) collective-permute-start(bf16[8,528,256]{2,1,0:T(8,128)(2,1)S(1)} %away_0.1.refs_8_), channel_id=1, source_target_pairs={{0,1},{1,0},{2,3},{3,2},{4,5},{5,4},{6,7},{7,6},{8,9},{9,8},{10,11... | collective-permute-start | bytes 6488072 | tf_op jit(solution)/shard_map/ppermute | solution.py:220
  19.8 10.2 %collective-permute-start.5 = (bf16[64,2304]{1,0:T(8,128)(2,1)S(1)}, bf16[64,2304]{1,0:T(8,128)(2,1)S(1)}, u32[]{:S(2)}, u32[]{:S(2)}) collective-permute-start(bf16[64,2304]{1,0:T(8,128)(2,1)S(1)} %collective-permute-done.refs_0_.refs_3_), channel_id=1, source_target_pairs={{0,16},{16,32},{32,48},{48,0},{64,80},{80,96},{96,112},{112,64},{1... | collective-permute-start | bytes 884744 | tf_op jit(solution)/shard_map/ppermute | solution.py:205
  20.9 9.7 %collective-permute-start.8 = (bf16[64,2304]{1,0:T(8,128)(2,1)S(1)}, bf16[64,2304]{1,0:T(8,128)(2,1)S(1)}, u32[]{:S(2)}, u32[]{:S(2)}) collective-permute-start(bf16[64,2304]{1,0:T(8,128)(2,1)S(1)} %collective-permute-done.refs_0_.refs_3_), channel_id=1, source_target_pairs={{0,64},{16,80},{32,96},{48,112},{64,0},{80,16},{96,32},{112,48},{1... | collective-permute-start | bytes 884744 | tf_op jit(solution)/shard_map/ppermute | solution.py:205
  22.4 8.2 %collective-permute-start.7 = (bf16[64,2304]{1,0:T(8,128)(2,1)S(1)}, bf16[64,2304]{1,0:T(8,128)(2,1)S(1)}, u32[]{:S(2)}, u32[]{:S(2)}) collective-permute-start(bf16[64,2304]{1,0:T(8,128)(2,1)S(1)} %collective-permute-done.2.refs_3_.refs_6_), channel_id=1, source_target_pairs={{0,48},{16,0},{32,16},{48,32},{64,112},{80,64},{96,80},{112,96},{1... | collective-permute-start | bytes 884744 | tf_op jit(solution)/shard_map/ppermute | solution.py:205
  34.2 5.5 %collective-permute-start.9 = (bf16[8,400,256]{2,1,0:T(8,128)(2,1)S(1)}, bf16[8,400,256]{2,1,0:T(8,128)(2,1)S(1)}, u32[]{:S(2)}, u32[]{:S(2)}) collective-permute-start(bf16[8,400,256]{2,1,0:T(8,128)(2,1)S(1)} %away_1.1.refs_7_), channel_id=1, source_target_pairs={{0,1},{1,0},{2,3},{3,2},{4,5},{5,4},{6,7},{7,6},{8,9},{9,8},{10,11... | collective-permute-start | bytes 4915208 | tf_op jit(solution)/shard_map/ppermute | solution.py:220
  35.4 16.0 %collective-permute-start.4 = (bf16[4,528,256]{2,1,0:T(8,128)(2,1)S(1)}, bf16[4,528,256]{2,1,0:T(8,128)(2,1)S(1)}, u32[]{:S(2)}, u32[]{:S(2)}) collective-permute-start(bf16[4,528,256]{2,1,0:T(8,128)(2,1)S(1)} %get-tuple-element.29.refs_6_), channel_id=1, source_target_pairs={{0,4},{1,13},{2,6},{3,15},{4,0},{5,9},{6,2},{7,11},{8,12},{9,5},{1... | collective-permute-start | bytes 3244040 | tf_op jit(solution)/shard_map/ppermute | solution.py:61
  38.2 10.2 %collective-permute-start.6 = (bf16[64,2304]{1,0:T(8,128)(2,1)S(1)}, bf16[64,2304]{1,0:T(8,128)(2,1)S(1)}, u32[]{:S(2)}, u32[]{:S(2)}) collective-permute-start(bf16[64,2304]{1,0:T(8,128)(2,1)S(1)} %collective-permute-done.5.refs_3_), channel_id=1, source_target_pairs={{0,64},{16,80},{32,96},{48,112},{64,0},{80,16},{96,32},{112,48},{1... | collective-permute-start | bytes 884744 | tf_op jit(solution)/shard_map/ppermute | solution.py:205
  43.3 16.2 %collective-permute-start.11 = (bf16[4,400,256]{2,1,0:T(8,128)(2,1)S(1)}, bf16[4,400,256]{2,1,0:T(8,128)(2,1)S(1)}, u32[]{:S(2)}, u32[]{:S(2)}) collective-permute-start(bf16[4,400,256]{2,1,0:T(8,128)(2,1)S(1)} %get-tuple-element.31.refs_4_), channel_id=1, source_target_pairs={{0,2},{1,13},{2,0},{3,15},{4,6},{5,9},{6,4},{7,11},{8,10},{9,5},{1... | collective-permute-start | bytes 2457608 | tf_op jit(solution)/shard_map/ppermute | solution.py:61
  51.4 2.1 %collective-permute-start.12 = (bf16[8,144,256]{2,1,0:T(8,128)(2,1)S(1)}, bf16[8,144,256]{2,1,0:T(8,128)(2,1)S(1)}, u32[]{:S(2)}, u32[]{:S(2)}) collective-permute-start(bf16[8,144,256]{2,1,0:T(8,128)(2,1)S(1)} %away_2.1.refs_2_), channel_id=1, source_target_pairs={{0,1},{1,0},{2,3},{3,2},{4,5},{5,4},{6,7},{7,6},{8,9},{9,8},{10,11... | collective-permute-start | bytes 1769480 | tf_op jit(solution)/shard_map/ppermute | solution.py:220
  52.5 9.3 %collective-permute-start.10 = (bf16[2,528,256]{2,1,0:T(8,128)(2,1)S(1)}, bf16[2,528,256]{2,1,0:T(8,128)(2,1)S(1)}, u32[]{:S(2)}, u32[]{:S(2)}) collective-permute-start(bf16[2,528,256]{2,1,0:T(8,128)(2,1)S(1)} %get-tuple-element.33.refs_5_), channel_id=1, source_target_pairs={{0,2},{1,5},{2,0},{3,7},{4,6},{5,1},{6,4},{7,3},{8,10},{9,13},{10,... | collective-permute-start | bytes 1622024 | tf_op jit(solution)/shard_map/ppermute | solution.py:61
  60.3 11.0 %collective-permute-start.14 = (bf16[2,400,256]{2,1,0:T(8,128)(2,1)S(1)}, bf16[2,400,256]{2,1,0:T(8,128)(2,1)S(1)}, u32[]{:S(2)}, u32[]{:S(2)}) collective-permute-start(bf16[2,400,256]{2,1,0:T(8,128)(2,1)S(1)} %get-tuple-element.36.refs_2_), channel_id=1, source_target_pairs={{0,12},{1,3},{2,14},{3,1},{4,8},{5,7},{6,10},{7,5},{8,4},{9,11},{1... | collective-permute-start | bytes 1228808 | tf_op jit(solution)/shard_map/ppermute | solution.py:61
  60.7 9.7 %collective-permute-start.15 = (bf16[4,144,256]{2,1,0:T(8,128)(2,1)S(1)}, bf16[4,144,256]{2,1,0:T(8,128)(2,1)S(1)}, u32[]{:S(2)}, u32[]{:S(2)}) collective-permute-start(bf16[4,144,256]{2,1,0:T(8,128)(2,1)S(1)} %get-tuple-element.35.refs_2_), channel_id=1, source_target_pairs={{0,4},{1,3},{2,6},{3,1},{4,0},{5,7},{6,2},{7,5},{8,12},{9,11},{10,... | collective-permute-start | bytes 884744 | tf_op jit(solution)/shard_map/ppermute | solution.py:61
  62.4 15.8 %collective-permute-start.13 = (bf16[1,528,256]{2,1,0:T(8,128)(2,1)S(1)}, bf16[1,528,256]{2,1,0:T(8,128)(2,1)S(1)}, u32[]{:S(2)}, u32[]{:S(2)}) collective-permute-start(bf16[1,528,256]{2,1,0:T(8,128)(2,1)S(1)} %get-tuple-element.38.refs_2_), channel_id=1, source_target_pairs={{0,12},{1,3},{2,14},{3,1},{4,8},{5,7},{6,10},{7,5},{8,4},{9,11},{1... | collective-permute-start | bytes 811016 | tf_op jit(solution)/shard_map/ppermute | solution.py:61
  70.6 4.4 %collective-permute-start.17 = (bf16[2,144,256]{2,1,0:T(8,128)(2,1)S(1)}, bf16[2,144,256]{2,1,0:T(8,128)(2,1)S(1)}, u32[]{:S(2)}, u32[]{:S(2)}) collective-permute-start(bf16[2,144,256]{2,1,0:T(8,128)(2,1)S(1)} %get-tuple-element.41.refs_2_), channel_id=1, source_target_pairs={{0,12},{1,5},{2,14},{3,7},{4,8},{5,1},{6,10},{7,3},{8,4},{9,13},{1... | collective-permute-start | bytes 442376 | tf_op jit(solution)/shard_map/ppermute | solution.py:61
  71.7 8.2 %collective-permute-start.16 = (bf16[1,400,256]{2,1,0:T(8,128)(2,1)S(1)}, bf16[1,400,256]{2,1,0:T(8,128)(2,1)S(1)}, u32[]{:S(2)}, u32[]{:S(2)}) collective-permute-start(bf16[1,400,256]{2,1,0:T(8,128)(2,1)S(1)} %get-tuple-element.43.refs_2_), channel_id=1, source_target_pairs={{0,4},{1,5},{2,6},{3,7},{4,0},{5,1},{6,2},{7,3},{8,12},{9,13},{10,... | collective-permute-start | bytes 614408 | tf_op jit(solution)/shard_map/ppermute | solution.py:61
  75.1 4.7 %collective-permute-start.18 = (bf16[1,144,256]{2,1,0:T(8,128)(2,1)S(1)}, bf16[1,144,256]{2,1,0:T(8,128)(2,1)S(1)}, u32[]{:S(2)}, u32[]{:S(2)}) collective-permute-start(bf16[1,144,256]{2,1,0:T(8,128)(2,1)S(1)} %get-tuple-element.46), channel_id=1, source_target_pairs={{0,2},{1,13},{2,0},{3,15},{4,6},{5,9},{6,4},{7,11},{8,10},{9,5},{1... | collective-permute-start | bytes 221192 | tf_op jit(solution)/shard_map/ppermute | solution.py:61

commit v5 on v4

--- a/solution.py
+++ b/solution.py
@@ -27,7 +27,7 @@
     ("own_two", "far_down", "far_up"),
     ("far_two",),
 )
-COST_OF = {}
+COST_OF = {'step_1_1': 10000000000}
 PLAN = (
     ("away", 0), ("home", 0), ("pass", 2), ("away", 1), ("home", 1), ("away", 2), ("step", 0, 1),
     ("home", 2), ("step", 1, 1), ("step", 0, 2), ("step", 2, 1), ("step", 1, 2), ("step", 2, 2),
@@ -122,6 +122,28 @@
         compiler_params=pltpu.CompilerParams(vmem_limit_bytes=VMEM),
         cost_estimate=pl.CostEstimate(flops=0, transcendentals=0, bytes_accessed=sum(x.size * 2 for x in arrays)),
     )(*(pltpu.with_memory_space_constraint(x, pltpu.HBM) for x in arrays))
+
+
+def pack_kernel(in_ref, out_ref, own_ref, sems):
+    n_in = in_ref.shape[1]
+    first = pltpu.make_async_copy(in_ref, own_ref.at[:, :n_in], sems.at[0])
+    second = pltpu.make_async_copy(out_ref, own_ref.at[:, n_in:], sems.at[1])
+    first.start()
+    second.start()
+    first.wait()
+    second.wait()
+
+
+def pack(q_in, q_out):
+    return pl.pallas_call(
+        pack_kernel,
+        in_specs=[pl.BlockSpec(memory_space=pltpu.HBM)] * 2,
+        out_specs=IN_VMEM,
+        out_shape=pltpu.VMEM((q_in.shape[0], q_in.shape[1] + q_out.shape[1]), q_in.dtype),
+        scratch_shapes=[pltpu.SemaphoreType.DMA((2,))],
+        compiler_params=pltpu.CompilerParams(vmem_limit_bytes=VMEM),
+        cost_estimate=pl.CostEstimate(flops=0, transcendentals=0, bytes_accessed=1024),
+    )(*(pltpu.with_memory_space_constraint(x, pltpu.HBM) for x in (q_in, q_out)))
 
 
 def away_kernel(blocks, orders, feat_ref, act_ref, grad_ref, *refs):
@@ -204,7 +226,7 @@
     }
     move = lambda value, way: lax.ppermute(value, "tok", pairs[way])
 
-    own = jnp.concatenate([query_in, query_out], axis=2).reshape(per * rank, -1)
+    own = pack(query_in.reshape(per * rank, -1), query_out.reshape(per * rank, -1))
     factor = {"own": own, "own_up": move(own, "up"), "own_down": move(own, "down"), "far": move(own, "across")}
     acts, grads = load((activations, out_grads))
     turn = {"after": None}

time: 81 us -> 80.9 us (level)
  other arithmetic: 1 us -> 0 us
  Pallas kernels: 30.7 us -> 31.6 us
    concatenate x1 -> x0, other arithmetic: 1 us -> none  [local(): own = jnp.concatenate([query_in, query_out], axis=2).reshape(per * rank, -1)]
    pallas_call x0 -> x1, Pallas kernels: none -> 0.97 us  [pack(): pl.pallas_call(pack_kernel, in_specs=[pl.BlockSpec(memory_space=pltpu.HBM...]
where the time goes in v5:
time: 80.9 us; the launch traced here: 80.8 us
  Pallas kernels  31.6 us (39%)
  starting transfers between devices  26.4 us (33%)
  waiting for transfers between devices  22.7 us (28%)
    pallas_call x13, Pallas kernels, call(): pl.pallas_call(kernel, in_specs=specs, out_specs=jax.tree.map(lambda _: I...  24.2 us
    ppermute x9, waiting for transfers between devices, halve(): lax.ppermute(value, 'feat', [(s, partner(s, orders[s & 1][stage])) for s...  14.8 us
    ppermute x7, starting transfers between devices, local(): move = lambda value, way: lax.ppermute(value, 'tok', pairs[way])  12.6 us
    ppermute x9, starting transfers between devices, halve(): lax.ppermute(value, 'feat', [(s, partner(s, orders[s & 1][stage])) for s...  11.1 us
    ppermute x7, waiting for transfers between devices, local(): move = lambda value, way: lax.ppermute(value, 'tok', pairs[way])  6.87 us
    pallas_call x1, Pallas kernels, load(): pl.pallas_call(functools.partial(load_kernel, parts), in_specs=[pl.BlockS...  6.48 us
    ppermute x3, starting transfers between devices, away(): got[c] = lax.ppermute(send, 'feat', [(s, s ^ 1) for s in range(16)])  2.67 us
  transfers between devices with their start and end apart: 19, of which 9 were waited for; matrix products, arithmetic and copies ran while one was open for 0% of the time, Pallas kernels for 28%

profile of v5, /device:TPU:1, one launch (start us, length us, event | category | flops | bytes accessed | tf_op | source)
XLA Modules:
  0.0 80.8 jit_solution(8675043522982937843)
XLA Ops:
  0.0 1.0 %shard_map.47.refs_2_.refs_5_ = bf16[64,2304]{1,0:T(8,128)(2,1)S(1)} custom-call(bf16[64,1792]{1,0:T(8,128)(2,1)} %bitcast.4, bf16[64,512]{1,0:T(8,128)(2,1)} %bitcast.5), custom_call_target="tpu_custom_call" | custom-call | bytes 1024 | tf_op jit(solution)/shard_map/pallas_call | solution.py:138
  1.0 2.5 %collective-permute-start = (bf16[64,2304]{1,0:T(8,128)(2,1)S(1)}, bf16[64,2304]{1,0:T(8,128)(2,1)S(1)}, u32[]{:S(2)}, u32[]{:S(2)}) collective-permute-start(bf16[64,2304]{1,0:T(8,128)(2,1)S(1)} %shard_map.47.refs_2_.refs_5_), channel_id=1, source_target_pairs={{0,16},{16,32},{32,48},{48,0},{64,80},{80,96},{96,112},{112,64},{1... | collective-permute-start | bytes 884744 | tf_op jit(solution)/shard_map/ppermute | solution.py:227
  3.5 2.7 %collective-permute-start.2 = (bf16[64,2304]{1,0:T(8,128)(2,1)S(1)}, bf16[64,2304]{1,0:T(8,128)(2,1)S(1)}, u32[]{:S(2)}, u32[]{:S(2)}) collective-permute-start(bf16[64,2304]{1,0:T(8,128)(2,1)S(1)} %shard_map.47.refs_2_.refs_5_), channel_id=1, source_target_pairs={{0,64},{16,80},{32,96},{48,112},{64,0},{80,16},{96,32},{112,48},{1... | collective-permute-start | bytes 884744 | tf_op jit(solution)/shard_map/ppermute | solution.py:227
  6.3 2.2 %collective-permute-start.1 = (bf16[64,2304]{1,0:T(8,128)(2,1)S(1)}, bf16[64,2304]{1,0:T(8,128)(2,1)S(1)}, u32[]{:S(2)}, u32[]{:S(2)}) collective-permute-start(bf16[64,2304]{1,0:T(8,128)(2,1)S(1)} %shard_map.47.refs_2_.refs_5_), channel_id=1, source_target_pairs={{0,48},{16,0},{32,16},{48,32},{64,112},{80,64},{96,80},{112,96},{1... | collective-permute-start | bytes 884744 | tf_op jit(solution)/shard_map/ppermute | solution.py:227
  8.5 6.5 %shard_map.46 = (bf16[4096,1792]{1,0:T(8,128)(2,1)S(1)}, bf16[4096,512]{1,0:T(8,128)(2,1)S(1)}) custom-call(bf16[4096,1792]{1,0:T(8,128)(2,1)} %act_ref.1, bf16[4096,512]{1,0:T(8,128)(2,1)} %grad_ref.1), custom_call_target="tpu_custom_call" | custom-call | bytes 18874368 | tf_op jit(solution)/shard_map/pallas_call | solution.py:116
  15.0 0.0 collective-permute-done.refs_0_.refs_3_
  15.0 0.0 collective-permute-done.2.refs_3_.refs_6_
  15.0 0.0 collective-permute-done.1.refs_1_.refs_4_
  15.0 3.5 %away_0.1.refs_8_ = bf16[8,528,256]{2,1,0:T(8,128)(2,1)S(1)} custom-call(s32[1]{0:T(128)} %bitcast.1.feat_ref.refs_0_, bf16[4096,1792]{1,0:T(8,128)(2,1)S(1)} %get-tuple-element.26.act_ref.refs_1_, bf16[4096,512]{1,0:T(8,128)(2,1)S(1)} %get-tuple-element.27.grad_ref.refs_2_, bf16[64,2304]{1,0:T(8,128)(2,1)S(1)} %collective-permute-done.refs_0_.refs_3_, ...), custom_call_target="tpu_custom_call" | custom-call | flops 1024 | bytes 1024 | tf_op jit(solution)/shard_map/away_0/pallas_call | solution.py:201
  18.4 1.3 %collective-permute-start.3 = (bf16[8,528,256]{2,1,0:T(8,128)(2,1)S(1)}, bf16[8,528,256]{2,1,0:T(8,128)(2,1)S(1)}, u32[]{:S(2)}, u32[]{:S(2)}) collective-permute-start(bf16[8,528,256]{2,1,0:T(8,128)(2,1)S(1)} %away_0.1.refs_8_), channel_id=1, source_target_pairs={{0,1},{1,0},{2,3},{3,2},{4,5},{5,4},{6,7},{7,6},{8,9},{9,8},{10,11... | collective-permute-start | bytes 6488072 | tf_op jit(solution)/shard_map/ppermute | solution.py:242
  19.8 1.1 %collective-permute-start.5 = (bf16[64,2304]{1,0:T(8,128)(2,1)S(1)}, bf16[64,2304]{1,0:T(8,128)(2,1)S(1)}, u32[]{:S(2)}, u32[]{:S(2)}) collective-permute-start(bf16[64,2304]{1,0:T(8,128)(2,1)S(1)} %collective-permute-done.refs_0_.refs_3_), channel_id=1, source_target_pairs={{0,16},{16,32},{32,48},{48,0},{64,80},{80,96},{96,112},{112,64},{1... | collective-permute-start | bytes 884744 | tf_op jit(solution)/shard_map/ppermute | solution.py:227
  20.9 1.5 %collective-permute-start.8 = (bf16[64,2304]{1,0:T(8,128)(2,1)S(1)}, bf16[64,2304]{1,0:T(8,128)(2,1)S(1)}, u32[]{:S(2)}, u32[]{:S(2)}) collective-permute-start(bf16[64,2304]{1,0:T(8,128)(2,1)S(1)} %collective-permute-done.refs_0_.refs_3_), channel_id=1, source_target_pairs={{0,64},{16,80},{32,96},{48,112},{64,0},{80,16},{96,32},{112,48},{1... | collective-permute-start | bytes 884744 | tf_op jit(solution)/shard_map/ppermute | solution.py:227
  22.4 1.0 %collective-permute-start.7 = (bf16[64,2304]{1,0:T(8,128)(2,1)S(1)}, bf16[64,2304]{1,0:T(8,128)(2,1)S(1)}, u32[]{:S(2)}, u32[]{:S(2)}) collective-permute-start(bf16[64,2304]{1,0:T(8,128)(2,1)S(1)} %collective-permute-done.2.refs_3_.refs_6_), channel_id=1, source_target_pairs={{0,48},{16,0},{32,16},{48,32},{64,112},{80,64},{96,80},{112,96},{1... | collective-permute-start | bytes 884744 | tf_op jit(solution)/shard_map/ppermute | solution.py:227
  23.4 0.2 collective-permute-done.3.refs_7_
  23.7 3.5 %home_0.1 = (bf16[4,528,256]{2,1,0:T(8,128)(2,1)S(1)}, f32[4,512,256]{2,1,0:T(8,128)S(1)}) custom-call(s32[1]{0:T(128)} %bitcast.1.feat_ref.refs_0_, bf16[4096,1792]{1,0:T(8,128)(2,1)S(1)} %get-tuple-element.26.act_ref.refs_1_, bf16[4096,512]{1,0:T(8,128)(2,1)S(1)} %get-tuple-element.27.grad_ref.refs_2_, ...), custom_call_target="tpu_custom_call" | custom-call | flops 1024 | bytes 1024 | tf_op jit(solution)/shard_map/home_0/pallas_call | solution.py:201
  27.1 2.8 %collective-permute-done.5.refs_3_ = bf16[64,2304]{1,0:T(8,128)(2,1)S(1)} collective-permute-done((bf16[64,2304]{1,0:T(8,128)(2,1)S(1)}, bf16[64,2304]{1,0:T(8,128)(2,1)S(1)}, u32[]{:S(2)}, u32[]{:S(2)}) %collective-permute-start.5) | collective-permute-done | bytes 294944 | tf_op jit(solution)/shard_map/ppermute | solution.py:227
  30.0 0.7 collective-permute-done.8.refs_5_
  30.6 0.0 collective-permute-done.7.refs_4_
  30.6 3.5 %away_1.1.refs_7_ = bf16[8,400,256]{2,1,0:T(8,128)(2,1)S(1)} custom-call(s32[1]{0:T(128)} %bitcast.1.feat_ref.refs_0_, bf16[4096,1792]{1,0:T(8,128)(2,1)S(1)} %get-tuple-element.26.act_ref.refs_1_, bf16[4096,512]{1,0:T(8,128)(2,1)S(1)} %get-tuple-element.27.grad_ref.refs_2_, bf16[64,2304]{1,0:T(8,128)(2,1)S(1)} %collective-permute-done.5.refs_3_, ...), custom_call_target="tpu_custom_call" | custom-call | flops 1024 | bytes 1024 | tf_op jit(solution)/shard_map/away_1/pallas_call | solution.py:201
  34.2 1.3 %collective-permute-start.9 = (bf16[8,400,256]{2,1,0:T(8,128)(2,1)S(1)}, bf16[8,400,256]{2,1,0:T(8,128)(2,1)S(1)}, u32[]{:S(2)}, u32[]{:S(2)}) collective-permute-start(bf16[8,400,256]{2,1,0:T(8,128)(2,1)S(1)} %away_1.1.refs_7_), channel_id=1, source_target_pairs={{0,1},{1,0},{2,3},{3,2},{4,5},{5,4},{6,7},{7,6},{8,9},{9,8},{10,11... | collective-permute-start | bytes 4915208 | tf_op jit(solution)/shard_map/ppermute | solution.py:242
  35.4 2.7 %collective-permute-start.4 = (bf16[4,528,256]{2,1,0:T(8,128)(2,1)S(1)}, bf16[4,528,256]{2,1,0:T(8,128)(2,1)S(1)}, u32[]{:S(2)}, u32[]{:S(2)}) collective-permute-start(bf16[4,528,256]{2,1,0:T(8,128)(2,1)S(1)} %get-tuple-element.29.refs_6_), channel_id=1, source_target_pairs={{0,4},{1,13},{2,6},{3,15},{4,0},{5,9},{6,2},{7,11},{8,12},{9,5},{1... | collective-permute-start | bytes 3244040 | tf_op jit(solution)/shard_map/ppermute | solution.py:61
  38.1 1.5 %collective-permute-start.6 = (bf16[64,2304]{1,0:T(8,128)(2,1)S(1)}, bf16[64,2304]{1,0:T(8,128)(2,1)S(1)}, u32[]{:S(2)}, u32[]{:S(2)}) collective-permute-start(bf16[64,2304]{1,0:T(8,128)(2,1)S(1)} %collective-permute-done.5.refs_3_), channel_id=1, source_target_pairs={{0,64},{16,80},{32,96},{48,112},{64,0},{80,16},{96,32},{112,48},{1... | collective-permute-start | bytes 884744 | tf_op jit(solution)/shard_map/ppermute | solution.py:227
  39.6 3.6 %home_1.1 = (bf16[4,400,256]{2,1,0:T(8,128)(2,1)S(1)}, f32[4,384,256]{2,1,0:T(8,128)S(1)}) custom-call(s32[1]{0:T(128)} %bitcast.1.feat_ref.refs_0_, bf16[4096,1792]{1,0:T(8,128)(2,1)S(1)} %get-tuple-element.26.act_ref.refs_1_, bf16[4096,512]{1,0:T(8,128)(2,1)S(1)} %get-tuple-element.27.grad_ref.refs_2_, ...), custom_call_target="tpu_custom_call" | custom-call | flops 1024 | bytes 1024 | tf_op jit(solution)/shard_map/home_1/pallas_call | solution.py:201
  43.3 1.7 %collective-permute-start.11 = (bf16[4,400,256]{2,1,0:T(8,128)(2,1)S(1)}, bf16[4,400,256]{2,1,0:T(8,128)(2,1)S(1)}, u32[]{:S(2)}, u32[]{:S(2)}) collective-permute-start(bf16[4,400,256]{2,1,0:T(8,128)(2,1)S(1)} %get-tuple-element.31.refs_4_), channel_id=1, source_target_pairs={{0,2},{1,13},{2,0},{3,15},{4,6},{5,9},{6,4},{7,11},{8,10},{9,5},{1... | collective-permute-start | bytes 2457608 | tf_op jit(solution)/shard_map/ppermute | solution.py:61
  45.0 3.4 %collective-permute-done.6.refs_3_ = bf16[64,2304]{1,0:T(8,128)(2,1)S(1)} collective-permute-done((bf16[64,2304]{1,0:T(8,128)(2,1)S(1)}, bf16[64,2304]{1,0:T(8,128)(2,1)S(1)}, u32[]{:S(2)}, u32[]{:S(2)}) %collective-permute-start.6) | collective-permute-done | bytes 294944 | tf_op jit(solution)/shard_map/ppermute | solution.py:227
  48.3 3.0 %away_2.1.refs_2_ = bf16[8,144,256]{2,1,0:T(8,128)(2,1)S(1)} custom-call(s32[1]{0:T(128)} %bitcast.1.feat_ref.refs_0_, bf16[4096,1792]{1,0:T(8,128)(2,1)S(1)} %get-tuple-element.26.act_ref.refs_1_, bf16[4096,512]{1,0:T(8,128)(2,1)S(1)} %get-tuple-element.27.grad_ref.refs_2_, bf16[64,2304]{1,0:T(8,128)(2,1)S(1)} %collective-permute-done.6.refs_3_, ...), custom_call_target="tpu_custom_call" | custom-call | flops 1024 | bytes 1024 | tf_op jit(solution)/shard_map/away_2/pallas_call | solution.py:201
  51.3 0.1 collective-permute-start.12
  51.4 1.1 %step_0_1.1 = (bf16[2,528,256]{2,1,0:T(8,128)(2,1)S(1)}, f32[2,512,256]{2,1,0:T(8,128)S(1)}) custom-call(f32[4,512,256]{2,1,0:T(8,128)S(1)} %get-tuple-element.28.refs_0_, bf16[4,528,256]{2,1,0:T(8,128)(2,1)S(1)} %collective-permute-done.4.refs_1_, bf16[8,144,256]{2,1,0:T(8,128)(2,1)S(1)} %away_2.1.refs_2_), custom_call_target="tpu_custom_call" | custom-call | flops 1024 | bytes 1024 | tf_op jit(solution)/shard_map/step_0_1/pallas_call | solution.py:201
  52.5 0.1 collective-permute-start.10
  52.6 0.8 collective-permute-done.12.refs_4_
  53.4 2.9 %home_2.1 = (bf16[4,144,256]{2,1,0:T(8,128)(2,1)S(1)}, f32[4,128,256]{2,1,0:T(8,128)S(1)}) custom-call(s32[1]{0:T(128)} %bitcast.1.feat_ref.refs_0_, bf16[4096,1792]{1,0:T(8,128)(2,1)S(1)} %get-tuple-element.26.act_ref.refs_1_, bf16[4096,512]{1,0:T(8,128)(2,1)S(1)} %get-tuple-element.27.grad_ref.refs_2_, ...), custom_call_target="tpu_custom_call" | custom-call | flops 1024 | bytes 1024 | tf_op jit(solution)/shard_map/home_2/pallas_call | solution.py:201
  56.4 3.1 %collective-permute-done.11.refs_1_ = bf16[4,400,256]{2,1,0:T(8,128)(2,1)S(1)} collective-permute-done((bf16[4,400,256]{2,1,0:T(8,128)(2,1)S(1)}, bf16[4,400,256]{2,1,0:T(8,128)(2,1)S(1)}, u32[]{:S(2)}, u32[]{:S(2)}) %collective-permute-start.11) | collective-permute-done | bytes 819232 | tf_op jit(solution)/shard_map/ppermute | solution.py:61
  59.5 0.8 step_1_1.1
  60.2 0.4 collective-permute-start.14
  60.6 1.2 %collective-permute-start.15 = (bf16[4,144,256]{2,1,0:T(8,128)(2,1)S(1)}, bf16[4,144,256]{2,1,0:T(8,128)(2,1)S(1)}, u32[]{:S(2)}, u32[]{:S(2)}) collective-permute-start(bf16[4,144,256]{2,1,0:T(8,128)(2,1)S(1)} %get-tuple-element.35.refs_2_), channel_id=1, source_target_pairs={{0,4},{1,3},{2,6},{3,1},{4,0},{5,7},{6,2},{7,5},{8,12},{9,11},{10,... | collective-permute-start | bytes 884744 | tf_op jit(solution)/shard_map/ppermute | solution.py:61
  61.8 0.0 collective-permute-done.10.refs_1_
  61.8 0.5 step_0_2.1
  62.3 0.4 collective-permute-start.13
  62.7 7.6 %collective-permute-done.15.refs_1_ = bf16[4,144,256]{2,1,0:T(8,128)(2,1)S(1)} collective-permute-done((bf16[4,144,256]{2,1,0:T(8,128)(2,1)S(1)}, bf16[4,144,256]{2,1,0:T(8,128)(2,1)S(1)}, u32[]{:S(2)}, u32[]{:S(2)}) %collective-permute-start.15) | collective-permute-done | bytes 294944 | tf_op jit(solution)/shard_map/ppermute | solution.py:61
  70.3 0.3 step_2_1.1
  70.6 0.7 collective-permute-start.17
  71.3 0.4 step_1_2.1
  71.7 1.0 %collective-permute-start.16 = (bf16[1,400,256]{2,1,0:T(8,128)(2,1)S(1)}, bf16[1,400,256]{2,1,0:T(8,128)(2,1)S(1)}, u32[]{:S(2)}, u32[]{:S(2)}) collective-permute-start(bf16[1,400,256]{2,1,0:T(8,128)(2,1)S(1)} %get-tuple-element.43.refs_2_), channel_id=1, source_target_pairs={{0,4},{1,5},{2,6},{3,7},{4,0},{5,1},{6,2},{7,3},{8,12},{9,13},{10,... | collective-permute-start | bytes 614408 | tf_op jit(solution)/shard_map/ppermute | solution.py:61
  72.6 2.3 %collective-permute-done.17.refs_1_ = bf16[2,144,256]{2,1,0:T(8,128)(2,1)S(1)} collective-permute-done((bf16[2,144,256]{2,1,0:T(8,128)(2,1)S(1)}, bf16[2,144,256]{2,1,0:T(8,128)(2,1)S(1)}, u32[]{:S(2)}, u32[]{:S(2)}) %collective-permute-start.17) | collective-permute-done | bytes 147488 | tf_op jit(solution)/shard_map/ppermute | solution.py:61
  74.9 0.1 step_2_2.1
  75.1 3.0 %collective-permute-start.18 = (bf16[1,144,256]{2,1,0:T(8,128)(2,1)S(1)}, bf16[1,144,256]{2,1,0:T(8,128)(2,1)S(1)}, u32[]{:S(2)}, u32[]{:S(2)}) collective-permute-start(bf16[1,144,256]{2,1,0:T(8,128)(2,1)S(1)} %get-tuple-element.46), channel_id=1, source_target_pairs={{0,2},{1,13},{2,0},{3,15},{4,6},{5,9},{6,4},{7,11},{8,10},{9,5},{1... | collective-permute-start | bytes 221192 | tf_op jit(solution)/shard_map/ppermute | solution.py:61
  78.1 1.7 %collective-permute-done.18.refs_5_ = bf16[1,144,256]{2,1,0:T(8,128)(2,1)S(1)} collective-permute-done((bf16[1,144,256]{2,1,0:T(8,128)(2,1)S(1)}, bf16[1,144,256]{2,1,0:T(8,128)(2,1)S(1)}, u32[]{:S(2)}, u32[]{:S(2)}) %collective-permute-start.18) | collective-permute-done | bytes 73760 | tf_op jit(solution)/shard_map/ppermute | solution.py:61
  79.9 1.0 %shard_map.48 = f32[16,256]{1,0:T(8,128)} custom-call(s32[1]{0:T(128)} %bitcast.tok_ref, f32[1,512,256]{2,1,0:T(8,128)S(1)} %get-tuple-element.37.refs_0_, bf16[1,528,256]{2,1,0:T(8,128)(2,1)S(1)} %collective-permute-done.13.refs_1_, f32[1,384,256]{2,1,0:T(8,128)S(1)} %get-tuple-element.42.refs_2_, bf16[1,400,256]{2,1,0:T(8,128)(2,1)S(1)} %collective-permute-done.16.refs_3_, ...), custom_call_target="tpu_custom_call" | custom-call | bytes 1024 | tf_op jit(solution)/shard_map/pallas_call | solution.py:201
  (5 shorter events, 0.0 us)
Async XLA Ops:
  1.0 14.0 %collective-permute-start = (bf16[64,2304]{1,0:T(8,128)(2,1)S(1)}, bf16[64,2304]{1,0:T(8,128)(2,1)S(1)}, u32[]{:S(2)}, u32[]{:S(2)}) collective-permute-start(bf16[64,2304]{1,0:T(8,128)(2,1)S(1)} %shard_map.47.refs_2_.refs_5_), channel_id=1, source_target_pairs={{0,16},{16,32},{32,48},{48,0},{64,80},{80,96},{96,112},{112,64},{1... | collective-permute-start | bytes 884744 | tf_op jit(solution)/shard_map/ppermute | solution.py:227
  3.5 11.5 %collective-permute-start.2 = (bf16[64,2304]{1,0:T(8,128)(2,1)S(1)}, bf16[64,2304]{1,0:T(8,128)(2,1)S(1)}, u32[]{:S(2)}, u32[]{:S(2)}) collective-permute-start(bf16[64,2304]{1,0:T(8,128)(2,1)S(1)} %shard_map.47.refs_2_.refs_5_), channel_id=1, source_target_pairs={{0,64},{16,80},{32,96},{48,112},{64,0},{80,16},{96,32},{112,48},{1... | collective-permute-start | bytes 884744 | tf_op jit(solution)/shard_map/ppermute | solution.py:227
  6.3 8.7 %collective-permute-start.1 = (bf16[64,2304]{1,0:T(8,128)(2,1)S(1)}, bf16[64,2304]{1,0:T(8,128)(2,1)S(1)}, u32[]{:S(2)}, u32[]{:S(2)}) collective-permute-start(bf16[64,2304]{1,0:T(8,128)(2,1)S(1)} %shard_map.47.refs_2_.refs_5_), channel_id=1, source_target_pairs={{0,48},{16,0},{32,16},{48,32},{64,112},{80,64},{96,80},{112,96},{1... | collective-permute-start | bytes 884744 | tf_op jit(solution)/shard_map/ppermute | solution.py:227
  18.4 5.2 %collective-permute-start.3 = (bf16[8,528,256]{2,1,0:T(8,128)(2,1)S(1)}, bf16[8,528,256]{2,1,0:T(8,128)(2,1)S(1)}, u32[]{:S(2)}, u32[]{:S(2)}) collective-permute-start(bf16[8,528,256]{2,1,0:T(8,128)(2,1)S(1)} %away_0.1.refs_8_), channel_id=1, source_target_pairs={{0,1},{1,0},{2,3},{3,2},{4,5},{5,4},{6,7},{7,6},{8,9},{9,8},{10,11... | collective-permute-start | bytes 6488072 | tf_op jit(solution)/shard_map/ppermute | solution.py:242
  19.8 10.2 %collective-permute-start.5 = (bf16[64,2304]{1,0:T(8,128)(2,1)S(1)}, bf16[64,2304]{1,0:T(8,128)(2,1)S(1)}, u32[]{:S(2)}, u32[]{:S(2)}) collective-permute-start(bf16[64,2304]{1,0:T(8,128)(2,1)S(1)} %collective-permute-done.refs_0_.refs_3_), channel_id=1, source_target_pairs={{0,16},{16,32},{32,48},{48,0},{64,80},{80,96},{96,112},{112,64},{1... | collective-permute-start | bytes 884744 | tf_op jit(solution)/shard_map/ppermute | solution.py:227
  20.9 9.7 %collective-permute-start.8 = (bf16[64,2304]{1,0:T(8,128)(2,1)S(1)}, bf16[64,2304]{1,0:T(8,128)(2,1)S(1)}, u32[]{:S(2)}, u32[]{:S(2)}) collective-permute-start(bf16[64,2304]{1,0:T(8,128)(2,1)S(1)} %collective-permute-done.refs_0_.refs_3_), channel_id=1, source_target_pairs={{0,64},{16,80},{32,96},{48,112},{64,0},{80,16},{96,32},{112,48},{1... | collective-permute-start | bytes 884744 | tf_op jit(solution)/shard_map/ppermute | solution.py:227
  22.4 8.2 %collective-permute-start.7 = (bf16[64,2304]{1,0:T(8,128)(2,1)S(1)}, bf16[64,2304]{1,0:T(8,128)(2,1)S(1)}, u32[]{:S(2)}, u32[]{:S(2)}) collective-permute-start(bf16[64,2304]{1,0:T(8,128)(2,1)S(1)} %collective-permute-done.2.refs_3_.refs_6_), channel_id=1, source_target_pairs={{0,48},{16,0},{32,16},{48,32},{64,112},{80,64},{96,80},{112,96},{1... | collective-permute-start | bytes 884744 | tf_op jit(solution)/shard_map/ppermute | solution.py:227
  34.2 5.5 %collective-permute-start.9 = (bf16[8,400,256]{2,1,0:T(8,128)(2,1)S(1)}, bf16[8,400,256]{2,1,0:T(8,128)(2,1)S(1)}, u32[]{:S(2)}, u32[]{:S(2)}) collective-permute-start(bf16[8,400,256]{2,1,0:T(8,128)(2,1)S(1)} %away_1.1.refs_7_), channel_id=1, source_target_pairs={{0,1},{1,0},{2,3},{3,2},{4,5},{5,4},{6,7},{7,6},{8,9},{9,8},{10,11... | collective-permute-start | bytes 4915208 | tf_op jit(solution)/shard_map/ppermute | solution.py:242
  35.4 16.0 %collective-permute-start.4 = (bf16[4,528,256]{2,1,0:T(8,128)(2,1)S(1)}, bf16[4,528,256]{2,1,0:T(8,128)(2,1)S(1)}, u32[]{:S(2)}, u32[]{:S(2)}) collective-permute-start(bf16[4,528,256]{2,1,0:T(8,128)(2,1)S(1)} %get-tuple-element.29.refs_6_), channel_id=1, source_target_pairs={{0,4},{1,13},{2,6},{3,15},{4,0},{5,9},{6,2},{7,11},{8,12},{9,5},{1... | collective-permute-start | bytes 3244040 | tf_op jit(solution)/shard_map/ppermute | solution.py:61
  38.1 10.2 %collective-permute-start.6 = (bf16[64,2304]{1,0:T(8,128)(2,1)S(1)}, bf16[64,2304]{1,0:T(8,128)(2,1)S(1)}, u32[]{:S(2)}, u32[]{:S(2)}) collective-permute-start(bf16[64,2304]{1,0:T(8,128)(2,1)S(1)} %collective-permute-done.5.refs_3_), channel_id=1, source_target_pairs={{0,64},{16,80},{32,96},{48,112},{64,0},{80,16},{96,32},{112,48},{1... | collective-permute-start | bytes 884744 | tf_op jit(solution)/shard_map/ppermute | solution.py:227
  43.3 16.2 %collective-permute-start.11 = (bf16[4,400,256]{2,1,0:T(8,128)(2,1)S(1)}, bf16[4,400,256]{2,1,0:T(8,128)(2,1)S(1)}, u32[]{:S(2)}, u32[]{:S(2)}) collective-permute-start(bf16[4,400,256]{2,1,0:T(8,128)(2,1)S(1)} %get-tuple-element.31.refs_4_), channel_id=1, source_target_pairs={{0,2},{1,13},{2,0},{3,15},{4,6},{5,9},{6,4},{7,11},{8,10},{9,5},{1... | collective-permute-start | bytes 2457608 | tf_op jit(solution)/shard_map/ppermute | solution.py:61
  51.3 2.1 %collective-permute-start.12 = (bf16[8,144,256]{2,1,0:T(8,128)(2,1)S(1)}, bf16[8,144,256]{2,1,0:T(8,128)(2,1)S(1)}, u32[]{:S(2)}, u32[]{:S(2)}) collective-permute-start(bf16[8,144,256]{2,1,0:T(8,128)(2,1)S(1)} %away_2.1.refs_2_), channel_id=1, source_target_pairs={{0,1},{1,0},{2,3},{3,2},{4,5},{5,4},{6,7},{7,6},{8,9},{9,8},{10,11... | collective-permute-start | bytes 1769480 | tf_op jit(solution)/shard_map/ppermute | solution.py:242
  52.5 9.3 %collective-permute-start.10 = (bf16[2,528,256]{2,1,0:T(8,128)(2,1)S(1)}, bf16[2,528,256]{2,1,0:T(8,128)(2,1)S(1)}, u32[]{:S(2)}, u32[]{:S(2)}) collective-permute-start(bf16[2,528,256]{2,1,0:T(8,128)(2,1)S(1)} %get-tuple-element.33.refs_5_), channel_id=1, source_target_pairs={{0,2},{1,5},{2,0},{3,7},{4,6},{5,1},{6,4},{7,3},{8,10},{9,13},{10,... | collective-permute-start | bytes 1622024 | tf_op jit(solution)/shard_map/ppermute | solution.py:61
  60.2 11.0 %collective-permute-start.14 = (bf16[2,400,256]{2,1,0:T(8,128)(2,1)S(1)}, bf16[2,400,256]{2,1,0:T(8,128)(2,1)S(1)}, u32[]{:S(2)}, u32[]{:S(2)}) collective-permute-start(bf16[2,400,256]{2,1,0:T(8,128)(2,1)S(1)} %get-tuple-element.36.refs_2_), channel_id=1, source_target_pairs={{0,12},{1,3},{2,14},{3,1},{4,8},{5,7},{6,10},{7,5},{8,4},{9,11},{1... | collective-permute-start | bytes 1228808 | tf_op jit(solution)/shard_map/ppermute | solution.py:61
  60.6 9.7 %collective-permute-start.15 = (bf16[4,144,256]{2,1,0:T(8,128)(2,1)S(1)}, bf16[4,144,256]{2,1,0:T(8,128)(2,1)S(1)}, u32[]{:S(2)}, u32[]{:S(2)}) collective-permute-start(bf16[4,144,256]{2,1,0:T(8,128)(2,1)S(1)} %get-tuple-element.35.refs_2_), channel_id=1, source_target_pairs={{0,4},{1,3},{2,6},{3,1},{4,0},{5,7},{6,2},{7,5},{8,12},{9,11},{10,... | collective-permute-start | bytes 884744 | tf_op jit(solution)/shard_map/ppermute | solution.py:61
  62.3 15.8 %collective-permute-start.13 = (bf16[1,528,256]{2,1,0:T(8,128)(2,1)S(1)}, bf16[1,528,256]{2,1,0:T(8,128)(2,1)S(1)}, u32[]{:S(2)}, u32[]{:S(2)}) collective-permute-start(bf16[1,528,256]{2,1,0:T(8,128)(2,1)S(1)} %get-tuple-element.38.refs_2_), channel_id=1, source_target_pairs={{0,12},{1,3},{2,14},{3,1},{4,8},{5,7},{6,10},{7,5},{8,4},{9,11},{1... | collective-permute-start | bytes 811016 | tf_op jit(solution)/shard_map/ppermute | solution.py:61
  70.6 4.3 %collective-permute-start.17 = (bf16[2,144,256]{2,1,0:T(8,128)(2,1)S(1)}, bf16[2,144,256]{2,1,0:T(8,128)(2,1)S(1)}, u32[]{:S(2)}, u32[]{:S(2)}) collective-permute-start(bf16[2,144,256]{2,1,0:T(8,128)(2,1)S(1)} %get-tuple-element.41.refs_2_), channel_id=1, source_target_pairs={{0,12},{1,5},{2,14},{3,7},{4,8},{5,1},{6,10},{7,3},{8,4},{9,13},{1... | collective-permute-start | bytes 442376 | tf_op jit(solution)/shard_map/ppermute | solution.py:61
  71.7 8.2 %collective-permute-start.16 = (bf16[1,400,256]{2,1,0:T(8,128)(2,1)S(1)}, bf16[1,400,256]{2,1,0:T(8,128)(2,1)S(1)}, u32[]{:S(2)}, u32[]{:S(2)}) collective-permute-start(bf16[1,400,256]{2,1,0:T(8,128)(2,1)S(1)} %get-tuple-element.43.refs_2_), channel_id=1, source_target_pairs={{0,4},{1,5},{2,6},{3,7},{4,0},{5,1},{6,2},{7,3},{8,12},{9,13},{10,... | collective-permute-start | bytes 614408 | tf_op jit(solution)/shard_map/ppermute | solution.py:61
  75.1 4.8 %collective-permute-start.18 = (bf16[1,144,256]{2,1,0:T(8,128)(2,1)S(1)}, bf16[1,144,256]{2,1,0:T(8,128)(2,1)S(1)}, u32[]{:S(2)}, u32[]{:S(2)}) collective-permute-start(bf16[1,144,256]{2,1,0:T(8,128)(2,1)S(1)} %get-tuple-element.46), channel_id=1, source_target_pairs={{0,2},{1,13},{2,0},{3,15},{4,6},{5,9},{6,4},{7,11},{8,10},{9,5},{1... | collective-permute-start | bytes 221192 | tf_op jit(solution)/shard_map/ppermute | solution.py:61
